TPU v7x, 32 devices: a whole 2x2x4 slice. The times are simulated.
32 devices in a mesh: tm: 4 (over x, core), space: 8 (over z, y).
Axes of the slice: x: 2, y: 2, z: 4, core: 2. Of those that a mesh axis runs over, the one named last changes fastest.
Arguments:
- start_states: float32 [4, 16, 64, 512], P('tm', 'space'), may hold values from -12 to 12
- diff_x: float32 [16, 64, 512], P('space'), may hold values from 0.3 to 3
- diff_y: float32 [16, 64, 512], P('space'), may hold values from 0.3 to 3
- diff_z: float32 [16, 64, 512], P('space'), may hold values from 0.3 to 3
- stress: float32 [16, 64, 512], P('space'), may hold values from -4 to 4
- trap_class: int32 [16, 64, 512], P('space'), may hold values from 0 to 3
- cotangent: float32 [4, 16, 64, 512], P('tm', 'space'), may hold values from -6 to 6
Outputs:
- new_ends: float32 [4, 16, 64, 512], P('tm', 'space')
- grad_x: float32 [16, 64, 512], P('space', 'tm')
- grad_y: float32 [16, 64, 512], P('space', 'tm')
- grad_z: float32 [16, 64, 512], P('space', 'tm')
- jump_norm: float32 [], replicated
All inputs are finite; a program needn't handle non-finite values.
Results may differ from a plain program's by a relative error of at most 0.0003.
Values sent between devices are 32-bit elements; how exact they have to be, the bound alone decides.
No kernel may reach another device: no remote copies, remote signals or barrier semaphores. Data moves between devices by JAX's collectives and lax.ppermute only.
A program may use at most 192 MiB of HBM per device.

v0:
```python
import jax
import jax.numpy as jnp
from jax import lax
from jax.sharding import PartitionSpec as P

FINE_STEPS = 2
SWEEPS = 8
COARSE_SWEEPS = 2


stress_coupling = 0.5
time_step = 1.0
trap_levels = (0.0, 1.0, 3.0, 7.0)


def extended(cells, sides, width):
    for axis, dim in sides:
        count = lax.axis_size(axis)
        ends = count - 1
        head = lax.slice_in_dim(cells, 0, width, axis=dim)
        tail = lax.slice_in_dim(cells, cells.shape[dim] - width, cells.shape[dim], axis=dim)
        cells = jnp.concatenate(
            [
                lax.ppermute(tail, axis, [(i, (i + 1) % count) for i in range(ends)]),
                cells,
                lax.ppermute(head, axis, [((i + 1) % count, i) for i in range(ends)]),
            ],
            axis=dim,
        )
    return cells


def passed_along(block, axis, distance):
    devices = range(lax.axis_size(axis))
    route = [(i - distance, i) for i in devices if i - distance in devices]
    return lax.ppermute(block, axis, route)


def below_along(values_in, which_axis):
    length = values_in.shape[which_axis]
    zero_plane = jnp.zeros_like(lax.slice_in_dim(values_in, 0, 1, axis=which_axis))
    return jnp.concatenate(
        [zero_plane, lax.slice_in_dim(values_in, 0, length - 1, axis=which_axis)], axis=which_axis
    )


def above_along(values_in, which_axis):
    length = values_in.shape[which_axis]
    zero_plane = jnp.zeros_like(lax.slice_in_dim(values_in, 0, 1, axis=which_axis))
    return jnp.concatenate(
        [lax.slice_in_dim(values_in, 1, length, axis=which_axis), zero_plane], axis=which_axis
    )


def restrict(values_in):
    shaped = values_in.reshape(
        values_in.shape[0], values_in.shape[1] // 2, 2, values_in.shape[2] // 2, 2
    )
    return shaped.mean(axis=(2, 4))


def prolong(values_in):
    return jnp.repeat(jnp.repeat(values_in, 2, axis=1), 2, axis=2)


def trap_capacity(stress, trap_class):
    trap_level = jnp.zeros(stress.shape, stress.dtype)
    for position in range(len(trap_levels)):
        trap_level = trap_level + jnp.where(
            trap_class == position, trap_levels[position], 0.0
        ).astype(stress.dtype)
    return (1.0 + trap_level) * jnp.exp(stress_coupling * stress)


def assemble(face_x, below_x, face_y, face_z, capacity, step_size):
    below_y = below_along(face_y, 1)
    below_z = below_along(face_z, 2)
    diagonal = capacity + step_size * (face_x + below_x + face_y + below_y + face_z + below_z)
    return (face_x, below_x, face_y, below_y, face_z, below_z, diagonal, capacity)


def coarse_coefficients(coeffs):
    return assemble(
        restrict(coeffs[0]),
        restrict(coeffs[1]),
        restrict(coeffs[2]) / 4.0,
        restrict(coeffs[4]) / 4.0,
        restrict(coeffs[7]),
        FINE_STEPS * time_step,
    )


def neighbour_sum(padded, coeffs):
    centre = padded[1:-1]
    result = coeffs[0] * padded[2:] + coeffs[1] * padded[:-2]
    result = result + coeffs[2] * above_along(centre, 1) + coeffs[3] * below_along(centre, 1)
    result = result + coeffs[4] * above_along(centre, 2) + coeffs[5] * below_along(centre, 2)
    return result


def fine_halo(values_in):
    return extended(values_in, (("space", 0),), 1)


def adjoint_halo(values_in):
    return extended(values_in, (("space", 0),), 1)


def coarse_apply(start, coarse):
    source = coarse[7] * start
    current = start
    for sweep_number in range(COARSE_SWEEPS):
        padded = extended(current, (("space", 0),), 1)
        current = (source + FINE_STEPS * time_step * neighbour_sum(padded, coarse)) / coarse[6]
    return current


def shards(start_states, diff_x, diff_y, diff_z, stress, trap_class, cotangent):
    capacity = trap_capacity(stress, trap_class)
    rim_plane = passed_along(diff_x[-1:], "space", 1)
    below_x = jnp.concatenate([rim_plane, diff_x[:-1]], axis=0)
    coeffs = assemble(diff_x, below_x, diff_y, diff_z, capacity, time_step)
    coarse = coarse_coefficients(coeffs)
    padded = fine_halo(start_states[0])
    stacks = []
    for step_number in range(FINE_STEPS):
        source = capacity * padded[1:-1]

        def sweep(carried, unused):
            field_new = (source + time_step * neighbour_sum(carried, coeffs)) / coeffs[6]
            return (fine_halo(field_new), carried)

        padded, inputs = lax.scan(sweep, padded, None, length=SWEEPS)
        stacks.append(inputs)
    following = padded
    span_end = following[1:-1]

    def back(carried, pair):
        adjoint_in, source_adj, grad_a, grad_b, grad_c = carried
        input_pad, output_pad = pair
        weighted = adjoint_in / coeffs[6]
        weighted_pad = adjoint_halo(weighted)
        field_in = input_pad[1:-1]
        field_out = output_pad[1:-1]
        grad_a = grad_a + time_step * (
            weighted * (input_pad[2:] - field_out) + weighted_pad[2:] * (field_in - output_pad[2:])
        )
        grad_b = grad_b + time_step * (
            weighted * (above_along(field_in, 1) - field_out)
            + above_along(weighted, 1) * (field_in - above_along(field_out, 1))
        )
        grad_c = grad_c + time_step * (
            weighted * (above_along(field_in, 2) - field_out)
            + above_along(weighted, 2) * (field_in - above_along(field_out, 2))
        )
        return (
            (
                time_step * neighbour_sum(weighted_pad, coeffs),
                source_adj + weighted,
                grad_a,
                grad_b,
                grad_c,
            ),
            None,
        )

    adjoint = cotangent[0]
    zero_field = jnp.zeros_like(span_end)
    local_grads = (zero_field, zero_field, zero_field)
    reduced_grads = None
    for step_number in reversed(range(FINE_STEPS)):
        inputs = stacks[step_number]
        outputs_pad = jnp.concatenate([inputs[1:], following[None]], axis=0)
        following = inputs[0]
        carried, leftover = lax.scan(
            back,
            (adjoint, zero_field, zero_field, zero_field, zero_field),
            (inputs, outputs_pad),
            reverse=True,
        )
        adjoint = carried[0] + capacity * carried[1]
        local_grads = (
            local_grads[0] + carried[2],
            local_grads[1] + carried[3],
            local_grads[2] + carried[4],
        )
    reduced_grads = (
        lax.psum_scatter(local_grads[0], "tm", scatter_dimension=1, tiled=True),
        lax.psum_scatter(local_grads[1], "tm", scatter_dimension=1, tiled=True),
        lax.psum_scatter(local_grads[2], "tm", scatter_dimension=1, tiled=True),
    )
    spans = lax.axis_size("tm")
    span_index = lax.axis_index("tm")
    next_start = passed_along(restrict(start_states[0]), "tm", -1)
    jumps = restrict(span_end) - next_start
    jumps = jnp.where(span_index == spans - 1, jnp.zeros_like(jumps), jumps)
    gathered = lax.all_gather(jumps[None], "tm", axis=0, tiled=True)
    coarse_state = gathered[0]
    own_state = jnp.where(span_index == 1, coarse_state, jnp.zeros_like(coarse_state))
    for turn in range(1, spans - 1):
        coarse_state = gathered[turn] + coarse_apply(coarse_state, coarse)
        own_state = jnp.where(span_index == turn + 1, coarse_state, own_state)
    jump_total = lax.psum(jnp.sum(gathered * gathered), "space")
    correction = coarse_apply(own_state, coarse)
    new_end = (span_end + prolong(correction))[None]
    cell_count = (spans - 1) * jumps.size * lax.axis_size("space")
    jump_norm = jnp.sqrt(jump_total / cell_count)
    return (new_end, reduced_grads[0], reduced_grads[1], reduced_grads[2], jump_norm)


def solution(mesh):
    in_specs = (
        P("tm", "space", None, None),
        P("space", None, None),
        P("space", None, None),
        P("space", None, None),
        P("space", None, None),
        P("space", None, None),
        P("tm", "space", None, None),
    )
    out_specs = (
        P("tm", "space", None, None),
        P("space", "tm", None),
        P("space", "tm", None),
        P("space", "tm", None),
        P(),
    )
    return jax.shard_map(shards, mesh=mesh, in_specs=in_specs, out_specs=out_specs, check_vma=False)
```

profile of v0, /device:TPU:0, one launch (start us, length us, event | category | flops | bytes accessed | tf_op | source)
XLA Modules:
  0.0 791.1 jit_solution(7009538209801719657)
XLA Ops:
  19.4 18.8 %reshape_squeeze.3 = f32[2,32,2,256,2]{4,3,2,1,0:T(8,128)} reshape(f32[1,2,64,512]{3,2,1,0:T(8,128)} %param.15) | data formatting | bytes 524288 | tf_op jit(solution)/shard_map/reshape;squeeze | solution.py:56
  38.3 8.0 %reduce_sum.74 = f32[2,32,256]{2,1,0:T(8,128)S(1)} reduce(f32[2,32,2,256,2]{4,3,2,1,0:T(8,128)} %reshape_squeeze.3, f32[]{:T(128)} %constant.149.clone.1), dimensions={2,4}, to_apply=%region_6.7 | reduce | flops 49152 | bytes 327684 | tf_op jit(solution)/shard_map/reduce_sum | solution.py:59
  48.5 18.1 %reshape.96 = f32[2,32,2,256,2]{4,3,2,1,0:T(8,128)} reshape(f32[2,64,512]{2,1,0:T(8,128)S(1)} %copy-done) | data formatting | bytes 524288 | tf_op jit(solution)/shard_map/reshape | solution.py:56
  66.6 18.1 %reshape.99 = f32[2,32,2,256,2]{4,3,2,1,0:T(8,128)} reshape(f32[2,64,512]{2,1,0:T(8,128)S(1)} %copy-done.1) | data formatting | bytes 524288 | tf_op jit(solution)/shard_map/reshape | solution.py:56
  84.7 8.0 %reduce_sum.78 = f32[2,32,256]{2,1,0:T(8,128)S(1)} reduce(f32[2,32,2,256,2]{4,3,2,1,0:T(8,128)} %reshape.99, f32[]{:T(128)} %constant.149.clone.1), dimensions={2,4}, to_apply=%region_10.11 | reduce | flops 49152 | bytes 327684 | tf_op jit(solution)/shard_map/reduce_sum | solution.py:59
  93.4 18.1 %reshape.98 = f32[2,32,2,256,2]{4,3,2,1,0:T(8,128)} reshape(f32[2,64,512]{2,1,0:T(8,128)S(1)} %copy-done.2) | data formatting | bytes 524288 | tf_op jit(solution)/shard_map/reshape | solution.py:56
  111.5 8.0 %reduce_sum.77 = f32[2,32,256]{2,1,0:T(8,128)S(1)} reduce(f32[2,32,2,256,2]{4,3,2,1,0:T(8,128)} %reshape.98, f32[]{:T(128)} %constant.149.clone.1), dimensions={2,4}, to_apply=%region_9.10 | reduce | flops 49152 | bytes 327684 | tf_op jit(solution)/shard_map/reduce_sum | solution.py:59
  119.5 8.7 %reduce_sum.75 = f32[2,32,256]{2,1,0:T(8,128)} reduce(f32[2,32,2,256,2]{4,3,2,1,0:T(8,128)} %reshape.96, f32[]{:T(128)} %constant.149.clone.1), dimensions={2,4}, to_apply=%region_7.8 | reduce | flops 49152 | bytes 327684 | tf_op jit(solution)/shard_map/reduce_sum | solution.py:59
  134.9 110.4 %while.68 = (s32[]{:T(128)}, f32[4,64,512]{2,1,0:T(8,128)S(1)}, f32[8,4,64,512]{3,2,1,0:T(8,128)}, f32[2,64,512]{2,1,0:T(8,128)S(1)}, f32[2,64,512]{2,1,0:T(8,12...) while((s32[]{:T(128)}, f32[4,64,512]{2,1,0:T(8,128)S(1)}, ...), condition=%wide.region_1.2_spmd, body=%wide.region_0.1_spmd.sunk | while | flops 1114114 | bytes 9671889 | solution.py:133
  248.9 109.1 %while.69 = (s32[]{:T(128)}, f32[4,64,512]{2,1,0:T(8,128)S(1)}, f32[8,4,64,512]{3,2,1,0:T(8,128)}, f32[2,64,512]{2,1,0:T(8,128)S(1)}, f32[2,64,512]{2,1,0:T(8,12...) while((s32[]{:T(128)}, f32[4,64,512]{2,1,0:T(8,128)S(1)}, ...), condition=%wide.region_3.4_spmd, body=%wide.region_2.3_spmd.sunk | while | flops 1114114 | bytes 9671889 | solution.py:133
  372.8 121.6 %while.70 = (s32[]{:T(128)}, f32[2,64,512]{2,1,0:T(8,128)S(1)}, f32[2,64,512]{2,1,0:T(8,128)}, f32[2,64,512]{2,1,0:T(8,128)}, f32[2,64,512]{2,1,0:T(8,128)}, /*i...) while((s32[]{:T(128)}, f32[2,64,512]{2,1,0:T(8,128)S(1)}, ...), condition=%wide.region_12.13_spmd.clone, body=%wide.region_11.12_spmd.clone.sunk | while | flops 2490374 | bytes 20518832 | solution.py:175
  421.6 6.2 collective-permute-start.4
  501.1 119.4 %while.71 = (s32[]{:T(128)}, f32[2,64,512]{2,1,0:T(8,128)}, f32[2,64,512]{2,1,0:T(8,128)}, f32[2,64,512]{2,1,0:T(8,128)S(1)}, f32[2,64,512]{2,1,0:T(8,128)S(1)},...) while((s32[]{:T(128)}, f32[2,64,512]{2,1,0:T(8,128)}, ...), condition=%wide.region_14.15_spmd.clone, body=%wide.region_13.14_spmd.clone.sunk | while | flops 2359302 | bytes 15800120 | solution.py:175
  504.2 6.1 collective-permute-start.6
  518.6 6.1 collective-permute-start.6
  533.2 6.1 collective-permute-start.6
  622.6 18.1 %reshape.95 = f32[2,32,2,256,2]{4,3,2,1,0:T(8,128)} reshape(f32[2,64,512]{2,1,0:T(8,128)S(1)} %copy.25) | data formatting | bytes 524288 | tf_op jit(solution)/shard_map/reshape | solution.py:56
  640.7 8.1 %reduce_sum.73 = f32[2,32,256]{2,1,0:T(8,128)S(1)} reduce(f32[2,32,2,256,2]{4,3,2,1,0:T(8,128)} %reshape.95, f32[]{:T(128)} %constant.149.clone.1), dimensions={2,4}, to_apply=%region_5.6 | reduce | flops 49152 | bytes 327684 | tf_op jit(solution)/shard_map/reduce_sum | solution.py:59
  649.6 6.4 all-gather
  664.4 20.9 %psum.7 = f32[]{:T(128)} all-reduce(f32[]{:T(128)} %multiply_reduce_fusion), channel_id=1, replica_groups=mesh['tm'=4,'space'=8] {'space'}, use_global_device_ids=true, to_apply=%region_19.20 | all-reduce | flops 1 | bytes 8 | tf_op jit(solution)/shard_map/psum | solution.py:203
  685.3 18.1 %reshape.97 = f32[2,32,2,256,2]{4,3,2,1,0:T(8,128)} reshape(f32[2,64,512]{2,1,0:T(8,128)S(1)} %get-tuple-element.1588) | data formatting | bytes 524288 | tf_op jit(solution)/shard_map/reshape | solution.py:56
  703.4 18.1 %reshape.94 = f32[2,32,2,256,2]{4,3,2,1,0:T(8,128)} reshape(f32[2,64,512]{2,1,0:T(8,128)S(1)} %copy-done.14) | data formatting | bytes 524288 | tf_op jit(solution)/shard_map/reshape | solution.py:56
  722.9 8.1 %reduce_sum.76 = f32[2,32,256]{2,1,0:T(8,128)S(1)} reduce(f32[2,32,2,256,2]{4,3,2,1,0:T(8,128)} %reshape.97, f32[]{:T(128)} %constant.149.clone.1), dimensions={2,4}, to_apply=%region_8.9 | reduce | flops 49152 | bytes 327684 | tf_op jit(solution)/shard_map/reduce_sum | solution.py:59
  731.1 8.1 %reduce_sum.72 = f32[2,32,256]{2,1,0:T(8,128)S(1)} reduce(f32[2,32,2,256,2]{4,3,2,1,0:T(8,128)} %reshape.94, f32[]{:T(128)} %constant.149.clone.1), dimensions={2,4}, to_apply=%region_4.5 | reduce | flops 49152 | bytes 327684 | tf_op jit(solution)/shard_map/reduce_sum | solution.py:59
  (610 shorter events, 535.4 us)
Async XLA Ops:
  7.2 775.8 %reduce-scatter.8.cloned.1.call-start = ((), (), s32[]{:S(2)}) async-start(), calls=%async_computation.5 | async-start | bytes 327680 | tf_op jit(solution)/shard_map/reduce_scatter | solution.py:190
  8.2 120.6 %collective-permute-start.10 = (f32[1,64,512]{2,1,0:T(8,128)S(1)}, f32[1,64,512]{2,1,0:T(8,128)S(1)}, u32[]{:S(2)}, u32[]{:S(2)}) collective-permute-start(f32[1,64,512]{2,1,0:T(8,128)S(1)} %get-tuple-element.968), channel_id=1, source_target_pairs={{0,1},{1,2},{2,3},{3,4},{4,5},{5,6},{6,7},{8,9},{9,10},{10,11},{11... | collective-permute-start | bytes 393224 | tf_op jit(solution)/shard_map/ppermute | solution.py:36
  14.1 116.7 %collective-permute-start.8 = (f32[1,64,512]{2,1,0:T(8,128)S(1)}, f32[1,64,512]{2,1,0:T(8,128)}, u32[]{:S(2)}, u32[]{:S(2)}) collective-permute-start(f32[1,64,512]{2,1,0:T(8,128)S(1)} %get-tuple-element.970), channel_id=1, source_target_pairs={{0,1},{1,2},{2,3},{3,4},{4,5},{5,6},{6,7},{8,9},{9,10},{10,11},{11... | collective-permute-start | bytes 393224 | tf_op jit(solution)/shard_map/ppermute | solution.py:24
  18.2 112.6 %collective-permute-start.9 = (f32[1,64,512]{2,1,0:T(8,128)S(1)}, f32[1,64,512]{2,1,0:T(8,128)}, u32[]{:S(2)}, u32[]{:S(2)}) collective-permute-start(f32[1,64,512]{2,1,0:T(8,128)S(1)} %get-tuple-element.971), channel_id=1, source_target_pairs={{1,0},{2,1},{3,2},{4,3},{5,4},{6,5},{7,6},{9,8},{10,9},{11,10},{12... | collective-permute-start | bytes 393224 | tf_op jit(solution)/shard_map/ppermute | solution.py:26
  47.0 601.8 %collective-permute-start.11 = (f32[2,32,256]{2,1,0:T(8,128)}, f32[2,32,256]{2,1,0:T(8,128)}, u32[]{:S(2)}, u32[]{:S(2)}) collective-permute-start(f32[2,32,256]{2,1,0:T(8,128)} %broadcast_multiply_fusion.2), channel_id=1, source_target_pairs={{8,0},{16,8},{24,16},{9,1},{17,9},{25,17},{10,2},{18,10},{26,18},{... | collective-permute-start | bytes 196616 | tf_op jit(solution)/shard_map/ppermute | solution.py:36
  137.5 11.0 %collective-permute-start.1 = (f32[1,64,512]{2,1,0:T(8,128)S(1)}, f32[1,64,512]{2,1,0:T(8,128)}, u32[]{:S(2)}, u32[]{:S(2)}) collective-permute-start(f32[1,64,512]{2,1,0:T(8,128)S(1)} %get-tuple-element.1313), channel_id=1, source_target_pairs={{0,1},{1,2},{2,3},{3,4},{4,5},{5,6},{6,7},{8,9},{9,10},{10,11},{11... | collective-permute-start | bytes 393224 | tf_op jit(solution)/shard_map/while/body/eval_jaxpr/ppermute | solution.py:24
  152.1 10.1 %collective-permute-start.1 = (f32[1,64,512]{2,1,0:T(8,128)S(1)}, f32[1,64,512]{2,1,0:T(8,128)}, u32[]{:S(2)}, u32[]{:S(2)}) collective-permute-start(f32[1,64,512]{2,1,0:T(8,128)S(1)} %get-tuple-element.1313), channel_id=1, source_target_pairs={{0,1},{1,2},{2,3},{3,4},{4,5},{5,6},{6,7},{8,9},{9,10},{10,11},{11... | collective-permute-start | bytes 393224 | tf_op jit(solution)/shard_map/while/body/eval_jaxpr/ppermute | solution.py:24
  165.9 10.1 %collective-permute-start.1 = (f32[1,64,512]{2,1,0:T(8,128)S(1)}, f32[1,64,512]{2,1,0:T(8,128)}, u32[]{:S(2)}, u32[]{:S(2)}) collective-permute-start(f32[1,64,512]{2,1,0:T(8,128)S(1)} %get-tuple-element.1313), channel_id=1, source_target_pairs={{0,1},{1,2},{2,3},{3,4},{4,5},{5,6},{6,7},{8,9},{9,10},{10,11},{11... | collective-permute-start | bytes 393224 | tf_op jit(solution)/shard_map/while/body/eval_jaxpr/ppermute | solution.py:24
  179.5 10.0 %collective-permute-start.1 = (f32[1,64,512]{2,1,0:T(8,128)S(1)}, f32[1,64,512]{2,1,0:T(8,128)}, u32[]{:S(2)}, u32[]{:S(2)}) collective-permute-start(f32[1,64,512]{2,1,0:T(8,128)S(1)} %get-tuple-element.1313), channel_id=1, source_target_pairs={{0,1},{1,2},{2,3},{3,4},{4,5},{5,6},{6,7},{8,9},{9,10},{10,11},{11... | collective-permute-start | bytes 393224 | tf_op jit(solution)/shard_map/while/body/eval_jaxpr/ppermute | solution.py:24
  193.1 10.0 %collective-permute-start.1 = (f32[1,64,512]{2,1,0:T(8,128)S(1)}, f32[1,64,512]{2,1,0:T(8,128)}, u32[]{:S(2)}, u32[]{:S(2)}) collective-permute-start(f32[1,64,512]{2,1,0:T(8,128)S(1)} %get-tuple-element.1313), channel_id=1, source_target_pairs={{0,1},{1,2},{2,3},{3,4},{4,5},{5,6},{6,7},{8,9},{9,10},{10,11},{11... | collective-permute-start | bytes 393224 | tf_op jit(solution)/shard_map/while/body/eval_jaxpr/ppermute | solution.py:24
  220.4 10.0 %collective-permute-start.1 = (f32[1,64,512]{2,1,0:T(8,128)S(1)}, f32[1,64,512]{2,1,0:T(8,128)}, u32[]{:S(2)}, u32[]{:S(2)}) collective-permute-start(f32[1,64,512]{2,1,0:T(8,128)S(1)} %get-tuple-element.1313), channel_id=1, source_target_pairs={{0,1},{1,2},{2,3},{3,4},{4,5},{5,6},{6,7},{8,9},{9,10},{10,11},{11... | collective-permute-start | bytes 393224 | tf_op jit(solution)/shard_map/while/body/eval_jaxpr/ppermute | solution.py:24
  251.5 10.0 %collective-permute-start.3 = (f32[1,64,512]{2,1,0:T(8,128)S(1)}, f32[1,64,512]{2,1,0:T(8,128)}, u32[]{:S(2)}, u32[]{:S(2)}) collective-permute-start(f32[1,64,512]{2,1,0:T(8,128)S(1)} %get-tuple-element.1330), channel_id=1, source_target_pairs={{0,1},{1,2},{2,3},{3,4},{4,5},{5,6},{6,7},{8,9},{9,10},{10,11},{11... | collective-permute-start | bytes 393224 | tf_op jit(solution)/shard_map/while/body/eval_jaxpr/ppermute | solution.py:24
  278.7 10.0 %collective-permute-start.3 = (f32[1,64,512]{2,1,0:T(8,128)S(1)}, f32[1,64,512]{2,1,0:T(8,128)}, u32[]{:S(2)}, u32[]{:S(2)}) collective-permute-start(f32[1,64,512]{2,1,0:T(8,128)S(1)} %get-tuple-element.1330), channel_id=1, source_target_pairs={{0,1},{1,2},{2,3},{3,4},{4,5},{5,6},{6,7},{8,9},{9,10},{10,11},{11... | collective-permute-start | bytes 393224 | tf_op jit(solution)/shard_map/while/body/eval_jaxpr/ppermute | solution.py:24
  292.4 10.0 %collective-permute-start.3 = (f32[1,64,512]{2,1,0:T(8,128)S(1)}, f32[1,64,512]{2,1,0:T(8,128)}, u32[]{:S(2)}, u32[]{:S(2)}) collective-permute-start(f32[1,64,512]{2,1,0:T(8,128)S(1)} %get-tuple-element.1330), channel_id=1, source_target_pairs={{0,1},{1,2},{2,3},{3,4},{4,5},{5,6},{6,7},{8,9},{9,10},{10,11},{11... | collective-permute-start | bytes 393224 | tf_op jit(solution)/shard_map/while/body/eval_jaxpr/ppermute | solution.py:24
  306.0 10.0 %collective-permute-start.3 = (f32[1,64,512]{2,1,0:T(8,128)S(1)}, f32[1,64,512]{2,1,0:T(8,128)}, u32[]{:S(2)}, u32[]{:S(2)}) collective-permute-start(f32[1,64,512]{2,1,0:T(8,128)S(1)} %get-tuple-element.1330), channel_id=1, source_target_pairs={{0,1},{1,2},{2,3},{3,4},{4,5},{5,6},{6,7},{8,9},{9,10},{10,11},{11... | collective-permute-start | bytes 393224 | tf_op jit(solution)/shard_map/while/body/eval_jaxpr/ppermute | solution.py:24
  375.6 10.1 %collective-permute-start.4 = (f32[1,64,512]{2,1,0:T(8,128)}, f32[1,64,512]{2,1,0:T(8,128)}, u32[]{:S(2)}, u32[]{:S(2)}) collective-permute-start(f32[1,64,512]{2,1,0:T(8,128)} %get-tuple-element.1347), channel_id=1, source_target_pairs={{0,1},{1,2},{2,3},{3,4},{4,5},{5,6},{6,7},{8,9},{9,10},{10,11},{11... | collective-permute-start | bytes 393224 | tf_op jit(solution)/shard_map/while/body/eval_jaxpr/ppermute | solution.py:24
  533.2 10.2 %collective-permute-start.6 = (f32[1,64,512]{2,1,0:T(8,128)}, f32[1,64,512]{2,1,0:T(8,128)}, u32[]{:S(2)}, u32[]{:S(2)}) collective-permute-start(f32[1,64,512]{2,1,0:T(8,128)} %get-tuple-element.1373), channel_id=1, source_target_pairs={{0,1},{1,2},{2,3},{3,4},{4,5},{5,6},{6,7},{8,9},{9,10},{10,11},{11... | collective-permute-start | bytes 393224 | tf_op jit(solution)/shard_map/while/body/eval_jaxpr/ppermute | solution.py:24
  548.3 11.0 %collective-permute-start.6 = (f32[1,64,512]{2,1,0:T(8,128)}, f32[1,64,512]{2,1,0:T(8,128)}, u32[]{:S(2)}, u32[]{:S(2)}) collective-permute-start(f32[1,64,512]{2,1,0:T(8,128)} %get-tuple-element.1373), channel_id=1, source_target_pairs={{0,1},{1,2},{2,3},{3,4},{4,5},{5,6},{6,7},{8,9},{9,10},{10,11},{11... | collective-permute-start | bytes 393224 | tf_op jit(solution)/shard_map/while/body/eval_jaxpr/ppermute | solution.py:24
  564.3 10.1 %collective-permute-start.6 = (f32[1,64,512]{2,1,0:T(8,128)}, f32[1,64,512]{2,1,0:T(8,128)}, u32[]{:S(2)}, u32[]{:S(2)}) collective-permute-start(f32[1,64,512]{2,1,0:T(8,128)} %get-tuple-element.1373), channel_id=1, source_target_pairs={{0,1},{1,2},{2,3},{3,4},{4,5},{5,6},{6,7},{8,9},{9,10},{10,11},{11... | collective-permute-start | bytes 393224 | tf_op jit(solution)/shard_map/while/body/eval_jaxpr/ppermute | solution.py:24
  579.4 10.1 %collective-permute-start.6 = (f32[1,64,512]{2,1,0:T(8,128)}, f32[1,64,512]{2,1,0:T(8,128)}, u32[]{:S(2)}, u32[]{:S(2)}) collective-permute-start(f32[1,64,512]{2,1,0:T(8,128)} %get-tuple-element.1373), channel_id=1, source_target_pairs={{0,1},{1,2},{2,3},{3,4},{4,5},{5,6},{6,7},{8,9},{9,10},{10,11},{11... | collective-permute-start | bytes 393224 | tf_op jit(solution)/shard_map/while/body/eval_jaxpr/ppermute | solution.py:24
  621.3 161.6 %reduce-scatter.6.cloned.1.call-start = ((), (), s32[]{:S(2)}) async-start(), calls=%async_computation.4 | async-start | bytes 327680 | tf_op jit(solution)/shard_map/reduce_scatter | solution.py:189
  656.0 83.2 %collective-permute-start.12 = (f32[1,32,256]{2,1,0:T(8,128)S(1)}, f32[1,32,256]{2,1,0:T(8,128)S(1)}, u32[]{:S(2)}, u32[]{:S(2)}) collective-permute-start(f32[1,32,256]{2,1,0:T(8,128)S(1)} %get-tuple-element.963), channel_id=1, source_target_pairs={{1,0},{2,1},{3,2},{4,3},{5,4},{6,5},{7,6},{9,8},{10,9},{11,10},{12... | collective-permute-start | bytes 98312 | tf_op jit(solution)/shard_map/ppermute | solution.py:26
  657.3 81.9 %collective-permute-start.13 = (f32[1,32,256]{2,1,0:T(8,128)S(1)}, f32[1,32,256]{2,1,0:T(8,128)S(1)}, u32[]{:S(2)}, u32[]{:S(2)}) collective-permute-start(f32[1,32,256]{2,1,0:T(8,128)S(1)} %get-tuple-element.964), channel_id=1, source_target_pairs={{0,1},{1,2},{2,3},{3,4},{4,5},{5,6},{6,7},{8,9},{9,10},{10,11},{11... | collective-permute-start | bytes 98312 | tf_op jit(solution)/shard_map/ppermute | solution.py:24
  663.6 119.4 %reduce-scatter.4.cloned.1.call-start = ((), (), s32[]{:S(2)}) async-start(), calls=%async_computation.3 | async-start | bytes 327680 | tf_op jit(solution)/shard_map/reduce_scatter | solution.py:188
  (114 other events, 1015.4 us)
Sparse Core Ops, SparseCore 0:
  621.4 22.6 reduce-scatter.7
  663.7 21.4 reduce-scatter.5
  723.0 17.3 reduce-scatter.3
where the time goes:
time: 802 us; the launch traced here: 791 us
  starting transfers between devices  281 us (35%)
  local copies, waits for them, and re-layouts  200 us (25%)
  other arithmetic  187 us (23%)
  waiting for transfers between devices  75.5 us (9%)
  blocking collectives  27.3 us (3%)
  between operations  16.7 us (2%)
    ppermute x39, starting transfers between devices, extended(): lax.ppermute(tail, axis, [(i, (i + 1) % count) for i in range(ends)])  225 us
    reshape x6, local copies, waits for them, and re-layouts, restrict(): values_in.reshape(values_in.shape[0], values_in.shape[1] // 2, 2, values_...  108 us
    ppermute x39, waiting for transfers between devices, extended(): lax.ppermute(tail, axis, [(i, (i + 1) % count) for i in range(ends)])  57.2 us
    reduce_sum x7, other arithmetic, restrict(): return shaped.mean(axis=(2, 4))  57.1 us
    ppermute x39, starting transfers between devices, extended(): lax.ppermute(head, axis, [((i + 1) % count, i) for i in range(ends)])  50.1 us
    add x16, other arithmetic, back(): grad_a + time_step * (weighted * (input_pad[2:] - field_out) + weighted_p...  34.2 us
    add x16, other arithmetic, neighbour_sum(): result + coeffs[4] * above_along(centre, 2)  25.6 us
    psum x1, blocking collectives, shards(): jump_total = lax.psum(jnp.sum(gathered * gathered), 'space')  20.9 us
  transfers between devices with their start and end apart: 83, of which 60 were waited for; matrix products, arithmetic and copies ran while one was open for 48% of the time, Pallas kernels for 0%

commit v1 on v0

v1 whole, which is shorter than its diff:
```python
import functools

import jax
import jax.numpy as jnp
from jax import lax
from jax.experimental import pallas as pl
from jax.experimental.pallas import tpu as pltpu
from jax.sharding import PartitionSpec as P

FINE_STEPS = 2
SWEEPS = 8
COARSE_SWEEPS = 2
TOTAL = FINE_STEPS * SWEEPS
LANES = 128
SUB = 8

STRESS_COUPLING = 0.5
TIME_STEP = 1.0
COARSE_STEP = FINE_STEPS * TIME_STEP
TRAP_LEVELS = (0.0, 1.0, 3.0, 7.0)

VMEM_BYTES = 56 * 1024 * 1024


class Sizes:
    def __init__(self, spans, space, planes, ny, nz):
        self.spans = spans
        self.space = space
        self.planes = planes
        self.nx = planes * space
        self.ny = ny
        self.nz = nz
        self.own = nz // space
        self.halo = (LANES - self.own) // 2
        self.quarter = ny // spans
        self.factor = LANES // self.own
        self.grad_parts = 3 * self.quarter // SUB
        self.grad_tiles = -(-self.grad_parts // self.factor)
        self.end_parts = ny // SUB
        self.end_tiles = self.end_parts // self.factor
        self.grad_rows = planes * self.grad_tiles * SUB
        self.end_rows = planes * self.end_tiles * SUB
        self.out_rows = self.grad_rows + self.end_rows + SUB
        assert TOTAL + 2 * COARSE_SWEEPS * (spans - 1) <= self.halo


def lane_of(shape):
    return lax.broadcasted_iota(jnp.int32, shape, len(shape) - 1)


def row_of(shape):
    return lax.broadcasted_iota(jnp.int32, shape, len(shape) - 2)


def z_up(v, by=1):
    return pltpu.roll(v, LANES - by, 1)


def z_down(v, by=1):
    return pltpu.roll(v, by, 1)


def roll_lanes(v, by):
    by = by % LANES
    return v if by == 0 else pltpu.roll(v, by, 1)


def windows_kernel(sz, start_ref, fx_ref, fy_ref, fz_ref, stress_ref, trap_ref, cot_ref, coef_out, start_out, cot_out):
    turn = lax.axis_index("tm")
    rows = pl.ds(pl.multiple_of(turn * sz.quarter, SUB), sz.quarter)
    tiles = sz.nz // LANES

    def cut(block_of, height, out_ref, row):
        parts = [block_of(n) for n in range(tiles)]
        lane = lane_of((height, LANES))
        for j in range(sz.space):
            first = sz.own * j - sz.halo
            tile, shift = first // LANES, first % LANES
            low = parts[tile] if 0 <= tile < tiles else None
            high = parts[tile + 1] if shift and tile + 1 < tiles else None
            zero = jnp.zeros((height, LANES), jnp.float32)
            low = zero if low is None else roll_lanes(low, -shift)
            if shift:
                high = zero if high is None else roll_lanes(high, -shift)
                low = jnp.where(lane < LANES - shift, low, high)
            out_ref[j, row : row + height, :] = low

    for p in range(sz.planes):
        span = lambda n: slice(n * LANES, (n + 1) * LANES)

        def capacity(n):
            trap = trap_ref[p, rows, span(n)]
            level = jnp.zeros(trap.shape, jnp.float32)
            for position, value in enumerate(TRAP_LEVELS):
                level = level + jnp.where(trap == position, value, 0.0)
            return (1.0 + level) * jnp.exp(STRESS_COUPLING * stress_ref[p, rows, span(n)])

        for f, ref in enumerate((fx_ref, fy_ref, fz_ref)):
            cut(lambda n: ref[p, rows, span(n)], sz.quarter, coef_out, (f * sz.planes + p) * sz.quarter)
        cut(capacity, sz.quarter, coef_out, (3 * sz.planes + p) * sz.quarter)
        for ref, out in ((start_ref, start_out), (cot_ref, cot_out)):
            for r in range(0, sz.ny, 16):
                cut(lambda n: ref[0, p, r : r + 16, span(n)], 16, out, p * sz.ny + r)


def valid_columns(sz):
    lane = lane_of((sz.ny, LANES))
    column = lax.axis_index("space") * sz.own - sz.halo + lane
    return (column >= 0) & (column < sz.nz)


def lay_out_faces(sz, pieces, faces):
    turn = lax.axis_index("tm")
    for key, piece in enumerate(pieces):
        rows = pl.ds(pl.multiple_of((turn ^ key) * sz.quarter, SUB), sz.quarter)
        for f in range(4):
            for p in range(sz.planes):
                first = (f * sz.planes + p) * sz.quarter
                for s in range(sz.space):
                    faces[f, s * sz.planes + p, rows, :] = piece[s, first : first + sz.quarter, :]


def row_down(v, by=1):
    return jnp.where(row_of(v.shape) < by, 0.0, pltpu.roll(v, by, 0))


def row_up(v, by=1):
    size = v.shape[0]
    return jnp.where(row_of(v.shape) >= size - by, 0.0, pltpu.roll(v, size - by, 0))


def averaged(v):
    lane, row = lane_of(v.shape), row_of(v.shape)
    v = v + jnp.where(lane % 2 == 0, z_up(v), z_down(v))
    size = v.shape[0]
    v = v + jnp.where(row % 2 == 0, pltpu.roll(v, size - 1, 0), pltpu.roll(v, 1, 0))
    return 0.25 * v


PAD = 8


def clear_rim(ref, at, nx, ny):
    zero = jnp.zeros((ny + 2 * PAD, LANES), jnp.float32)
    ref[at + (0,)] = zero
    ref[at + (nx + 1,)] = zero
    edge = jnp.zeros((PAD, LANES), jnp.float32)
    for i in range(1, nx + 1):
        ref[at + (i, slice(0, PAD))] = edge
        ref[at + (i, slice(PAD + ny, 2 * PAD + ny))] = edge


def fine_kernel(sz, *refs):
    pieces = refs[: sz.spans]
    start_ref, cot_ref, end_out, rough_out, grads_out = refs[sz.spans : sz.spans + 5]
    faces, coef, u, w, source, total, sx, sy, sz_acc, product = refs[sz.spans + 5 :]
    nx, ny = sz.nx, sz.ny
    body = slice(PAD, PAD + ny)
    XP, XM, YP, YM, ZP, ZM, CAP, INV = range(8)

    lay_out_faces(sz, pieces, faces)

    def clear_u(k, c):
        clear_rim(u, (k,), nx, ny)
        return c

    lax.fori_loop(0, TOTAL + 1, clear_u, 0)
    clear_rim(w, (0,), nx, ny)
    clear_rim(w, (1,), nx, ny)
    clear_rim(product, (), nx, ny)

    valid = valid_columns(sz)

    def normalise(i, c):
        fx, fy, fz, cap = (faces[f, i] for f in range(4))
        bx = jnp.where(i == 0, 0.0, faces[0, jnp.maximum(i - 1, 0)])
        by, bz = row_down(fy), z_down(fz)
        diagonal = cap + TIME_STEP * (fx + bx + fy + by + fz + bz)
        inv = jnp.where(valid, 1.0 / diagonal, 0.0)
        scaled = TIME_STEP * inv
        for n, face in ((XP, fx), (XM, bx), (YP, fy), (YM, by), (ZP, fz), (ZM, bz)):
            coef[n, i] = face * scaled
        coef[CAP, i] = cap * inv
        coef[INV, i] = inv
        return c

    lax.fori_loop(0, nx, normalise, 0)

    for s in range(sz.space):
        for p in range(sz.planes):
            i = s * sz.planes + p
            rows = slice(p * ny, (p + 1) * ny)
            u[0, i + 1, body, :] = start_ref[s, rows, :]
            w[0, i + 1, body, :] = coef[INV, i] * cot_ref[s, rows, :]

    def moved(i, ref, at):
        v = ref[at, i + 1, body, :]
        return (
            v,
            ref[at, i + 2, body, :],
            ref[at, i, body, :],
            ref[at, i + 1, PAD + 1 : PAD + 1 + ny, :],
            ref[at, i + 1, PAD - 1 : PAD - 1 + ny, :],
            z_up(v),
            z_down(v),
        )

    def gathered(i, near):
        result = coef[0, i] * near[0]
        for n in range(1, 6):
            result = result + coef[n, i] * near[n]
        return result

    for step in range(FINE_STEPS):
        base = step * SWEEPS

        def set_source(i, c):
            source[i] = coef[CAP, i] * u[base, i + 1, body, :]
            return c

        lax.fori_loop(0, nx, set_source, 0)

        def sweep(k, c):
            def plane(i, c):
                near = moved(i, u, k)
                u[k + 1, i + 1, body, :] = source[i] + gathered(i, near[1:])
                return c

            return lax.fori_loop(0, nx, plane, c)

        lax.fori_loop(base, base + SWEEPS, sweep, 0)

    lane, row = lane_of((SUB, LANES)), row_of((SUB, LANES))

    def finish(i, c):
        end = u[TOTAL, i + 1, body, :]
        end_out[i] = end
        rough_out[i] = packed(averaged(end))
        return c

    lax.fori_loop(0, nx, finish, 0)

    def zero_plane(i, c):
        zero = jnp.zeros((ny, LANES), jnp.float32)
        sx[i] = zero
        sy[i] = zero
        sz_acc[i] = zero
        product[i + 1, body, :] = zero
        return c

    lax.fori_loop(0, nx, zero_plane, 0)

    for step in reversed(range(FINE_STEPS)):
        base = step * SWEEPS

        def zero_total(i, c):
            total[i] = jnp.zeros((ny, LANES), jnp.float32)
            return c

        lax.fori_loop(0, nx, zero_total, 0)

        def back(n, c):
            k = base + SWEEPS - 1 - n
            now, later = n % 2, (n + 1) % 2

            def plane(i, c):
                near = moved(i, w, now)
                v, xp, yp, zp = near[0], near[1], near[3], near[5]
                field = u[k, i + 1, body, :]
                sx[i] = sx[i] + (v * u[k, i + 2, body, :] + xp * field)
                sy[i] = sy[i] + (v * u[k, i + 1, PAD + 1 : PAD + 1 + ny, :] + yp * field)
                sz_acc[i] = sz_acc[i] + (v * z_up(field) + zp * field)
                product[i + 1, body, :] = product[i + 1, body, :] + v * u[k + 1, i + 1, body, :]
                total[i] = total[i] + v
                w[later, i + 1, body, :] = gathered(i, near[1:])
                return c

            return lax.fori_loop(0, nx, plane, c)

        lax.fori_loop(0, SWEEPS, back, 0)

        if step:

            def restart(i, c):
                w[0, i + 1, body, :] = w[0, i + 1, body, :] + coef[CAP, i] * total[i]
                return c

            lax.fori_loop(0, nx, restart, 0)

    turn = lax.axis_index("tm")

    def write_grads(i, c):
        own = product[i + 1, body, :]
        dest, p = i // sz.planes, i % sz.planes
        sx[i] = TIME_STEP * (sx[i] - own - product[i + 2, body, :])
        sy[i] = TIME_STEP * (sy[i] - own - product[i + 1, PAD + 1 : PAD + 1 + ny, :])
        sz_acc[i] = TIME_STEP * (sz_acc[i] - own - z_up(own))
        for key in range(sz.spans):
            first = (turn ^ key) * sz.quarter
            for g in range(sz.grad_tiles):
                tile = None
                for q in range(sz.factor):
                    n = g * sz.factor + q
                    if n >= sz.grad_parts:
                        continue
                    f, r = divmod(n, sz.quarter // SUB)
                    rows = pl.ds(pl.multiple_of(first + r * SUB, SUB), SUB)
                    part = roll_lanes((sx, sy, sz_acc)[f][i, rows, :], sz.own * q - sz.halo)
                    tile = part if tile is None else jnp.where(lane < sz.own * q, tile, part)
                at = pl.multiple_of((p * sz.grad_tiles + g) * SUB, SUB)
                grads_out[key, dest, pl.ds(at, SUB), :] = tile
        return c

    lax.fori_loop(0, nx, write_grads, 0)


def packed(v):
    lane = lane_of((SUB, LANES))
    row = row_of((SUB, LANES))
    out = []
    for n in range(v.shape[0] // (4 * SUB)):
        tile = None
        for q in range(4):
            part = v[(4 * n + q) * SUB : (4 * n + q + 1) * SUB]
            keep = (lane % 2) + 2 * (row % 2)
            tile = part if tile is None else jnp.where(keep == q, part, tile)
        out.append(tile)
    return jnp.concatenate(out, axis=0)


def unpacked(v):
    lane = lane_of((SUB, LANES))
    row = row_of((SUB, LANES))
    out = []
    for n in range(v.shape[0] // SUB):
        tile = v[n * SUB : (n + 1) * SUB]
        for q in range(4):
            part = jnp.where(lane % 2 == q % 2, tile, z_up(tile) if q % 2 else z_down(tile))
            low = q // 2
            turned = pltpu.roll(part, SUB - 1 if low else 1, 0)
            out.append(jnp.where(row % 2 == low, part, turned))
    return jnp.concatenate(out, axis=0)


def rough_kernel(sz, start_ref, out_ref):
    for s in range(sz.space):
        for p in range(sz.planes):
            out_ref[s * sz.planes + p] = packed(averaged(start_ref[s, p * sz.ny : (p + 1) * sz.ny, :]))


def coarse_kernel(sz, *refs):
    pieces = refs[: sz.spans]
    jumps_ref, end_ref, out_ref = refs[sz.spans : sz.spans + 3]
    faces, coef, state, source = refs[sz.spans + 3 :]
    nx, ny = sz.nx, sz.ny
    body = slice(PAD, PAD + ny)
    turn = lax.axis_index("tm")
    lay_out_faces(sz, pieces, faces)
    for n in range(COARSE_SWEEPS + 1):
        clear_rim(state, (n,), nx, ny)
    valid = valid_columns(sz)

    def restricted(i, c):
        faces[0, i] = averaged(faces[0, i])
        faces[1, i] = 0.25 * averaged(faces[1, i])
        faces[2, i] = 0.25 * averaged(faces[2, i])
        faces[3, i] = averaged(faces[3, i])
        return c

    lax.fori_loop(0, nx, restricted, 0)

    def normalise(i, c):
        fx, fy, fz, cap = (faces[f, i] for f in range(4))
        bx = jnp.where(i == 0, 0.0, faces[0, jnp.maximum(i - 1, 0)])
        by, bz = row_down(fy, 2), z_down(fz, 2)
        diagonal = cap + COARSE_STEP * (fx + bx + fy + by + fz + bz)
        inv = jnp.where(valid, 1.0 / diagonal, 0.0)
        scaled = COARSE_STEP * inv
        for n, face in enumerate((fx, bx, fy, by, fz, bz)):
            coef[n, i] = face * scaled
        coef[6, i] = cap * inv
        return c

    lax.fori_loop(0, nx, normalise, 0)

    lane = lane_of((jumps_ref.shape[2], LANES))
    mine = (lane >= sz.halo) & (lane < sz.halo + sz.own)

    def squares(i, c):
        for k in range(sz.spans - 1):
            jump = jnp.where(mine, jumps_ref[k, i], 0.0)
            c = c + jump * jump
        return c

    square = lax.fori_loop(0, nx, squares, jnp.zeros((jumps_ref.shape[2], LANES), jnp.float32))
    square = functools.reduce(lambda a, b: a + b, [square[n : n + SUB] for n in range(0, square.shape[0], SUB)])

    def begin(i, c):
        state[0, i + 1, body, :] = jnp.zeros((ny, LANES), jnp.float32)
        state[COARSE_SWEEPS, i + 1, body, :] = jnp.zeros((ny, LANES), jnp.float32)
        return c

    lax.fori_loop(0, nx, begin, 0)

    for d in reversed(range(1, sz.spans)):
        which = jnp.maximum(turn - d, 0)
        there = turn >= d

        def take(i, c):
            jump = jnp.where(there, unpacked(jumps_ref[which, i]), 0.0)
            now = state[COARSE_SWEEPS, i + 1, body, :] + jump
            state[0, i + 1, body, :] = now
            source[i] = coef[6, i] * now
            return c

        lax.fori_loop(0, nx, take, 0)
        for n in range(COARSE_SWEEPS):

            def plane(i, c):
                v = state[n, i + 1, body, :]
                result = source[i] + coef[0, i] * state[n, i + 2, body, :] + coef[1, i] * state[n, i, body, :]
                result = result + coef[2, i] * state[n, i + 1, PAD + 2 : PAD + 2 + ny, :]
                result = result + coef[3, i] * state[n, i + 1, PAD - 2 : PAD - 2 + ny, :]
                result = result + coef[4, i] * z_up(v, 2) + coef[5, i] * z_down(v, 2)
                state[n + 1, i + 1, body, :] = result
                return c

            lax.fori_loop(0, nx, plane, 0)

    lane = lane_of((SUB, LANES))

    def write(i, c):
        dest, p = i // sz.planes, i % sz.planes
        result = state[COARSE_SWEEPS, i + 1, body, :] + end_ref[i]
        for g in range(sz.end_tiles):
            tile = None
            for q in range(sz.factor):
                n = g * sz.factor + q
                part = roll_lanes(result[n * SUB : (n + 1) * SUB], sz.own * q - sz.halo)
                tile = part if tile is None else jnp.where(lane < sz.own * q, tile, part)
            at = pl.multiple_of((p * sz.end_tiles + g) * SUB, SUB)
            out_ref[dest, pl.ds(at, SUB), :] = tile
        return c

    lax.fori_loop(0, nx, write, 0)
    for s in range(sz.space):
        out_ref[s, sz.end_rows : sz.end_rows + SUB, :] = square


def join_kernel(sz, kept_ref, come_ref, ends_ref, out_ref):
    for s in range(sz.space):
        out_ref[s, : sz.grad_rows, :] = kept_ref[0, s] + come_ref[0, s]
        out_ref[s, sz.grad_rows :, :] = ends_ref[s]


def unpack_kernel(sz, in_ref, ends_out, gx_out, gy_out, gz_out, norm_out):
    lane = lane_of((SUB, LANES))

    def whole_tile(tile, row, slot):
        result = None
        for q in range(sz.factor):
            block = tile * sz.factor + q
            part = roll_lanes(in_ref[block, row : row + SUB, :], sz.own * (q - slot))
            result = part if result is None else jnp.where(lane < sz.own * q, result, part)
        return result

    for t in range(sz.nz // LANES):
        columns = slice(t * LANES, (t + 1) * LANES)
        for p in range(sz.planes):
            for n in range(sz.grad_parts):
                f, r = divmod(n, sz.quarter // SUB)
                row = (p * sz.grad_tiles + n // sz.factor) * SUB
                (gx_out, gy_out, gz_out)[f][p, r * SUB : (r + 1) * SUB, columns] = whole_tile(t, row, n % sz.factor)
            for n in range(sz.end_parts):
                row = sz.grad_rows + (p * sz.end_tiles + n // sz.factor) * SUB
                ends_out[0, p, n * SUB : (n + 1) * SUB, columns] = whole_tile(t, row, n % sz.factor)
    squares = in_ref[0, sz.grad_rows + sz.end_rows :, :]
    for s in range(1, sz.space):
        squares = squares + in_ref[s, sz.grad_rows + sz.end_rows :, :]
    cells = (sz.spans - 1) * sz.nx * (sz.ny // 2) * (sz.nz // 2)
    whole = jnp.sum(jnp.sum(squares, axis=1, keepdims=True), axis=0, keepdims=True)
    norm_out[...] = jnp.sqrt(jnp.broadcast_to(whole, (SUB, LANES)) / cells)


def f32(*shape):
    return jax.ShapeDtypeStruct(shape, jnp.float32)


def call(kernel, sz, outs, scratch, *args, name):
    return pl.pallas_call(
        functools.partial(kernel, sz),
        out_shape=outs,
        scratch_shapes=[pltpu.VMEM(shape, jnp.float32) for shape in scratch],
        compiler_params=pltpu.CompilerParams(vmem_limit_bytes=VMEM_BYTES),
        name=name,
    )(*args)


def exchange(values, axis, bit):
    size = lax.axis_size(axis)
    return lax.ppermute(values, axis, [(i, i ^ bit) for i in range(size)])


def shards(start_states, diff_x, diff_y, diff_z, stress, trap_class, cotangent):
    spans, space = lax.axis_size("tm"), lax.axis_size("space")
    sz = Sizes(spans, space, *diff_x.shape)
    nx, ny = sz.nx, sz.ny
    part = f32(space, sz.planes * ny, LANES)
    coef, start, cot = call(
        windows_kernel,
        sz,
        (f32(space, 4 * sz.planes * sz.quarter, LANES), part, part),
        (),
        start_states,
        diff_x,
        diff_y,
        diff_z,
        stress,
        trap_class,
        cotangent,
        name="windows",
    )
    coef = lax.all_to_all(coef, "space", 0, 0)
    start = lax.all_to_all(start, "space", 0, 0)
    cot = lax.all_to_all(cot, "space", 0, 0)

    pieces = {0: coef}
    bit = spans // 2
    while bit:
        for key, piece in list(pieces.items()):
            pieces[key | bit] = exchange(piece, "tm", bit)
        bit //= 2
    pieces = [pieces[key] for key in range(spans)]

    rough = call(rough_kernel, sz, f32(nx, ny // 4, LANES), (), start, name="rough")
    following = lax.ppermute(rough, "tm", [(i + 1, i) for i in range(spans - 1)])

    padded = (nx + 2, ny + 2 * PAD, LANES)
    field = (nx, ny, LANES)
    end, rough_end, grads = call(
        fine_kernel,
        sz,
        (f32(*field), f32(nx, ny // 4, LANES), f32(spans, space, sz.grad_rows, LANES)),
        ((4,) + field, (8,) + field, (TOTAL + 1,) + padded, (2,) + padded)
        + (field, field, field, field, field, padded),
        *pieces,
        start,
        cot,
        name="fine",
    )

    jumps = jnp.where(lax.axis_index("tm") == spans - 1, 0.0, rough_end - following)
    jumps = lax.all_gather(jumps, "tm", axis=0)

    bit = spans // 2
    while bit:
        come = exchange(grads[bit:], "tm", bit)
        kept = grads[:bit]
        grads = kept + come if bit > 1 else None
        bit //= 2

    ends = call(
        coarse_kernel,
        sz,
        f32(space, sz.end_rows + SUB, LANES),
        ((4,) + field, (7,) + field, (COARSE_SWEEPS + 1,) + padded, field),
        *pieces,
        jumps,
        end,
        name="coarse",
    )
    joined = call(join_kernel, sz, f32(space, sz.out_rows, LANES), (), kept, come, ends, name="join")
    joined = lax.all_to_all(joined, "space", 0, 0)
    quarter = f32(sz.planes, sz.quarter, sz.nz)
    new_end, gx, gy, gz, norm = call(
        unpack_kernel,
        sz,
        (f32(1, sz.planes, ny, sz.nz), quarter, quarter, quarter, f32(SUB, LANES)),
        (),
        joined,
        name="unpack",
    )
    return new_end, gx, gy, gz, norm[0, 0]


def solution(mesh):
    fields = P("tm", "space", None, None)
    faces = P("space", None, None)
    quarter = P("space", "tm", None)
    return jax.shard_map(
        shards,
        mesh=mesh,
        in_specs=(fields, faces, faces, faces, faces, faces, fields),
        out_specs=(fields, quarter, quarter, quarter, P()),
        check_vma=False,
    )
```

time: 802 us -> 189 us (0.24); the launches traced: 791 us -> 188 us
  starting transfers between devices: 281 us -> 13.4 us
  local copies, waits for them, and re-layouts: 200 us -> 6.25 us
  other arithmetic: 187 us -> 0.06 us
  Pallas kernels: 0 us -> 87.9 us
  waiting for transfers between devices: 75.5 us -> 31.2 us
  blocking collectives: 27.3 us -> 48.8 us
  between operations: 16.7 us -> 0.72 us
    ppermute x80 -> x6, starting transfers between devices: 281 us -> 6.19 us  [the longest x5 4.91 us: exchange(): return lax.ppermute(values, axis, [(i, i ^ bit) for i in range(size)])]
    reshape x7 -> x0, local copies, waits for them, and re-layouts: 109 us -> none  [the longest x6 108 us: restrict(): values_in.reshape(values_in.shape[0], values_in.shape[1] // 2, 2, values_...]
    pallas_call x0 -> x6, Pallas kernels: none -> 87.9 us  [call(): pl.pallas_call(functools.partial(kernel, sz), out_shape=outs, scratch_sha...]
    add x62 -> x1, other arithmetic: 83.7 us -> 0.04 us  [shards(): grads = kept + come if bit > 1 else None]
    ppermute x80 -> x6, waiting for transfers between devices: 75.5 us -> 4.68 us  [the longest x5 2.54 us: exchange(): return lax.ppermute(values, axis, [(i, i ^ bit) for i in range(size)])]
    reduce_sum x8 -> x0, other arithmetic: 57.8 us -> none  [the longest x7 57.1 us: restrict(): return shaped.mean(axis=(2, 4))]
    slice x186 -> x3, local copies, waits for them, and re-layouts: 45.3 us -> 2.99 us  [the longest x2 1.8 us: shards(): come = exchange(grads[bit:], 'tm', bit)]
    all_to_all x0 -> x2, blocking collectives: none -> 41.4 us  [the longest x1 21.8 us: shards(): coef = lax.all_to_all(coef, 'space', 0, 0)]
  transfers between devices with their start and end apart: 83 -> 8, of which waited for: 60 -> 4; matrix products, arithmetic and copies ran while one was open for 48% -> 0% of each run, Pallas kernels for 0% -> 12%
where the time goes in v1:
time: 189 us; the launch traced here: 188 us
  Pallas kernels  87.9 us (47%)
  blocking collectives  48.8 us (26%)
  waiting for transfers between devices  31.2 us (17%)
  starting transfers between devices  13.4 us (7%)
  local copies, waits for them, and re-layouts  6.25 us (3%)
    pallas_call x6, Pallas kernels, call(): pl.pallas_call(functools.partial(kernel, sz), out_shape=outs, scratch_sha...  87.9 us
    all_to_all x1, blocking collectives, shards(): coef = lax.all_to_all(coef, 'space', 0, 0)  21.8 us
    all_to_all x1, blocking collectives, shards(): joined = lax.all_to_all(joined, 'space', 0, 0)  19.6 us
    all_to_all x1, waiting for transfers between devices, shards(): cot = lax.all_to_all(cot, 'space', 0, 0)  13.8 us
    all_to_all x1, waiting for transfers between devices, shards(): start = lax.all_to_all(start, 'space', 0, 0)  12.7 us
    all_gather x1, blocking collectives, shards(): jumps = lax.all_gather(jumps, 'tm', axis=0)  7.38 us
    ppermute x5, starting transfers between devices, exchange(): return lax.ppermute(values, axis, [(i, i ^ bit) for i in range(size)])  4.91 us
  transfers between devices with their start and end apart: 8, of which 4 were waited for; matrix products, arithmetic and copies ran while one was open for 0% of the time, Pallas kernels for 12%

profile of v1, /device:TPU:0, one launch (start us, length us, event | category | flops | bytes accessed | tf_op | source)
XLA Modules:
  0.0 188.3 jit_solution(9438618405955184673)
XLA Ops:
  0.6 2.9 %windows.1 = (f32[8,128,128]{2,1,0:T(8,128)}, f32[8,128,128]{2,1,0:T(8,128)}, f32[8,128,128]{2,1,0:T(8,128)}) custom-call(f32[1,2,64,512]{3,2,1,0:T(8,128)} %start_ref.1, f32[2,64,512]{2,1,0:T(8,128)} %fx_ref.1, f32[2,64,512]{2,1,0:T(8,128)} %fy_ref.1, f32[2,64,512]{2,1,0:T(8,128)} %fz_ref.1, f32[2,64,512]{2,1,0:T(8,128)} %stress_ref.1, ...), custom_call_target="tpu_custom_call" | custom-call | tf_op jit(solution)/shard_map/windows/pallas_call | solution.py:490
  3.6 21.8 %all_to_all.20.refs_0_ = f32[8,128,128]{2,1,0:T(8,128)S(1)} all-to-all(f32[8,128,128]{2,1,0:T(8,128)} %get-tuple-element.16), channel_id=1, replica_groups=mesh['tm'=4,'space'=8] {'space'}, dimensions={0} | all-to-all | bytes 1048576 | tf_op jit(solution)/shard_map/all_to_all | solution.py:523
  25.4 3.6 %all-to-all-start.1 = ((f32[8,128,128]{2,1,0:T(8,128)}), f32[8,128,128]{2,1,0:T(8,128)S(1)}, u32[]{:S(2)}, u32[]{:S(2)}) async-start(f32[8,128,128]{2,1,0:T(8,128)} %get-tuple-element.17), calls=%async_computation.1 | async-start | bytes 1048576 | tf_op jit(solution)/shard_map/all_to_all | solution.py:524
  29.0 1.5 collective-permute-start.1
  30.5 12.7 %all-to-all-done.1.refs_4_.start_ref = f32[8,128,128]{2,1,0:T(8,128)S(1)} async-done(((f32[8,128,128]{2,1,0:T(8,128)}), f32[8,128,128]{2,1,0:T(8,128)S(1)}, u32[]{:S(2)}, u32[]{:S(2)}) %all-to-all-start.1) | async-done | bytes 524320 | tf_op jit(solution)/shard_map/all_to_all | solution.py:524
  43.2 0.8 copy-done
  44.0 3.6 %all-to-all-start.2 = ((f32[8,128,128]{2,1,0:T(8,128)}), f32[8,128,128]{2,1,0:T(8,128)S(1)}, u32[]{:S(2)}, u32[]{:S(2)}) async-start(f32[8,128,128]{2,1,0:T(8,128)} %get-tuple-element.18), calls=%async_computation.2 | async-start | bytes 1048576 | tf_op jit(solution)/shard_map/all_to_all | solution.py:525
  48.2 13.8 %all-to-all-done.2.refs_5_ = f32[8,128,128]{2,1,0:T(8,128)S(1)} async-done(((f32[8,128,128]{2,1,0:T(8,128)}), f32[8,128,128]{2,1,0:T(8,128)S(1)}, u32[]{:S(2)}, u32[]{:S(2)}) %all-to-all-start.2) | async-done | bytes 524320 | tf_op jit(solution)/shard_map/all_to_all | solution.py:525
  62.1 0.8 copy-done.2
  63.0 0.8 copy-done.5
  63.8 58.6 %fine.1 = (f32[16,64,128]{2,1,0:T(8,128)}, f32[16,16,128]{2,1,0:T(8,128)}, f32[4,8,48,128]{3,2,1,0:T(8,128)}) custom-call(f32[8,128,128]{2,1,0:T(8,128)} %copy-done.1, f32[8,128,128]{2,1,0:T(8,128)} %copy-done.4, f32[8,128,128]{2,1,0:T(8,128)} %copy-done.3, f32[8,128,128]{2,1,0:T(8,128)} %copy-done.5, f32[8,128,128]{2,1,0:T(8,128)} %copy-done, ...), custom_call_target="tpu_custom_call" | custom-call | tf_op jit(solution)/shard_map/fine/pallas_call | solution.py:490
  122.4 1.1 slice.16
  123.5 1.6 collective-permute-start.3
  125.1 2.0 %rough.1 = f32[16,16,128]{2,1,0:T(8,128)} custom-call(f32[8,128,128]{2,1,0:T(8,128)} %copy-done), custom_call_target="tpu_custom_call" | custom-call | tf_op jit(solution)/shard_map/rough/pallas_call | solution.py:490
  127.1 1.3 collective-permute-start.5
  128.4 2.1 %collective-permute-done.5 = f32[16,16,128]{2,1,0:T(8,128)S(1)} collective-permute-done((f32[16,16,128]{2,1,0:T(8,128)}, f32[16,16,128]{2,1,0:T(8,128)S(1)}, u32[]{:S(2)}, u32[]{:S(2)}) %collective-permute-start.5) | collective-permute-done | bytes 131104 | tf_op jit(solution)/shard_map/ppermute | solution.py:536
  130.6 2.5 %collective-permute-done.3 = f32[2,8,48,128]{3,2,1,0:T(8,128)S(1)} collective-permute-done((f32[2,8,48,128]{3,2,1,0:T(8,128)S(1)}, f32[2,8,48,128]{3,2,1,0:T(8,128)S(1)}, u32[]{:S(2)}, u32[]{:S(2)}) %collective-permute-start.3) | collective-permute-done | bytes 393248 | tf_op jit(solution)/shard_map/ppermute | solution.py:501
  133.9 1.3 collective-permute-start.4
  135.1 7.4 %all-gather = f32[64,16,128]{2,1,0:T(8,128)} all-gather(f32[16,16,128]{2,1,0:T(8,128)S(1)} %subtract_select_fusion), channel_id=2, replica_groups=mesh['tm'=4,'space'=8] {'tm'}, dimensions={0}, use_global_device_ids=true | all-gather | bytes 655360 | tf_op jit(solution)/shard_map/all_gather | solution.py:553
  142.5 20.4 %coarse.1.ends_ref = f32[8,72,128]{2,1,0:T(8,128)} custom-call(f32[8,128,128]{2,1,0:T(8,128)} %copy-done.1, f32[8,128,128]{2,1,0:T(8,128)} %copy-done.4, f32[8,128,128]{2,1,0:T(8,128)} %copy-done.3, f32[8,128,128]{2,1,0:T(8,128)} %copy-done.5, f32[4,16,16,128]{3,2,1,0:T(8,128)} %bitcast.2, f32[16,64,128]{2,1,0:T(8,128)} %get-tuple-element.21.refs_5_), custom_call_target="tpu_custom_call" | custom-call | tf_op jit(solution)/shard_map/coarse/pallas_call | solution.py:490
  163.6 2.0 %join.1 = f32[8,120,128]{2,1,0:T(8,128)} custom-call(f32[1,8,48,128]{3,2,1,0:T(8,128)} %get-tuple-element.28.kept_ref, f32[1,8,48,128]{3,2,1,0:T(8,128)} %copy-done.7, f32[8,72,128]{2,1,0:T(8,128)} %coarse.1.ends_ref), custom_call_target="tpu_custom_call" | custom-call | tf_op jit(solution)/shard_map/join/pallas_call | solution.py:490
  165.6 19.6 %all_to_all.21.in_ref = f32[8,120,128]{2,1,0:T(8,128)} all-to-all(f32[8,120,128]{2,1,0:T(8,128)} %join.1), channel_id=1, replica_groups=mesh['tm'=4,'space'=8] {'space'}, dimensions={0} | all-to-all | bytes 983040 | tf_op jit(solution)/shard_map/all_to_all | solution.py:573
  185.1 2.0 %unpack.1 = (f32[1,2,64,512]{3,2,1,0:T(8,128)}, f32[2,16,512]{2,1,0:T(8,128)}, f32[2,16,512]{2,1,0:T(8,128)}, f32[2,16,512]{2,1,0:T(8,128)}, f32[8,128]{1,0:T(8,128)}) custom-call(f32[8,120,128]{2,1,0:T(8,128)} %all_to_all.21.in_ref), custom_call_target="tpu_custom_call" | custom-call | tf_op jit(solution)/shard_map/unpack/pallas_call | solution.py:490
  187.1 1.2 slice.19
  (24 shorter events, 2.2 us)
Async XLA Ops:
  25.4 22.2 %copy-start.1 = (f32[8,128,128]{2,1,0:T(8,128)}, f32[8,128,128]{2,1,0:T(8,128)S(1)}, u32[]{:S(2)}) copy-start(f32[8,128,128]{2,1,0:T(8,128)S(1)} %all_to_all.20.refs_0_) | copy-start | bytes 1572868
  25.4 17.8 %all-to-all-start.1 = ((f32[8,128,128]{2,1,0:T(8,128)}), f32[8,128,128]{2,1,0:T(8,128)S(1)}, u32[]{:S(2)}, u32[]{:S(2)}) async-start(f32[8,128,128]{2,1,0:T(8,128)} %get-tuple-element.17), calls=%async_computation.1 | async-start | bytes 1048576 | tf_op jit(solution)/shard_map/all_to_all | solution.py:524
  29.0 18.7 %collective-permute-start.1 = (f32[8,128,128]{2,1,0:T(8,128)S(1)}, f32[8,128,128]{2,1,0:T(8,128)S(1)}, u32[]{:S(2)}, u32[]{:S(2)}) collective-permute-start(f32[8,128,128]{2,1,0:T(8,128)S(1)} %all_to_all.20.refs_0_), channel_id=1, source_target_pairs={{0,16},{8,24},{16,0},{24,8},{1,17},{9,25},{17,1},{25,9},{2,18},{10... | collective-permute-start | bytes 1572872 | tf_op jit(solution)/shard_map/ppermute | solution.py:501
  43.2 0.8 copy-start
  44.0 18.1 %all-to-all-start.2 = ((f32[8,128,128]{2,1,0:T(8,128)}), f32[8,128,128]{2,1,0:T(8,128)S(1)}, u32[]{:S(2)}, u32[]{:S(2)}) async-start(f32[8,128,128]{2,1,0:T(8,128)} %get-tuple-element.18), calls=%async_computation.2 | async-start | bytes 1048576 | tf_op jit(solution)/shard_map/all_to_all | solution.py:525
  47.6 14.4 %collective-permute-start = (f32[8,128,128]{2,1,0:T(8,128)S(1)}, f32[8,128,128]{2,1,0:T(8,128)S(1)}, u32[]{:S(2)}, u32[]{:S(2)}) collective-permute-start(f32[8,128,128]{2,1,0:T(8,128)S(1)} %all_to_all.20.refs_0_), channel_id=1, source_target_pairs={{0,8},{8,0},{16,24},{24,16},{1,9},{9,1},{17,25},{25,17},{2,10},{10... | collective-permute-start | bytes 1572872 | tf_op jit(solution)/shard_map/ppermute | solution.py:501
  47.7 14.4 %copy-start.3 = (f32[8,128,128]{2,1,0:T(8,128)}, f32[8,128,128]{2,1,0:T(8,128)S(1)}, u32[]{:S(2)}) copy-start(f32[8,128,128]{2,1,0:T(8,128)S(1)} %collective-permute-done.1.refs_2_) | copy-start | bytes 1572868
  47.7 14.3 %collective-permute-start.2 = (f32[8,128,128]{2,1,0:T(8,128)S(1)}, f32[8,128,128]{2,1,0:T(8,128)S(1)}, u32[]{:S(2)}, u32[]{:S(2)}) collective-permute-start(f32[8,128,128]{2,1,0:T(8,128)S(1)} %collective-permute-done.1.refs_2_), channel_id=1, source_target_pairs={{0,8},{8,0},{16,24},{24,16},{1,9},{9,1},{17,25},{25,17},{2,10},{10... | collective-permute-start | bytes 1572872 | tf_op jit(solution)/shard_map/ppermute | solution.py:501
  62.0 0.8 copy-start.2
  62.0 1.0 copy-start.4
  63.0 0.8 copy-start.5
  122.4 10.7 %copy-start.6 = (f32[4,8,48,128]{3,2,1,0:T(8,128)S(1)}, f32[4,8,48,128]{3,2,1,0:T(8,128)}, u32[]{:S(2)}) copy-start(f32[4,8,48,128]{3,2,1,0:T(8,128)} %get-tuple-element.19) | copy-start | bytes 2359300
  123.5 7.1 %copy-start.8 = (f32[16,16,128]{2,1,0:T(8,128)S(1)}, f32[16,16,128]{2,1,0:T(8,128)}, u32[]{:S(2)}) copy-start(f32[16,16,128]{2,1,0:T(8,128)} %get-tuple-element.20) | copy-start | bytes 393220
  123.5 9.6 %collective-permute-start.3 = (f32[2,8,48,128]{3,2,1,0:T(8,128)S(1)}, f32[2,8,48,128]{3,2,1,0:T(8,128)S(1)}, u32[]{:S(2)}, u32[]{:S(2)}) collective-permute-start(f32[2,8,48,128]{3,2,1,0:T(8,128)S(1)} %slice.16), channel_id=1, source_target_pairs={{0,16},{8,24},{16,0},{24,8},{1,17},{9,25},{17,1},{25,9},{2,18},{10... | collective-permute-start | bytes 1179656 | tf_op jit(solution)/shard_map/ppermute | solution.py:501
  127.1 3.4 %collective-permute-start.5 = (f32[16,16,128]{2,1,0:T(8,128)}, f32[16,16,128]{2,1,0:T(8,128)S(1)}, u32[]{:S(2)}, u32[]{:S(2)}) collective-permute-start(f32[16,16,128]{2,1,0:T(8,128)} %rough.1), channel_id=1, source_target_pairs={{8,0},{16,8},{24,16},{9,1},{17,9},{25,17},{10,2},{18,10},{26,18},{... | collective-permute-start | bytes 393224 | tf_op jit(solution)/shard_map/ppermute | solution.py:536
  133.9 29.0 %collective-permute-start.4 = (f32[1,8,48,128]{3,2,1,0:T(8,128)S(1)}, f32[1,8,48,128]{3,2,1,0:T(8,128)S(1)}, u32[]{:S(2)}, u32[]{:S(2)}) collective-permute-start(f32[1,8,48,128]{3,2,1,0:T(8,128)S(1)} %get-tuple-element.27), channel_id=1, source_target_pairs={{0,8},{8,0},{16,24},{24,16},{1,9},{9,1},{17,25},{25,17},{2,10},{10... | collective-permute-start | bytes 589832 | tf_op jit(solution)/shard_map/ppermute | solution.py:501
  162.9 0.7 copy-start.7

commit v2 on v1

v2 whole, which is shorter than its diff:
```python
import functools
import math

import jax
import jax.numpy as jnp
from jax import lax
from jax.experimental import pallas as pl
from jax.experimental.pallas import tpu as pltpu
from jax.sharding import PartitionSpec as P

FINE_STEPS = 2
SWEEPS = 8
COARSE_SWEEPS = 2
TOTAL = FINE_STEPS * SWEEPS
LANES = 128
SUB = 8

STRESS_COUPLING = 0.5
TIME_STEP = 1.0
COARSE_STEP = FINE_STEPS * TIME_STEP
TRAP_LEVELS = (0.0, 1.0, 3.0, 7.0)

SPARE_BYTES = 2 * 1024 * 1024


class Sizes:
    def __init__(self, spans, space, planes, ny, nz):
        self.spans = spans
        self.space = space
        self.planes = planes
        self.nx = planes * space
        self.ny = ny
        self.nz = nz
        self.own = nz // space
        self.halo = (LANES - self.own) // 2
        self.quarter = ny // spans
        self.share = self.quarter // SUB
        self.tiles = ny // SUB
        self.factor = LANES // self.own
        self.grad_parts = 3 * self.share
        self.grad_tiles = -(-self.grad_parts // self.factor)
        self.end_parts = self.tiles
        self.end_tiles = self.end_parts // self.factor
        self.grad_rows = planes * self.grad_tiles * SUB
        self.end_rows = planes * self.end_tiles * SUB
        self.out_rows = self.grad_rows + self.end_rows + SUB
        assert self.tiles == SUB
        assert TOTAL + 2 * COARSE_SWEEPS * (spans - 1) <= self.halo


def lane_of(shape):
    return lax.broadcasted_iota(jnp.int32, shape, len(shape) - 1)


def row_of(shape):
    return lax.broadcasted_iota(jnp.int32, shape, len(shape) - 2)


def z_up(v, by=1):
    return pltpu.roll(v, LANES - by, v.ndim - 1)


def z_down(v, by=1):
    return pltpu.roll(v, by, v.ndim - 1)


def roll_lanes(v, by):
    by = by % LANES
    return v if by == 0 else pltpu.roll(v, by, 1)


def windows_kernel(sz, *refs):
    coef_out, field_out, columns = refs[7:10]
    start_ref, fx_ref, fy_ref, fz_ref, stress_ref, trap_ref, cot_ref = refs[10:17]
    copies = [pltpu.make_async_copy(refs[n], refs[10 + n], refs[17].at[n]) for n in range(7)]
    for n in (1, 2, 3, 4, 5, 0, 6):
        copies[n].start()
    for n in (1, 2, 3, 4, 5):
        copies[n].wait()
    turn = lax.axis_index("tm")
    count = sz.nz // LANES
    lane = lane_of((SUB, LANES))
    zero = jnp.zeros((SUB, LANES), jnp.float32)

    def cut(parts, out_ref, rows):
        for j in range(sz.space):
            first = sz.own * j - sz.halo
            tile, shift = first // LANES, first % LANES
            low = parts[tile] if 0 <= tile < count else zero
            if shift:
                high = parts[tile + 1] if tile + 1 < count else zero
                low = roll_lanes(jnp.where(lane < shift, high, low), -shift)
            out_ref[j, rows, :] = low

    for p in range(sz.planes):
        for n in range(count):
            cells = slice(n * LANES, (n + 1) * LANES)
            for f, ref in enumerate((fx_ref, fy_ref, fz_ref)):
                columns[f, p, n] = ref[p, :, cells]
            trap = trap_ref[p, :, cells]
            level = jnp.zeros(trap.shape, jnp.float32)
            for position, value in enumerate(TRAP_LEVELS):
                level = level + jnp.where(trap == position, value, 0.0)
            columns[3, p, n] = (1.0 + level) * jnp.exp(STRESS_COUPLING * stress_ref[p, :, cells])
        for f in range(4):
            for a in range(sz.share):
                rows = pl.ds(turn * sz.share + a, SUB, stride=sz.tiles)
                row = ((f * sz.planes + p) * sz.share + a) * SUB
                cut([columns[f, p, n, rows, :] for n in range(count)], coef_out, slice(row, row + SUB))
    for f, ref in enumerate((start_ref, cot_ref)):
        copies[6 * f].wait()
        for p in range(sz.planes):
            for r in range(SUB):
                parts = [
                    ref[0, p, r * sz.tiles : (r + 1) * sz.tiles, n * LANES : (n + 1) * LANES] for n in range(count)
                ]
                cut(parts, field_out, pl.ds((f * sz.planes + p) * sz.ny + r, sz.tiles, stride=SUB))


def valid_columns(sz):
    column = lax.axis_index("space") * sz.own - sz.halo + lane_of((SUB, LANES))
    return (column >= 0) & (column < sz.nz)


def lay_out_faces(sz, pieces, faces):
    turn = lax.axis_index("tm")
    for key, piece in enumerate(pieces):
        for f in range(4):
            for p in range(sz.planes):
                for a in range(sz.share):
                    row = ((f * sz.planes + p) * sz.share + a) * SUB
                    for s in range(sz.space):
                        faces[f, s * sz.planes + p, (turn ^ key) * sz.share + a] = piece[s, row : row + SUB, :]


def next_sublane(v):
    return jnp.where(row_of(v.shape) == SUB - 1, 0.0, pltpu.roll(v, SUB - 1, v.ndim - 2))


def last_sublane(v):
    return jnp.where(row_of(v.shape) == 0, 0.0, pltpu.roll(v, 1, v.ndim - 2))


def normalise(sz, faces, coef, count, step, apart):
    valid = valid_columns(sz)

    def one(i):
        for t in range(count):
            fx, fy, fz, cap = (faces[f, i, t] for f in range(4))
            bx = jnp.where(i == 0, 0.0, faces[0, jnp.maximum(i - 1, 0), t])
            by = faces[1, i, t - 1] if t else last_sublane(faces[1, i, count - 1])
            bz = z_down(fz, apart)
            diagonal = cap + step * (fx + bx + fy + by + fz + bz)
            inv = jnp.where(valid, 1.0 / diagonal, 0.0)
            scaled = step * inv
            for n, face in enumerate((fx, bx, fy, by, fz, bz)):
                coef[n, i, t] = face * scaled
            faces[2, i, t] = cap * inv
            faces[3, i, t] = inv

    def some(g, c):
        for q in range(4):
            one(4 * g + q)
        return c

    lax.fori_loop(0, sz.nx // 4, some, 0)


def store_plane(ref, at, v, count):
    ref[at, 0] = last_sublane(v[count - 1])
    ref[at, 1 : count + 1] = v
    ref[at, count + 1] = next_sublane(v[0])


def sweep(sz, coef, now, later, count, apart, source=None, kept=None):
    for i in range(sz.nx):
        v = now[i, 1 : count + 1]
        result = coef[2, i] * now[i, 2 : count + 2] + coef[3, i] * now[i, 0:count]
        result = result + coef[4, i] * z_up(v, apart) + coef[5, i] * z_down(v, apart)
        if i + 1 < sz.nx:
            result = result + coef[0, i] * now[i + 1, 1 : count + 1]
        if i:
            result = result + coef[1, i] * now[i - 1, 1 : count + 1]
        if source is not None:
            result = result + source[i]
        store_plane(later, i, result, count)
        if kept is not None:
            keep_plane(kept[0], kept[1], i, result, count)


def keep_plane(ref, k, i, v, count):
    ref[k, i, 0:count] = v
    ref[k, i, count] = next_sublane(v[0])


def coarse_rows(tile_of, m):
    v = tile_of(2 * m) + tile_of(2 * m + 1)
    return 0.25 * (v + jnp.where(lane_of(v.shape) % 2 == 0, z_up(v), z_down(v)))


def packed(low, high):
    return jnp.where(lane_of(low.shape) % 2 == 0, low, high)


def unpacked(v):
    even = lane_of(v.shape) % 2 == 0
    return jnp.where(even, v, z_down(v)), jnp.where(even, z_up(v), v)


def pack_rough(sz, tile_of):
    return [packed(coarse_rows(tile_of, 2 * m), coarse_rows(tile_of, 2 * m + 1)) for m in range(sz.tiles // 4)]


def fine_kernel(sz, *refs):
    pieces = refs[: sz.spans]
    field_ref, end_out, rough_out, grads_out = refs[sz.spans : sz.spans + 4]
    faces, coef, even, odd, source, fields, weights = refs[sz.spans + 4 :]
    nx, count = sz.nx, sz.tiles
    body = slice(1, count + 1)
    turn = lax.axis_index("tm")

    lay_out_faces(sz, pieces, faces)
    normalise(sz, faces, coef, count, TIME_STEP, 1)

    rim = jnp.zeros((count + 1, SUB, LANES), jnp.float32)
    for k in range(TOTAL + 1):
        fields[k, nx] = rim
        if k:
            weights[k - 1, nx] = rim

    def whole_plane(f, i):
        s, p = divmod(i, sz.planes)
        row = (f * sz.planes + p) * sz.ny
        return field_ref[s, row : row + sz.ny, :].reshape(count, SUB, LANES)

    for i in range(nx):
        v = whole_plane(0, i)
        store_plane(even, i, v, count)
        keep_plane(fields, 0, i, v, count)
    for step in range(FINE_STEPS):
        base = step * SWEEPS
        for i in range(nx):
            source[i] = faces[2, i] * even[i, body]

        def two(n, c):
            k = base + 2 * n
            sweep(sz, coef, even, odd, count, 1, source, (fields, k + 1))
            sweep(sz, coef, odd, even, count, 1, source, (fields, k + 2))
            return c

        lax.fori_loop(0, SWEEPS // 2, two, 0)

    for i in range(nx):
        end_out[i] = even[i, body]
        for m, rough in enumerate(pack_rough(sz, lambda t: even[i, 1 + t])):
            rough_out[i, m] = rough

    for i in range(nx):
        v = faces[3, i] * whole_plane(1, i)
        store_plane(even, i, v, count)
        keep_plane(weights, TOTAL - 1, i, v, count)
    for step in reversed(range(FINE_STEPS)):
        base = step * SWEEPS

        def two_back(n, c):
            k = base + SWEEPS - 1 - 2 * n
            sweep(sz, coef, even, odd, count, 1, None, (weights, k - 1))
            sweep(sz, coef, odd, even, count, 1, None, (weights, k - 2))
            return c

        lax.fori_loop(0, SWEEPS // 2 - 1, two_back, 0)
        sweep(sz, coef, even, odd, count, 1, None, (weights, base))
        if step:
            sweep(sz, coef, odd, even, count, 1, None)
            for i in range(nx):
                total = weights[base, i, 0:count]
                for k in range(base + 1, base + SWEEPS):
                    total = total + weights[k, i, 0:count]
                v = even[i, body] + faces[2, i] * total
                store_plane(odd, i, v, count)
                keep_plane(weights, base - 1, i, v, count)
            for i in range(nx):
                even[i] = odd[i]

    def gather_sums(i, c):
        for t in range(count):
            along = [None, None, None]
            whole = None
            for k in range(TOTAL):
                w, u = weights[k, i, t], fields[k, i, t]
                for d, (up_w, up_u) in enumerate(
                    (
                        (weights[k, i + 1, t], fields[k, i + 1, t]),
                        (weights[k, i, t + 1], fields[k, i, t + 1]),
                        (z_up(w), z_up(u)),
                    )
                ):
                    term = w * up_u + up_w * u
                    along[d] = term if along[d] is None else along[d] + term
                term = w * fields[k + 1, i, t]
                whole = term if whole is None else whole + term
            for d in range(3):
                faces[d, i, t] = along[d]
            even[i, t] = whole
            if t == 0:
                even[i, count] = next_sublane(whole)
        return c

    lax.fori_loop(0, nx, gather_sums, 0)
    rows = weights.reshape(TOTAL, nx + 1, (count + 1) * SUB, LANES)

    for i in range(nx):
        for t in range(count):
            here = even[i, t]
            for d, there in enumerate((even[i + 1, t] if i + 1 < nx else None, even[i, t + 1], z_up(here))):
                value = faces[d, i, t] - here
                if there is not None:
                    value = value - there
                rows[d, i, pl.ds(t, SUB, stride=count), :] = TIME_STEP * value

    lane = lane_of((SUB, LANES))
    for key in range(sz.spans):
        first = (turn ^ key) * sz.quarter
        for i in range(nx):
            dest, p = divmod(i, sz.planes)
            for g in range(sz.grad_tiles):
                tile = None
                for q in range(sz.factor):
                    n = g * sz.factor + q
                    if n >= sz.grad_parts:
                        continue
                    f, r = divmod(n, sz.share)
                    at = pl.ds(pl.multiple_of(first + r * SUB, SUB), SUB)
                    part = roll_lanes(rows[f, i, at, :], sz.own * q - sz.halo)
                    tile = part if tile is None else jnp.where(lane < sz.own * q, tile, part)
                row = (p * sz.grad_tiles + g) * SUB
                grads_out[key, dest, row : row + SUB, :] = tile


def rough_kernel(sz, start_ref, out_ref):
    for i in range(sz.nx):
        s, p = divmod(i, sz.planes)
        tile_of = lambda t: start_ref[s, (p * sz.tiles + t) * SUB : (p * sz.tiles + t + 1) * SUB, :]
        for m, rough in enumerate(pack_rough(sz, tile_of)):
            out_ref[i, m] = rough


def coarse_kernel(sz, *refs):
    pieces = refs[: sz.spans]
    jumps_ref, end_ref, out_ref = refs[sz.spans : sz.spans + 3]
    faces, rough, coef, even, odd, source = refs[sz.spans + 3 :]
    nx, count = sz.nx, sz.tiles // 2
    body = slice(1, count + 1)
    turn = lax.axis_index("tm")
    lay_out_faces(sz, pieces, faces)
    for i in range(nx):
        for f, scale in enumerate((1.0, 0.25, 0.25, 1.0)):
            for m in range(count):
                v = coarse_rows(lambda t: faces[f, i, t], m)
                rough[f, i, m] = v if scale == 1.0 else scale * v
    normalise(sz, rough, coef, count, COARSE_STEP, 2)

    lane = lane_of((SUB, LANES))
    mine = (lane >= sz.halo) & (lane < sz.halo + sz.own)
    square = jnp.zeros((SUB, LANES), jnp.float32)
    for k in range(sz.spans - 1):
        for i in range(nx):
            for m in range(count // 2):
                square = square + jumps_ref[k, i, m] * jumps_ref[k, i, m]
    square = jnp.where(mine, square, 0.0)

    for d in reversed(range(1, sz.spans)):
        which = jnp.maximum(turn - d, 0)
        there = turn >= d
        for i in range(nx):
            jump = []
            for m in range(count // 2):
                jump += unpacked(jnp.where(there, jumps_ref[which, i, m], 0.0))
            v = jnp.stack(jump)
            if d < sz.spans - 1:
                v = v + even[i, body]
            store_plane(even, i, v, count)
            source[i] = rough[2, i] * v
        for n in range(COARSE_SWEEPS // 2):
            sweep(sz, coef, even, odd, count, 2, source)
            sweep(sz, coef, odd, even, count, 2, source)

    for i in range(nx):
        dest, p = divmod(i, sz.planes)
        for g in range(sz.end_tiles):
            tile = None
            for q in range(sz.factor):
                n = g * sz.factor + q
                part = roll_lanes(end_ref[i, n] + even[i, 1 + n // 2], sz.own * q - sz.halo)
                tile = part if tile is None else jnp.where(lane < sz.own * q, tile, part)
            row = (p * sz.end_tiles + g) * SUB
            out_ref[dest, row : row + SUB, :] = tile
    for s in range(sz.space):
        out_ref[s, sz.end_rows : sz.end_rows + SUB, :] = square


def join_kernel(sz, kept_ref, come_ref, ends_ref, out_ref):
    for s in range(sz.space):
        out_ref[s, : sz.grad_rows, :] = kept_ref[0, s] + come_ref[0, s]
        out_ref[s, sz.grad_rows :, :] = ends_ref[s]


def unpack_kernel(sz, in_ref, ends_out, gx_out, gy_out, gz_out, norm_out, rows):
    lane = lane_of((SUB, LANES))

    def whole_tile(tile, row, slot):
        result = None
        for q in range(sz.factor):
            block = tile * sz.factor + q
            part = roll_lanes(in_ref[block, row : row + SUB, :], sz.own * (q - slot))
            result = part if result is None else jnp.where(lane < sz.own * q, result, part)
        return result

    for t in range(sz.nz // LANES):
        columns = slice(t * LANES, (t + 1) * LANES)
        for p in range(sz.planes):
            for n in range(sz.grad_parts):
                f, r = divmod(n, sz.share)
                row = (p * sz.grad_tiles + n // sz.factor) * SUB
                (gx_out, gy_out, gz_out)[f][p, r * SUB : (r + 1) * SUB, columns] = whole_tile(t, row, n % sz.factor)
            for n in range(sz.end_parts):
                row = sz.grad_rows + (p * sz.end_tiles + n // sz.factor) * SUB
                rows[t, p, pl.ds(n, SUB, stride=sz.tiles), :] = whole_tile(t, row, n % sz.factor)
            ends_out[0, p, :, columns] = rows[t, p]
    squares = in_ref[0, sz.grad_rows + sz.end_rows :, :]
    for s in range(1, sz.space):
        squares = squares + in_ref[s, sz.grad_rows + sz.end_rows :, :]
    cells = (sz.spans - 1) * sz.nx * (sz.ny // 2) * (sz.nz // 2)
    whole = jnp.sum(jnp.sum(squares, axis=1, keepdims=True), axis=0, keepdims=True)
    norm_out[...] = jnp.sqrt(jnp.broadcast_to(whole, (SUB, LANES)) / cells)


def f32(*shape):
    return jax.ShapeDtypeStruct(shape, jnp.float32)


def call(kernel, sz, outs, scratch, *args, name):
    held = sum(4 * math.prod(shape) for shape in scratch)
    held += sum(4 * math.prod(array.shape) for array in jax.tree.leaves((outs, args)))
    return pl.pallas_call(
        functools.partial(kernel, sz),
        out_shape=outs,
        scratch_shapes=[pltpu.VMEM(shape, jnp.float32) for shape in scratch],
        compiler_params=pltpu.CompilerParams(vmem_limit_bytes=held + SPARE_BYTES),
        name=name,
    )(*args)


def exchange(values, axis, bit):
    size = lax.axis_size(axis)
    return lax.ppermute(values, axis, [(i, i ^ bit) for i in range(size)])


def shards(start_states, diff_x, diff_y, diff_z, stress, trap_class, cotangent):
    spans, space = lax.axis_size("tm"), lax.axis_size("space")
    sz = Sizes(spans, space, *diff_x.shape)
    nx, ny = sz.nx, sz.ny
    inputs = (start_states, diff_x, diff_y, diff_z, stress, trap_class, cotangent)
    coef, both = pl.pallas_call(
        functools.partial(windows_kernel, sz),
        out_shape=(f32(space, 4 * sz.planes * sz.quarter, LANES), f32(space, 2 * sz.planes * ny, LANES)),
        in_specs=[pl.BlockSpec(memory_space=pltpu.HBM)] * len(inputs),
        scratch_shapes=[pltpu.VMEM((4, sz.planes, sz.nz // LANES, ny, LANES), jnp.float32)]
        + [pltpu.VMEM(array.shape, array.dtype) for array in inputs]
        + [pltpu.SemaphoreType.DMA((len(inputs),))],
        compiler_params=pltpu.CompilerParams(vmem_limit_bytes=60 * 1024 * 1024),
        name="windows",
    )(*inputs)
    coef = lax.all_to_all(coef, "space", 0, 0)
    both = lax.all_to_all(both, "space", 0, 0)

    pieces = {0: coef}
    bit = spans // 2
    while bit:
        for key, piece in list(pieces.items()):
            pieces[key | bit] = exchange(piece, "tm", bit)
        bit //= 2
    pieces = [pieces[key] for key in range(spans)]

    tiles = sz.tiles
    rough_shape = f32(nx, tiles // 4, SUB, LANES)
    rough = call(rough_kernel, sz, rough_shape, (), both, name="rough")
    following = lax.ppermute(rough, "tm", [(i + 1, i) for i in range(spans - 1)])

    def field(count, *front):
        return front + (count, SUB, LANES)

    both, rough = lax.optimization_barrier((both, rough))
    end, rough_end, grads = call(
        fine_kernel,
        sz,
        (f32(*field(tiles, nx)), rough_shape, f32(spans, space, sz.grad_rows, LANES)),
        (
            field(tiles, 4, nx),
            field(tiles, 6, nx),
            field(tiles + 2, nx),
            field(tiles + 2, nx),
            field(tiles, nx),
            field(tiles + 1, TOTAL + 1, nx + 1),
            field(tiles + 1, TOTAL, nx + 1),
        ),
        *pieces,
        both,
        name="fine",
    )
    jumps = jnp.where(lax.axis_index("tm") == spans - 1, 0.0, rough_end - following)
    jumps = lax.all_gather(jumps, "tm", axis=0)

    bit = spans // 2
    while bit:
        come = exchange(grads[bit:], "tm", bit)
        kept = grads[:bit]
        if bit == spans // 2:
            come, jumps = lax.optimization_barrier((come, jumps))
        grads = kept + come if bit > 1 else None
        bit //= 2

    ends = call(
        coarse_kernel,
        sz,
        f32(space, sz.end_rows + SUB, LANES),
        (
            field(tiles, 4, nx),
            field(tiles // 2, 4, nx),
            field(tiles // 2, 6, nx),
            field(tiles // 2 + 2, nx),
            field(tiles // 2 + 2, nx),
            field(tiles // 2, nx),
        ),
        *pieces,
        jumps,
        end,
        name="coarse",
    )
    joined = call(join_kernel, sz, f32(space, sz.out_rows, LANES), (), kept, come, ends, name="join")
    joined = lax.all_to_all(joined, "space", 0, 0)
    quarter = f32(sz.planes, sz.quarter, sz.nz)
    new_end, gx, gy, gz, norm = call(
        unpack_kernel,
        sz,
        (f32(1, sz.planes, ny, sz.nz), quarter, quarter, quarter, f32(SUB, LANES)),
        ((sz.nz // LANES, sz.planes, ny, LANES),),
        joined,
        name="unpack",
    )
    return new_end, gx, gy, gz, norm[0, 0]


def solution(mesh):
    fields = P("tm", "space", None, None)
    faces = P("space", None, None)
    quarter = P("space", "tm", None)
    return jax.shard_map(
        shards,
        mesh=mesh,
        in_specs=(fields, faces, faces, faces, faces, faces, fields),
        out_specs=(fields, quarter, quarter, quarter, P()),
        check_vma=False,
    )
```

time: 189 us -> 115 us (0.61)
  Pallas kernels: 87.9 us -> 27.6 us
  waiting for transfers between devices: 31.2 us -> 24.1 us
  local copies, waits for them, and re-layouts: 6.25 us -> 0.57 us
  starting transfers between devices: 13.4 us -> 9.02 us
  blocking collectives: 48.8 us -> 52.8 us
    pallas_call x6 -> x5, Pallas kernels: 87.9 us -> 24.5 us  [call(): pl.pallas_call(functools.partial(kernel, sz), out_shape=outs, scratch_sha...]
    all_to_all x2 -> x1, waiting for transfers between devices: 26.5 us -> 12.6 us  [shards(): both = lax.all_to_all(both, 'space', 0, 0)]
    ppermute x5, waiting for transfers between devices: 2.54 us -> 11.5 us  [exchange(): return lax.ppermute(values, axis, [(i, i ^ bit) for i in range(size)])]
    all_gather x1, blocking collectives: 7.38 us -> 13.6 us  [shards(): jumps = lax.all_gather(jumps, 'tm', axis=0)]
    all_to_all x2 -> x1, starting transfers between devices: 7.23 us -> 3.59 us  [shards(): both = lax.all_to_all(both, 'space', 0, 0)]
    unnamed x18 -> x0, local copies, waits for them, and re-layouts: 3.27 us -> none
    pallas_call x0 -> x1, Pallas kernels: none -> 3.04 us  [shards(): pl.pallas_call(functools.partial(windows_kernel, sz), out_shape=(f32(spac...]
    ppermute x1, waiting for transfers between devices: 2.15 us -> 0.01 us  [shards(): lax.ppermute(rough, 'tm', [(i + 1, i) for i in range(spans - 1)])]
  transfers between devices with their start and end apart: 8 -> 7, of which waited for: 4 -> 2; matrix products, arithmetic and copies ran while one was open for 0% -> 0% of each run, Pallas kernels for 12% -> 20%
where the time goes in v2:
time: 115 us
  blocking collectives  52.8 us (46%)
  Pallas kernels  27.6 us (24%)
  waiting for transfers between devices  24.1 us (21%)
  starting transfers between devices  9.02 us (8%)
    pallas_call x5, Pallas kernels, call(): pl.pallas_call(functools.partial(kernel, sz), out_shape=outs, scratch_sha...  24.5 us
    all_to_all x1, blocking collectives, shards(): coef = lax.all_to_all(coef, 'space', 0, 0)  21.8 us
    all_to_all x1, blocking collectives, shards(): joined = lax.all_to_all(joined, 'space', 0, 0)  17.4 us
    all_gather x1, blocking collectives, shards(): jumps = lax.all_gather(jumps, 'tm', axis=0)  13.6 us
    all_to_all x1, waiting for transfers between devices, shards(): both = lax.all_to_all(both, 'space', 0, 0)  12.6 us
    ppermute x5, waiting for transfers between devices, exchange(): return lax.ppermute(values, axis, [(i, i ^ bit) for i in range(size)])  11.5 us
    ppermute x5, starting transfers between devices, exchange(): return lax.ppermute(values, axis, [(i, i ^ bit) for i in range(size)])  4.14 us
    all_to_all x1, starting transfers between devices, shards(): both = lax.all_to_all(both, 'space', 0, 0)  3.59 us
  transfers between devices with their start and end apart: 7, of which 2 were waited for; matrix products, arithmetic and copies ran while one was open for 0% of the time, Pallas kernels for 20%

profile of v2, /device:TPU:0, one launch (start us, length us, event | category | flops | bytes accessed | tf_op | source)
XLA Modules:
  0.0 114.8 jit_solution(12773298870396861570)
XLA Ops:
  0.6 3.0 %windows.1 = (f32[8,128,128]{2,1,0:T(8,128)}, f32[8,256,128]{2,1,0:T(8,128)}) custom-call(f32[1,2,64,512]{3,2,1,0:T(8,128)} %refs_0_.1, f32[2,64,512]{2,1,0:T(8,128)} %refs_1_.1, f32[2,64,512]{2,1,0:T(8,128)} %refs_2_.1, f32[2,64,512]{2,1,0:T(8,128)} %refs_3_.1, f32[2,64,512]{2,1,0:T(8,128)} %refs_4_.1, s32[2,64,512]{2,1,0:T(8,128)} %refs_5_.1, ...), custom_call_target="tpu_custom_call" | custom-call | tf_op jit(solution)/shard_map/windows/pallas_call | solution.py:464
  3.7 21.8 %all_to_all.15.refs_0_ = f32[8,128,128]{2,1,0:T(8,128)S(1)} all-to-all(f32[8,128,128]{2,1,0:T(8,128)} %get-tuple-element.18), channel_id=1, replica_groups=mesh['tm'=4,'space'=8] {'space'}, dimensions={0} | all-to-all | bytes 1048576 | tf_op jit(solution)/shard_map/all_to_all | solution.py:474
  25.5 3.6 %all-to-all-start.1 = ((f32[8,256,128]{2,1,0:T(8,128)}), f32[8,256,128]{2,1,0:T(8,128)S(1)}, u32[]{:S(2)}, u32[]{:S(2)}) async-start(f32[8,256,128]{2,1,0:T(8,128)} %get-tuple-element.19), calls=%async_computation.1 | async-start | bytes 2097152 | tf_op jit(solution)/shard_map/all_to_all | solution.py:475
  29.1 1.5 %collective-permute-start.1 = (f32[8,128,128]{2,1,0:T(8,128)S(1)}, f32[8,128,128]{2,1,0:T(8,128)S(1)}, u32[]{:S(2)}, u32[]{:S(2)}) collective-permute-start(f32[8,128,128]{2,1,0:T(8,128)S(1)} %all_to_all.15.refs_0_), channel_id=1, source_target_pairs={{0,16},{8,24},{16,0},{24,8},{1,17},{9,25},{17,1},{25,9},{2,18},{10... | collective-permute-start | bytes 1572872 | tf_op jit(solution)/shard_map/ppermute | solution.py:456
  30.6 0.0 collective-permute-start
  30.6 11.5 %collective-permute-done.1.refs_2_ = f32[8,128,128]{2,1,0:T(8,128)S(1)} collective-permute-done((f32[8,128,128]{2,1,0:T(8,128)S(1)}, f32[8,128,128]{2,1,0:T(8,128)S(1)}, u32[]{:S(2)}, u32[]{:S(2)}) %collective-permute-start.1) | collective-permute-done | bytes 524320 | tf_op jit(solution)/shard_map/ppermute | solution.py:456
  42.1 0.0 collective-permute-start.2
  42.1 12.6 %all-to-all-done.1.start_ref.refs_4_ = f32[8,256,128]{2,1,0:T(8,128)S(1)} async-done(((f32[8,256,128]{2,1,0:T(8,128)}), f32[8,256,128]{2,1,0:T(8,128)S(1)}, u32[]{:S(2)}, u32[]{:S(2)}) %all-to-all-start.1) | async-done | bytes 1048608 | tf_op jit(solution)/shard_map/all_to_all | solution.py:475
  54.7 0.2 rough.1
  54.9 1.3 %collective-permute-start.4 = (f32[16,2,8,128]{3,2,1,0:T(8,128)S(1)}, f32[16,2,8,128]{3,2,1,0:T(8,128)S(1)}, u32[]{:S(2)}, u32[]{:S(2)}) collective-permute-start(f32[16,2,8,128]{3,2,1,0:T(8,128)S(1)} %rough.1), channel_id=1, source_target_pairs={{8,0},{16,8},{24,16},{9,1},{17,9},{25,17},{10,2},{18,10},{26,18},{... | collective-permute-start | bytes 393224 | tf_op jit(solution)/shard_map/ppermute | solution.py:488
  56.2 0.0 collective-permute-done.refs_1_
  56.2 0.0 collective-permute-done.2.refs_3_
  56.2 19.8 %fine.1 = (f32[16,8,8,128]{3,2,1,0:T(8,128)S(1)}, f32[16,2,8,128]{3,2,1,0:T(8,128)S(1)}, f32[4,8,48,128]{3,2,1,0:T(8,128)S(1)}) custom-call(f32[8,128,128]{2,1,0:T(8,128)S(1)} %all_to_all.15.refs_0_, f32[8,128,128]{2,1,0:T(8,128)S(1)} %collective-permute-done.refs_1_, f32[8,128,128]{2,1,0:T(8,128)S(1)} %collective-permute-done.1.refs_2_, ...), custom_call_target="tpu_custom_call" | custom-call | tf_op jit(solution)/shard_map/fine/pallas_call | solution.py:445
  76.0 2.2 %collective-permute-start.3 = (f32[2,8,48,128]{3,2,1,0:T(8,128)S(1)}, f32[2,8,48,128]{3,2,1,0:T(8,128)S(1)}, u32[]{:S(2)}, u32[]{:S(2)}) collective-permute-start(f32[2,8,48,128]{3,2,1,0:T(8,128)S(1)} %slice.16), channel_id=1, source_target_pairs={{0,16},{8,24},{16,0},{24,8},{1,17},{9,25},{17,1},{25,9},{2,18},{10... | collective-permute-start | bytes 1179656 | tf_op jit(solution)/shard_map/ppermute | solution.py:456
  78.2 0.0 collective-permute-done.4
  78.3 13.6 %all-gather = f32[64,2,8,128]{3,2,1,0:T(8,128)S(1)} all-gather(f32[16,2,8,128]{3,2,1,0:T(8,128)S(1)} %subtract_select_fusion), channel_id=2, replica_groups=mesh['tm'=4,'space'=8] {'tm'}, dimensions={0}, use_global_device_ids=true | all-gather | bytes 655360 | tf_op jit(solution)/shard_map/all_gather | solution.py:512
  91.8 0.0 collective-permute-done.3
  91.9 0.4 collective-permute-start.5
  92.3 3.6 %coarse.1.ends_ref = f32[8,72,128]{2,1,0:T(8,128)S(1)} custom-call(f32[8,128,128]{2,1,0:T(8,128)S(1)} %all_to_all.15.refs_0_, f32[8,128,128]{2,1,0:T(8,128)S(1)} %collective-permute-done.refs_1_, f32[8,128,128]{2,1,0:T(8,128)S(1)} %collective-permute-done.1.refs_2_, f32[8,128,128]{2,1,0:T(8,128)S(1)} %collective-permute-done.2.refs_3_, ...), custom_call_target="tpu_custom_call" | custom-call | tf_op jit(solution)/shard_map/coarse/pallas_call | solution.py:445
  95.9 0.0 collective-permute-done.5.come_ref
  95.9 17.4 %all_to_all.16.in_ref = f32[8,120,128]{2,1,0:T(8,128)S(1)} all-to-all(f32[8,120,128]{2,1,0:T(8,128)S(1)} %join.1), channel_id=1, replica_groups=mesh['tm'=4,'space'=8] {'space'}, dimensions={0} | all-to-all | bytes 983040 | tf_op jit(solution)/shard_map/all_to_all | solution.py:541
  113.4 1.0 unpack.1
  114.3 0.5 slice.19
  (5 shorter events, 0.2 us)
Async XLA Ops:
  25.5 29.2 %all-to-all-start.1 = ((f32[8,256,128]{2,1,0:T(8,128)}), f32[8,256,128]{2,1,0:T(8,128)S(1)}, u32[]{:S(2)}, u32[]{:S(2)}) async-start(f32[8,256,128]{2,1,0:T(8,128)} %get-tuple-element.19), calls=%async_computation.1 | async-start | bytes 2097152 | tf_op jit(solution)/shard_map/all_to_all | solution.py:475
  29.1 13.0 %collective-permute-start.1 = (f32[8,128,128]{2,1,0:T(8,128)S(1)}, f32[8,128,128]{2,1,0:T(8,128)S(1)}, u32[]{:S(2)}, u32[]{:S(2)}) collective-permute-start(f32[8,128,128]{2,1,0:T(8,128)S(1)} %all_to_all.15.refs_0_), channel_id=1, source_target_pairs={{0,16},{8,24},{16,0},{24,8},{1,17},{9,25},{17,1},{25,9},{2,18},{10... | collective-permute-start | bytes 1572872 | tf_op jit(solution)/shard_map/ppermute | solution.py:456
  30.6 25.6 %collective-permute-start = (f32[8,128,128]{2,1,0:T(8,128)S(1)}, f32[8,128,128]{2,1,0:T(8,128)S(1)}, u32[]{:S(2)}, u32[]{:S(2)}) collective-permute-start(f32[8,128,128]{2,1,0:T(8,128)S(1)} %all_to_all.15.refs_0_), channel_id=1, source_target_pairs={{0,8},{8,0},{16,24},{24,16},{1,9},{9,1},{17,25},{25,17},{2,10},{10... | collective-permute-start | bytes 1572872 | tf_op jit(solution)/shard_map/ppermute | solution.py:456
  42.1 14.1 %collective-permute-start.2 = (f32[8,128,128]{2,1,0:T(8,128)S(1)}, f32[8,128,128]{2,1,0:T(8,128)S(1)}, u32[]{:S(2)}, u32[]{:S(2)}) collective-permute-start(f32[8,128,128]{2,1,0:T(8,128)S(1)} %collective-permute-done.1.refs_2_), channel_id=1, source_target_pairs={{0,8},{8,0},{16,24},{24,16},{1,9},{9,1},{17,25},{25,17},{2,10},{10... | collective-permute-start | bytes 1572872 | tf_op jit(solution)/shard_map/ppermute | solution.py:456
  54.9 23.3 %collective-permute-start.4 = (f32[16,2,8,128]{3,2,1,0:T(8,128)S(1)}, f32[16,2,8,128]{3,2,1,0:T(8,128)S(1)}, u32[]{:S(2)}, u32[]{:S(2)}) collective-permute-start(f32[16,2,8,128]{3,2,1,0:T(8,128)S(1)} %rough.1), channel_id=1, source_target_pairs={{8,0},{16,8},{24,16},{9,1},{17,9},{25,17},{10,2},{18,10},{26,18},{... | collective-permute-start | bytes 393224 | tf_op jit(solution)/shard_map/ppermute | solution.py:488
  76.0 15.8 %collective-permute-start.3 = (f32[2,8,48,128]{3,2,1,0:T(8,128)S(1)}, f32[2,8,48,128]{3,2,1,0:T(8,128)S(1)}, u32[]{:S(2)}, u32[]{:S(2)}) collective-permute-start(f32[2,8,48,128]{3,2,1,0:T(8,128)S(1)} %slice.16), channel_id=1, source_target_pairs={{0,16},{8,24},{16,0},{24,8},{1,17},{9,25},{17,1},{25,9},{2,18},{10... | collective-permute-start | bytes 1179656 | tf_op jit(solution)/shard_map/ppermute | solution.py:456
  91.9 4.0 %collective-permute-start.5 = (f32[1,8,48,128]{3,2,1,0:T(8,128)S(1)}, f32[1,8,48,128]{3,2,1,0:T(8,128)S(1)}, u32[]{:S(2)}, u32[]{:S(2)}) collective-permute-start(f32[1,8,48,128]{3,2,1,0:T(8,128)S(1)} %get-tuple-element.31), channel_id=1, source_target_pairs={{0,8},{8,0},{16,24},{24,16},{1,9},{9,1},{17,25},{25,17},{2,10},{10... | collective-permute-start | bytes 589832 | tf_op jit(solution)/shard_map/ppermute | solution.py:456

commit v3 on v2

--- a/solution.py
+++ b/solution.py
@@ -44,6 +44,13 @@
         self.grad_rows = planes * self.grad_tiles * SUB
         self.end_rows = planes * self.end_tiles * SUB
         self.out_rows = self.grad_rows + self.end_rows + SUB
+        self.reach = TOTAL
+        self.width = self.own + 2 * self.reach
+        self.spare = LANES - self.width
+        self.mains = self.width // self.spare
+        self.start_tiles = planes * self.tiles
+        self.cot_tiles = planes * self.tiles * self.mains // (self.mains + 1)
+        assert self.mains * self.spare == self.width and self.start_tiles % (self.mains + 1) == 0
         assert self.tiles == SUB
         assert TOTAL + 2 * COARSE_SWEEPS * (spans - 1) <= self.halo
 
@@ -71,6 +78,7 @@
 
 def windows_kernel(sz, *refs):
     coef_out, field_out, columns = refs[7:10]
+    ordered = refs[18]
     start_ref, fx_ref, fy_ref, fz_ref, stress_ref, trap_ref, cot_ref = refs[10:17]
     copies = [pltpu.make_async_copy(refs[n], refs[10 + n], refs[17].at[n]) for n in range(7)]
     for n in (1, 2, 3, 4, 5, 0, 6):
@@ -82,15 +90,17 @@
     lane = lane_of((SUB, LANES))
     zero = jnp.zeros((SUB, LANES), jnp.float32)
 
+    def window(parts, first):
+        tile, shift = first // LANES, first % LANES
+        low = parts[tile] if 0 <= tile < count else zero
+        if shift:
+            high = parts[tile + 1] if tile + 1 < count else zero
+            low = roll_lanes(jnp.where(lane < shift, high, low), -shift)
+        return low
+
     def cut(parts, out_ref, rows):
         for j in range(sz.space):
-            first = sz.own * j - sz.halo
-            tile, shift = first // LANES, first % LANES
-            low = parts[tile] if 0 <= tile < count else zero
-            if shift:
-                high = parts[tile + 1] if tile + 1 < count else zero
-                low = roll_lanes(jnp.where(lane < shift, high, low), -shift)
-            out_ref[j, rows, :] = low
+            out_ref[j, rows, :] = window(parts, sz.own * j - sz.halo)
 
     for p in range(sz.planes):
         for n in range(count):
@@ -107,14 +117,32 @@
                 rows = pl.ds(turn * sz.share + a, SUB, stride=sz.tiles)
                 row = ((f * sz.planes + p) * sz.share + a) * SUB
                 cut([columns[f, p, n, rows, :] for n in range(count)], coef_out, slice(row, row + SUB))
-    for f, ref in enumerate((start_ref, cot_ref)):
-        copies[6 * f].wait()
+    def tiled(ref, at):
         for p in range(sz.planes):
-            for r in range(SUB):
-                parts = [
-                    ref[0, p, r * sz.tiles : (r + 1) * sz.tiles, n * LANES : (n + 1) * LANES] for n in range(count)
-                ]
-                cut(parts, field_out, pl.ds((f * sz.planes + p) * sz.ny + r, sz.tiles, stride=SUB))
+            for n in range(count):
+                for r in range(SUB):
+                    rows = slice(r * sz.tiles, (r + 1) * sz.tiles)
+                    ordered[at, p, n, pl.ds(r, sz.tiles, stride=SUB), :] = ref[0, p, rows, n * LANES : (n + 1) * LANES]
+
+    def tile_parts(at, q):
+        p, t = divmod(q, sz.tiles)
+        return [ordered[at, p, n, t * SUB : (t + 1) * SUB, :] for n in range(count)]
+
+    copies[0].wait()
+    tiled(start_ref, 0)
+    for q in range(sz.start_tiles):
+        cut(tile_parts(0, q), field_out, slice(q * SUB, (q + 1) * SUB))
+    copies[6].wait()
+    tiled(cot_ref, 1)
+    for g in range(sz.cot_tiles // sz.mains):
+        parts = [tile_parts(1, g * (sz.mains + 1) + q) for q in range(sz.mains + 1)]
+        for j in range(sz.space):
+            first = sz.own * j - sz.reach
+            last = window(parts[sz.mains], first)
+            for q in range(sz.mains):
+                piece = roll_lanes(last, sz.width - sz.spare * q)
+                row = (sz.start_tiles + g * sz.mains + q) * SUB
+                field_out[j, row : row + SUB, :] = jnp.where(lane < sz.width, window(parts[q], first), piece)
 
 
 def valid_columns(sz):
@@ -228,13 +256,31 @@
         if k:
             weights[k - 1, nx] = rim
 
-    def whole_plane(f, i):
+    lane = lane_of((SUB, LANES))
+    aside = sz.halo - sz.reach
+
+    def start_plane(i):
         s, p = divmod(i, sz.planes)
-        row = (f * sz.planes + p) * sz.ny
-        return field_ref[s, row : row + sz.ny, :].reshape(count, SUB, LANES)
+        return field_ref[s, p * sz.ny : (p + 1) * sz.ny, :].reshape(count, SUB, LANES)
+
+    def cot_tile(s, n):
+        g, q = divmod(n, sz.mains + 1)
+        mains = [sz.start_tiles + g * sz.mains + m for m in range(sz.mains)]
+        main = lambda m: field_ref[s, mains[m] * SUB : (mains[m] + 1) * SUB, :]
+        if q < sz.mains:
+            return roll_lanes(main(q), aside)
+        result = None
+        for m in range(sz.mains):
+            part = roll_lanes(main(m), sz.spare * m - sz.width + aside)
+            result = part if result is None else jnp.where(lane < sz.spare * m + aside, result, part)
+        return result
+
+    def cot_plane(i):
+        s, p = divmod(i, sz.planes)
+        return jnp.stack([cot_tile(s, p * count + t) for t in range(count)])
 
     for i in range(nx):
-        v = whole_plane(0, i)
+        v = start_plane(i)
         store_plane(even, i, v, count)
         keep_plane(fields, 0, i, v, count)
     for step in range(FINE_STEPS):
@@ -256,7 +302,7 @@
             rough_out[i, m] = rough
 
     for i in range(nx):
-        v = faces[3, i] * whole_plane(1, i)
+        v = faces[3, i] * cot_plane(i)
         store_plane(even, i, v, count)
         keep_plane(weights, TOTAL - 1, i, v, count)
     for step in reversed(range(FINE_STEPS)):
@@ -318,9 +364,8 @@
                     value = value - there
                 rows[d, i, pl.ds(t, SUB, stride=count), :] = TIME_STEP * value
 
-    lane = lane_of((SUB, LANES))
-    for key in range(sz.spans):
-        first = (turn ^ key) * sz.quarter
+    for at in range(sz.spans):
+        first = (turn ^ turned(at, sz.spans)) * sz.quarter
         for i in range(nx):
             dest, p = divmod(i, sz.planes)
             for g in range(sz.grad_tiles):
@@ -330,11 +375,11 @@
                     if n >= sz.grad_parts:
                         continue
                     f, r = divmod(n, sz.share)
-                    at = pl.ds(pl.multiple_of(first + r * SUB, SUB), SUB)
-                    part = roll_lanes(rows[f, i, at, :], sz.own * q - sz.halo)
+                    place = pl.ds(pl.multiple_of(first + r * SUB, SUB), SUB)
+                    part = roll_lanes(rows[f, i, place, :], sz.own * q - sz.halo)
                     tile = part if tile is None else jnp.where(lane < sz.own * q, tile, part)
                 row = (p * sz.grad_tiles + g) * SUB
-                grads_out[key, dest, row : row + SUB, :] = tile
+                grads_out[at, dest, row : row + SUB, :] = tile
 
 
 def rough_kernel(sz, start_ref, out_ref):
@@ -432,7 +477,7 @@
         squares = squares + in_ref[s, sz.grad_rows + sz.end_rows :, :]
     cells = (sz.spans - 1) * sz.nx * (sz.ny // 2) * (sz.nz // 2)
     whole = jnp.sum(jnp.sum(squares, axis=1, keepdims=True), axis=0, keepdims=True)
-    norm_out[...] = jnp.sqrt(jnp.broadcast_to(whole, (SUB, LANES)) / cells)
+    norm_out[...] = jnp.sqrt(whole / cells)
 
 
 def f32(*shape):
@@ -451,6 +496,13 @@
     )(*args)
 
 
+def turned(index, size):
+    result = 0
+    while size > 1:
+        result, index, size = result * 2 + index % 2, index // 2, size // 2
+    return result
+
+
 def exchange(values, axis, bit):
     size = lax.axis_size(axis)
     return lax.ppermute(values, axis, [(i, i ^ bit) for i in range(size)])
@@ -463,11 +515,12 @@
     inputs = (start_states, diff_x, diff_y, diff_z, stress, trap_class, cotangent)
     coef, both = pl.pallas_call(
         functools.partial(windows_kernel, sz),
-        out_shape=(f32(space, 4 * sz.planes * sz.quarter, LANES), f32(space, 2 * sz.planes * ny, LANES)),
+        out_shape=(f32(space, 4 * sz.planes * sz.quarter, LANES), f32(space, (sz.start_tiles + sz.cot_tiles) * SUB, LANES)),
         in_specs=[pl.BlockSpec(memory_space=pltpu.HBM)] * len(inputs),
         scratch_shapes=[pltpu.VMEM((4, sz.planes, sz.nz // LANES, ny, LANES), jnp.float32)]
         + [pltpu.VMEM(array.shape, array.dtype) for array in inputs]
-        + [pltpu.SemaphoreType.DMA((len(inputs),))],
+        + [pltpu.SemaphoreType.DMA((len(inputs),))]
+        + [pltpu.VMEM((2, sz.planes, sz.nz // LANES, ny, LANES), jnp.float32)],
         compiler_params=pltpu.CompilerParams(vmem_limit_bytes=60 * 1024 * 1024),
         name="windows",
     )(*inputs)
@@ -511,14 +564,14 @@
     jumps = jnp.where(lax.axis_index("tm") == spans - 1, 0.0, rough_end - following)
     jumps = lax.all_gather(jumps, "tm", axis=0)
 
-    bit = spans // 2
-    while bit:
-        come = exchange(grads[bit:], "tm", bit)
-        kept = grads[:bit]
-        if bit == spans // 2:
+    half, bit = spans // 2, 1
+    while half:
+        come = exchange(grads[half:], "tm", bit)
+        kept = grads[:half]
+        if bit == 1:
             come, jumps = lax.optimization_barrier((come, jumps))
-        grads = kept + come if bit > 1 else None
-        bit //= 2
+        grads = kept + come if half > 1 else None
+        half, bit = half // 2, bit * 2
 
     ends = call(
         coarse_kernel,
@@ -543,12 +596,12 @@
     new_end, gx, gy, gz, norm = call(
         unpack_kernel,
         sz,
-        (f32(1, sz.planes, ny, sz.nz), quarter, quarter, quarter, f32(SUB, LANES)),
+        (f32(1, sz.planes, ny, sz.nz), quarter, quarter, quarter, f32(1, 1)),
         ((sz.nz // LANES, sz.planes, ny, LANES),),
         joined,
         name="unpack",
     )
-    return new_end, gx, gy, gz, norm[0, 0]
+    return new_end, gx, gy, gz, norm.reshape(())
 
 
 def solution(mesh):

time: 115 us -> 108 us (0.939)
  blocking collectives: 52.8 us -> 45.7 us
    all_gather x1, blocking collectives: 13.6 us -> 7.18 us  [shards(): jumps = lax.all_gather(jumps, 'tm', axis=0)]
    all_to_all x1, waiting for transfers between devices: 12.6 us -> 9.79 us  [shards(): both = lax.all_to_all(both, 'space', 0, 0)]
    ppermute x5, waiting for transfers between devices: 11.5 us -> 13.8 us  [exchange(): return lax.ppermute(values, axis, [(i, i ^ bit) for i in range(size)])]
  transfers between devices with their start and end apart: 7 -> 7, of which waited for: 2 -> 3; matrix products, arithmetic and copies ran while one was open for 0% -> 0% of each run, Pallas kernels for 20% -> 22%
where the time goes in v3:
time: 108 us
  blocking collectives  45.7 us (42%)
  Pallas kernels  28.7 us (27%)
  waiting for transfers between devices  23.6 us (22%)
  starting transfers between devices  8.98 us (8%)
    pallas_call x5, Pallas kernels, call(): pl.pallas_call(functools.partial(kernel, sz), out_shape=outs, scratch_sha...  24.7 us
    all_to_all x1, blocking collectives, shards(): coef = lax.all_to_all(coef, 'space', 0, 0)  21.8 us
    all_to_all x1, blocking collectives, shards(): joined = lax.all_to_all(joined, 'space', 0, 0)  16.7 us
    ppermute x5, waiting for transfers between devices, exchange(): return lax.ppermute(values, axis, [(i, i ^ bit) for i in range(size)])  13.8 us
    all_to_all x1, waiting for transfers between devices, shards(): both = lax.all_to_all(both, 'space', 0, 0)  9.79 us
    all_gather x1, blocking collectives, shards(): jumps = lax.all_gather(jumps, 'tm', axis=0)  7.18 us
    ppermute x5, starting transfers between devices, exchange(): return lax.ppermute(values, axis, [(i, i ^ bit) for i in range(size)])  4.1 us
    pallas_call x1, Pallas kernels, shards(): pl.pallas_call(functools.partial(windows_kernel, sz), out_shape=(f32(spac...  4.01 us
  transfers between devices with their start and end apart: 7, of which 3 were waited for; matrix products, arithmetic and copies ran while one was open for 0% of the time, Pallas kernels for 22%

profile of v3, /device:TPU:0, one launch (start us, length us, event | category | flops | bytes accessed | tf_op | source)
XLA Modules:
  0.0 107.8 jit_solution(13332573892761864191)
XLA Ops:
  0.6 4.0 %windows.1 = (f32[8,128,128]{2,1,0:T(8,128)}, f32[8,224,128]{2,1,0:T(8,128)}) custom-call(f32[1,2,64,512]{3,2,1,0:T(8,128)} %refs_0_.1, f32[2,64,512]{2,1,0:T(8,128)} %refs_1_.1, f32[2,64,512]{2,1,0:T(8,128)} %refs_2_.1, f32[2,64,512]{2,1,0:T(8,128)} %refs_3_.1, f32[2,64,512]{2,1,0:T(8,128)} %refs_4_.1, s32[2,64,512]{2,1,0:T(8,128)} %refs_5_.1, ...), custom_call_target="tpu_custom_call" | custom-call | tf_op jit(solution)/shard_map/windows/pallas_call | solution.py:516
  4.7 21.8 %all_to_all.15.refs_0_ = f32[8,128,128]{2,1,0:T(8,128)S(1)} all-to-all(f32[8,128,128]{2,1,0:T(8,128)} %get-tuple-element.18), channel_id=1, replica_groups=mesh['tm'=4,'space'=8] {'space'}, dimensions={0} | all-to-all | bytes 1048576 | tf_op jit(solution)/shard_map/all_to_all | solution.py:527
  26.5 3.6 %all-to-all-start.1 = ((f32[8,224,128]{2,1,0:T(8,128)}), f32[8,224,128]{2,1,0:T(8,128)S(1)}, u32[]{:S(2)}, u32[]{:S(2)}) async-start(f32[8,224,128]{2,1,0:T(8,128)} %get-tuple-element.19), calls=%async_computation.1 | async-start | bytes 1835008 | tf_op jit(solution)/shard_map/all_to_all | solution.py:528
  30.1 1.5 %collective-permute-start.1 = (f32[8,128,128]{2,1,0:T(8,128)S(1)}, f32[8,128,128]{2,1,0:T(8,128)S(1)}, u32[]{:S(2)}, u32[]{:S(2)}) collective-permute-start(f32[8,128,128]{2,1,0:T(8,128)S(1)} %all_to_all.15.refs_0_), channel_id=1, source_target_pairs={{0,16},{8,24},{16,0},{24,8},{1,17},{9,25},{17,1},{25,9},{2,18},{10... | collective-permute-start | bytes 1572872 | tf_op jit(solution)/shard_map/ppermute | solution.py:508
  31.6 0.0 collective-permute-start
  31.6 11.5 %collective-permute-done.1.refs_2_ = f32[8,128,128]{2,1,0:T(8,128)S(1)} collective-permute-done((f32[8,128,128]{2,1,0:T(8,128)S(1)}, f32[8,128,128]{2,1,0:T(8,128)S(1)}, u32[]{:S(2)}, u32[]{:S(2)}) %collective-permute-start.1) | collective-permute-done | bytes 524320 | tf_op jit(solution)/shard_map/ppermute | solution.py:508
  43.1 0.0 collective-permute-start.2
  43.1 9.8 %all-to-all-done.1.start_ref.refs_4_ = f32[8,224,128]{2,1,0:T(8,128)S(1)} async-done(((f32[8,224,128]{2,1,0:T(8,128)}), f32[8,224,128]{2,1,0:T(8,128)S(1)}, u32[]{:S(2)}, u32[]{:S(2)}) %all-to-all-start.1) | async-done | bytes 917536 | tf_op jit(solution)/shard_map/all_to_all | solution.py:528
  52.9 0.2 rough.1
  53.1 1.3 %collective-permute-start.4 = (f32[16,2,8,128]{3,2,1,0:T(8,128)S(1)}, f32[16,2,8,128]{3,2,1,0:T(8,128)S(1)}, u32[]{:S(2)}, u32[]{:S(2)}) collective-permute-start(f32[16,2,8,128]{3,2,1,0:T(8,128)S(1)} %rough.1), channel_id=1, source_target_pairs={{8,0},{16,8},{24,16},{9,1},{17,9},{25,17},{10,2},{18,10},{26,18},{... | collective-permute-start | bytes 393224 | tf_op jit(solution)/shard_map/ppermute | solution.py:541
  54.4 0.0 collective-permute-done.refs_1_
  54.4 0.0 collective-permute-done.2.refs_3_
  54.4 19.9 %fine.1 = (f32[16,8,8,128]{3,2,1,0:T(8,128)S(1)}, f32[16,2,8,128]{3,2,1,0:T(8,128)S(1)}, f32[4,8,48,128]{3,2,1,0:T(8,128)S(1)}) custom-call(f32[8,128,128]{2,1,0:T(8,128)S(1)} %all_to_all.15.refs_0_, f32[8,128,128]{2,1,0:T(8,128)S(1)} %collective-permute-done.refs_1_, f32[8,128,128]{2,1,0:T(8,128)S(1)} %collective-permute-done.1.refs_2_, ...), custom_call_target="tpu_custom_call" | custom-call | tf_op jit(solution)/shard_map/fine/pallas_call | solution.py:490
  74.4 1.2 %collective-permute-start.3 = (f32[2,8,48,128]{3,2,1,0:T(8,128)S(1)}, f32[2,8,48,128]{3,2,1,0:T(8,128)S(1)}, u32[]{:S(2)}, u32[]{:S(2)}) collective-permute-start(f32[2,8,48,128]{3,2,1,0:T(8,128)S(1)} %slice.13), channel_id=1, source_target_pairs={{0,8},{8,0},{16,24},{24,16},{1,9},{9,1},{17,25},{25,17},{2,10},{10... | collective-permute-start | bytes 1179656 | tf_op jit(solution)/shard_map/ppermute | solution.py:508
  75.6 0.0 collective-permute-done.4
  75.6 7.2 %all-gather = f32[64,2,8,128]{3,2,1,0:T(8,128)S(1)} all-gather(f32[16,2,8,128]{3,2,1,0:T(8,128)S(1)} %subtract_select_fusion), channel_id=2, replica_groups=mesh['tm'=4,'space'=8] {'tm'}, dimensions={0}, use_global_device_ids=true | all-gather | bytes 655360 | tf_op jit(solution)/shard_map/all_gather | solution.py:565
  82.8 0.0 collective-permute-done.3
  82.9 1.4 %collective-permute-start.5 = (f32[1,8,48,128]{3,2,1,0:T(8,128)S(1)}, f32[1,8,48,128]{3,2,1,0:T(8,128)S(1)}, u32[]{:S(2)}, u32[]{:S(2)}) collective-permute-start(f32[1,8,48,128]{3,2,1,0:T(8,128)S(1)} %get-tuple-element.31), channel_id=1, source_target_pairs={{0,16},{8,24},{16,0},{24,8},{1,17},{9,25},{17,1},{25,9},{2,18},{10... | collective-permute-start | bytes 589832 | tf_op jit(solution)/shard_map/ppermute | solution.py:508
  84.2 3.6 %coarse.1.ends_ref = f32[8,72,128]{2,1,0:T(8,128)S(1)} custom-call(f32[8,128,128]{2,1,0:T(8,128)S(1)} %all_to_all.15.refs_0_, f32[8,128,128]{2,1,0:T(8,128)S(1)} %collective-permute-done.refs_1_, f32[8,128,128]{2,1,0:T(8,128)S(1)} %collective-permute-done.1.refs_2_, f32[8,128,128]{2,1,0:T(8,128)S(1)} %collective-permute-done.2.refs_3_, ...), custom_call_target="tpu_custom_call" | custom-call | tf_op jit(solution)/shard_map/coarse/pallas_call | solution.py:490
  87.8 2.3 %collective-permute-done.5.come_ref = f32[1,8,48,128]{3,2,1,0:T(8,128)S(1)} collective-permute-done((f32[1,8,48,128]{3,2,1,0:T(8,128)S(1)}, f32[1,8,48,128]{3,2,1,0:T(8,128)S(1)}, u32[]{:S(2)}, u32[]{:S(2)}) %collective-permute-start.5) | collective-permute-done | bytes 196640 | tf_op jit(solution)/shard_map/ppermute | solution.py:508
  90.1 16.7 %all_to_all.16.in_ref = f32[8,120,128]{2,1,0:T(8,128)S(1)} all-to-all(f32[8,120,128]{2,1,0:T(8,128)S(1)} %join.1), channel_id=1, replica_groups=mesh['tm'=4,'space'=8] {'space'}, dimensions={0} | all-to-all | bytes 983040 | tf_op jit(solution)/shard_map/all_to_all | solution.py:594
  106.8 1.0 unpack.1
  (5 shorter events, 0.2 us)
Async XLA Ops:
  26.5 26.4 %all-to-all-start.1 = ((f32[8,224,128]{2,1,0:T(8,128)}), f32[8,224,128]{2,1,0:T(8,128)S(1)}, u32[]{:S(2)}, u32[]{:S(2)}) async-start(f32[8,224,128]{2,1,0:T(8,128)} %get-tuple-element.19), calls=%async_computation.1 | async-start | bytes 1835008 | tf_op jit(solution)/shard_map/all_to_all | solution.py:528
  30.1 13.0 %collective-permute-start.1 = (f32[8,128,128]{2,1,0:T(8,128)S(1)}, f32[8,128,128]{2,1,0:T(8,128)S(1)}, u32[]{:S(2)}, u32[]{:S(2)}) collective-permute-start(f32[8,128,128]{2,1,0:T(8,128)S(1)} %all_to_all.15.refs_0_), channel_id=1, source_target_pairs={{0,16},{8,24},{16,0},{24,8},{1,17},{9,25},{17,1},{25,9},{2,18},{10... | collective-permute-start | bytes 1572872 | tf_op jit(solution)/shard_map/ppermute | solution.py:508
  31.6 22.8 %collective-permute-start = (f32[8,128,128]{2,1,0:T(8,128)S(1)}, f32[8,128,128]{2,1,0:T(8,128)S(1)}, u32[]{:S(2)}, u32[]{:S(2)}) collective-permute-start(f32[8,128,128]{2,1,0:T(8,128)S(1)} %all_to_all.15.refs_0_), channel_id=1, source_target_pairs={{0,8},{8,0},{16,24},{24,16},{1,9},{9,1},{17,25},{25,17},{2,10},{10... | collective-permute-start | bytes 1572872 | tf_op jit(solution)/shard_map/ppermute | solution.py:508
  43.1 11.3 %collective-permute-start.2 = (f32[8,128,128]{2,1,0:T(8,128)S(1)}, f32[8,128,128]{2,1,0:T(8,128)S(1)}, u32[]{:S(2)}, u32[]{:S(2)}) collective-permute-start(f32[8,128,128]{2,1,0:T(8,128)S(1)} %collective-permute-done.1.refs_2_), channel_id=1, source_target_pairs={{0,8},{8,0},{16,24},{24,16},{1,9},{9,1},{17,25},{25,17},{2,10},{10... | collective-permute-start | bytes 1572872 | tf_op jit(solution)/shard_map/ppermute | solution.py:508
  53.1 22.5 %collective-permute-start.4 = (f32[16,2,8,128]{3,2,1,0:T(8,128)S(1)}, f32[16,2,8,128]{3,2,1,0:T(8,128)S(1)}, u32[]{:S(2)}, u32[]{:S(2)}) collective-permute-start(f32[16,2,8,128]{3,2,1,0:T(8,128)S(1)} %rough.1), channel_id=1, source_target_pairs={{8,0},{16,8},{24,16},{9,1},{17,9},{25,17},{10,2},{18,10},{26,18},{... | collective-permute-start | bytes 393224 | tf_op jit(solution)/shard_map/ppermute | solution.py:541
  74.4 8.4 %collective-permute-start.3 = (f32[2,8,48,128]{3,2,1,0:T(8,128)S(1)}, f32[2,8,48,128]{3,2,1,0:T(8,128)S(1)}, u32[]{:S(2)}, u32[]{:S(2)}) collective-permute-start(f32[2,8,48,128]{3,2,1,0:T(8,128)S(1)} %slice.13), channel_id=1, source_target_pairs={{0,8},{8,0},{16,24},{24,16},{1,9},{9,1},{17,25},{25,17},{2,10},{10... | collective-permute-start | bytes 1179656 | tf_op jit(solution)/shard_map/ppermute | solution.py:508
  82.9 7.2 %collective-permute-start.5 = (f32[1,8,48,128]{3,2,1,0:T(8,128)S(1)}, f32[1,8,48,128]{3,2,1,0:T(8,128)S(1)}, u32[]{:S(2)}, u32[]{:S(2)}) collective-permute-start(f32[1,8,48,128]{3,2,1,0:T(8,128)S(1)} %get-tuple-element.31), channel_id=1, source_target_pairs={{0,16},{8,24},{16,0},{24,8},{1,17},{9,25},{17,1},{25,9},{2,18},{10... | collective-permute-start | bytes 589832 | tf_op jit(solution)/shard_map/ppermute | solution.py:508

commit v4 on v3

--- a/solution.py
+++ b/solution.py
@@ -20,7 +20,7 @@
 COARSE_STEP = FINE_STEPS * TIME_STEP
 TRAP_LEVELS = (0.0, 1.0, 3.0, 7.0)
 
-SPARE_BYTES = 2 * 1024 * 1024
+SPARE_BYTES = 3 * 512 * 1024
 
 
 class Sizes:
@@ -76,47 +76,65 @@
     return v if by == 0 else pltpu.roll(v, by, 1)
 
 
-def windows_kernel(sz, *refs):
-    coef_out, field_out, columns = refs[7:10]
-    ordered = refs[18]
-    start_ref, fx_ref, fy_ref, fz_ref, stress_ref, trap_ref, cot_ref = refs[10:17]
-    copies = [pltpu.make_async_copy(refs[n], refs[10 + n], refs[17].at[n]) for n in range(7)]
-    for n in (1, 2, 3, 4, 5, 0, 6):
-        copies[n].start()
-    for n in (1, 2, 3, 4, 5):
-        copies[n].wait()
+def window(parts, first):
+    lane = lane_of((SUB, LANES))
+    zero = jnp.zeros((SUB, LANES), jnp.float32)
+    tile, shift = first // LANES, first % LANES
+    low = parts[tile] if 0 <= tile < len(parts) else zero
+    if shift:
+        high = parts[tile + 1] if tile + 1 < len(parts) else zero
+        low = roll_lanes(jnp.where(lane < shift, high, low), -shift)
+    return low
+
+
+def start_copies(refs, count):
+    copies = [pltpu.make_async_copy(refs[n], refs[count + 1 + n], refs[-1].at[n]) for n in range(count)]
+    for copy in copies:
+        copy.start()
+    return copies
+
+
+def face_windows_kernel(sz, *refs):
+    fx_ref, fy_ref, fz_ref, stress_ref, trap_ref = refs[6:11]
+    coef_out, columns = refs[5], refs[11]
     turn = lax.axis_index("tm")
     count = sz.nz // LANES
-    lane = lane_of((SUB, LANES))
-    zero = jnp.zeros((SUB, LANES), jnp.float32)
-
-    def window(parts, first):
-        tile, shift = first // LANES, first % LANES
-        low = parts[tile] if 0 <= tile < count else zero
-        if shift:
-            high = parts[tile + 1] if tile + 1 < count else zero
-            low = roll_lanes(jnp.where(lane < shift, high, low), -shift)
-        return low
-
-    def cut(parts, out_ref, rows):
-        for j in range(sz.space):
-            out_ref[j, rows, :] = window(parts, sz.own * j - sz.halo)
-
+    copies = start_copies(refs, 5)
+
+    def cut_field(f, p):
+        for a in range(sz.share):
+            rows = pl.ds(turn * sz.share + a, SUB, stride=sz.tiles)
+            row = ((f * sz.planes + p) * sz.share + a) * SUB
+            parts = [columns[f, p, n, rows, :] for n in range(count)]
+            for j in range(sz.space):
+                coef_out[j, row : row + SUB, :] = window(parts, sz.own * j - sz.halo)
+
+    for f, ref in enumerate((fx_ref, fy_ref, fz_ref)):
+        copies[f].wait()
+        for p in range(sz.planes):
+            for n in range(count):
+                columns[f, p, n] = ref[p, :, n * LANES : (n + 1) * LANES]
+            cut_field(f, p)
+    copies[3].wait()
+    copies[4].wait()
     for p in range(sz.planes):
         for n in range(count):
             cells = slice(n * LANES, (n + 1) * LANES)
-            for f, ref in enumerate((fx_ref, fy_ref, fz_ref)):
-                columns[f, p, n] = ref[p, :, cells]
             trap = trap_ref[p, :, cells]
             level = jnp.zeros(trap.shape, jnp.float32)
             for position, value in enumerate(TRAP_LEVELS):
                 level = level + jnp.where(trap == position, value, 0.0)
             columns[3, p, n] = (1.0 + level) * jnp.exp(STRESS_COUPLING * stress_ref[p, :, cells])
-        for f in range(4):
-            for a in range(sz.share):
-                rows = pl.ds(turn * sz.share + a, SUB, stride=sz.tiles)
-                row = ((f * sz.planes + p) * sz.share + a) * SUB
-                cut([columns[f, p, n, rows, :] for n in range(count)], coef_out, slice(row, row + SUB))
+        cut_field(3, p)
+
+
+def field_windows_kernel(sz, *refs):
+    start_ref, cot_ref = refs[3:5]
+    field_out, ordered = refs[2], refs[5]
+    count = sz.nz // LANES
+    lane = lane_of((SUB, LANES))
+    copies = start_copies(refs, 2)
+
     def tiled(ref, at):
         for p in range(sz.planes):
             for n in range(count):
@@ -131,8 +149,10 @@
     copies[0].wait()
     tiled(start_ref, 0)
     for q in range(sz.start_tiles):
-        cut(tile_parts(0, q), field_out, slice(q * SUB, (q + 1) * SUB))
-    copies[6].wait()
+        parts = tile_parts(0, q)
+        for j in range(sz.space):
+            field_out[j, q * SUB : (q + 1) * SUB, :] = window(parts, sz.own * j - sz.halo)
+    copies[1].wait()
     tiled(cot_ref, 1)
     for g in range(sz.cot_tiles // sz.mains):
         parts = [tile_parts(1, g * (sz.mains + 1) + q) for q in range(sz.mains + 1)]
@@ -169,7 +189,7 @@
     return jnp.where(row_of(v.shape) == 0, 0.0, pltpu.roll(v, 1, v.ndim - 2))
 
 
-def normalise(sz, faces, coef, count, step, apart):
+def normalise(sz, faces, coef, scale, count, step, apart):
     valid = valid_columns(sz)
 
     def one(i):
@@ -183,8 +203,8 @@
             scaled = step * inv
             for n, face in enumerate((fx, bx, fy, by, fz, bz)):
                 coef[n, i, t] = face * scaled
-            faces[2, i, t] = cap * inv
-            faces[3, i, t] = inv
+            scale[0, i, t] = cap * inv
+            scale[1, i, t] = inv
 
     def some(g, c):
         for q in range(4):
@@ -216,6 +236,27 @@
             keep_plane(kept[0], kept[1], i, result, count)
 
 
+def two_sweeps(sz, coef, count, source, forward, adjoint):
+    for i in range(sz.nx):
+        factors = [coef[n, i] for n in range(6)]
+        for job in (forward, adjoint):
+            if job is None:
+                continue
+            now, later, kept, at = job
+            v = now[i, 1 : count + 1]
+            result = factors[2] * now[i, 2 : count + 2] + factors[3] * now[i, 0:count]
+            result = result + factors[4] * z_up(v) + factors[5] * z_down(v)
+            if i + 1 < sz.nx:
+                result = result + factors[0] * now[i + 1, 1 : count + 1]
+            if i:
+                result = result + factors[1] * now[i - 1, 1 : count + 1]
+            if job is forward:
+                result = result + source[0, i]
+            store_plane(later, i, result, count)
+            if kept is not None:
+                keep_plane(kept, at, i, result, count)
+
+
 def keep_plane(ref, k, i, v, count):
     ref[k, i, 0:count] = v
     ref[k, i, count] = next_sublane(v[0])
@@ -239,16 +280,19 @@
     return [packed(coarse_rows(tile_of, 2 * m), coarse_rows(tile_of, 2 * m + 1)) for m in range(sz.tiles // 4)]
 
 
+def factors_kernel(sz, *refs):
+    pieces = refs[: sz.spans]
+    coef_out, scale_out, faces = refs[sz.spans :]
+    lay_out_faces(sz, pieces, faces)
+    normalise(sz, faces, coef_out, scale_out, sz.tiles, TIME_STEP, 1)
+
+
 def fine_kernel(sz, *refs):
-    pieces = refs[: sz.spans]
-    field_ref, end_out, rough_out, grads_out = refs[sz.spans : sz.spans + 4]
-    faces, coef, even, odd, source, fields, weights = refs[sz.spans + 4 :]
+    coef, scale, field_ref, end_out, rough_out, grads_out = refs[:6]
+    sums, even, odd, back, forth, fields, weights = refs[6:]
     nx, count = sz.nx, sz.tiles
     body = slice(1, count + 1)
     turn = lax.axis_index("tm")
-
-    lay_out_faces(sz, pieces, faces)
-    normalise(sz, faces, coef, count, TIME_STEP, 1)
 
     rim = jnp.zeros((count + 1, SUB, LANES), jnp.float32)
     for k in range(TOTAL + 1):
@@ -283,57 +327,48 @@
         v = start_plane(i)
         store_plane(even, i, v, count)
         keep_plane(fields, 0, i, v, count)
+        v = scale[1, i] * cot_plane(i)
+        store_plane(back, i, v, count)
+        keep_plane(weights, TOTAL - 1, i, v, count)
+
     for step in range(FINE_STEPS):
-        base = step * SWEEPS
+        up, down = step * SWEEPS, (FINE_STEPS - 1 - step) * SWEEPS
+        final = down == 0
         for i in range(nx):
-            source[i] = faces[2, i] * even[i, body]
-
-        def two(n, c):
-            k = base + 2 * n
-            sweep(sz, coef, even, odd, count, 1, source, (fields, k + 1))
-            sweep(sz, coef, odd, even, count, 1, source, (fields, k + 2))
+            sums[0, i] = scale[0, i] * even[i, body]
+
+        def pair(n, c):
+            k, m = up + 2 * n, down + SWEEPS - 1 - 2 * n
+            two_sweeps(sz, coef, count, sums, (even, odd, fields, k + 1), (back, forth, weights, m - 1))
+            two_sweeps(sz, coef, count, sums, (odd, even, fields, k + 2), (forth, back, weights, m - 2))
             return c
 
-        lax.fori_loop(0, SWEEPS // 2, two, 0)
+        lax.fori_loop(0, SWEEPS // 2 - final, pair, 0)
+        if final:
+            k = up + SWEEPS
+            two_sweeps(sz, coef, count, sums, (even, odd, fields, k - 1), (back, forth, weights, 0))
+            two_sweeps(sz, coef, count, sums, (odd, even, fields, k), None)
+        else:
+            for i in range(nx):
+                total = weights[down, i, 0:count]
+                for k in range(down + 1, down + SWEEPS):
+                    total = total + weights[k, i, 0:count]
+                v = back[i, body] + scale[0, i] * total
+                store_plane(back, i, v, count)
+                keep_plane(weights, down - 1, i, v, count)
 
     for i in range(nx):
         end_out[i] = even[i, body]
         for m, rough in enumerate(pack_rough(sz, lambda t: even[i, 1 + t])):
             rough_out[i, m] = rough
 
-    for i in range(nx):
-        v = faces[3, i] * cot_plane(i)
-        store_plane(even, i, v, count)
-        keep_plane(weights, TOTAL - 1, i, v, count)
-    for step in reversed(range(FINE_STEPS)):
-        base = step * SWEEPS
-
-        def two_back(n, c):
-            k = base + SWEEPS - 1 - 2 * n
-            sweep(sz, coef, even, odd, count, 1, None, (weights, k - 1))
-            sweep(sz, coef, odd, even, count, 1, None, (weights, k - 2))
-            return c
-
-        lax.fori_loop(0, SWEEPS // 2 - 1, two_back, 0)
-        sweep(sz, coef, even, odd, count, 1, None, (weights, base))
-        if step:
-            sweep(sz, coef, odd, even, count, 1, None)
-            for i in range(nx):
-                total = weights[base, i, 0:count]
-                for k in range(base + 1, base + SWEEPS):
-                    total = total + weights[k, i, 0:count]
-                v = even[i, body] + faces[2, i] * total
-                store_plane(odd, i, v, count)
-                keep_plane(weights, base - 1, i, v, count)
-            for i in range(nx):
-                even[i] = odd[i]
-
     def gather_sums(i, c):
         for t in range(count):
             along = [None, None, None]
             whole = None
+            following = fields[0, i, t]
             for k in range(TOTAL):
-                w, u = weights[k, i, t], fields[k, i, t]
+                w, u, following = weights[k, i, t], following, fields[k + 1, i, t]
                 for d, (up_w, up_u) in enumerate(
                     (
                         (weights[k, i + 1, t], fields[k, i + 1, t]),
@@ -343,10 +378,10 @@
                 ):
                     term = w * up_u + up_w * u
                     along[d] = term if along[d] is None else along[d] + term
-                term = w * fields[k + 1, i, t]
+                term = w * following
                 whole = term if whole is None else whole + term
             for d in range(3):
-                faces[d, i, t] = along[d]
+                sums[d, i, t] = along[d]
             even[i, t] = whole
             if t == 0:
                 even[i, count] = next_sublane(whole)
@@ -359,7 +394,7 @@
         for t in range(count):
             here = even[i, t]
             for d, there in enumerate((even[i + 1, t] if i + 1 < nx else None, even[i, t + 1], z_up(here))):
-                value = faces[d, i, t] - here
+                value = sums[d, i, t] - here
                 if there is not None:
                     value = value - there
                 rows[d, i, pl.ds(t, SUB, stride=count), :] = TIME_STEP * value
@@ -393,17 +428,17 @@
 def coarse_kernel(sz, *refs):
     pieces = refs[: sz.spans]
     jumps_ref, end_ref, out_ref = refs[sz.spans : sz.spans + 3]
-    faces, rough, coef, even, odd, source = refs[sz.spans + 3 :]
+    faces, rough, coef, scale, even, odd, source = refs[sz.spans + 3 :]
     nx, count = sz.nx, sz.tiles // 2
     body = slice(1, count + 1)
     turn = lax.axis_index("tm")
     lay_out_faces(sz, pieces, faces)
     for i in range(nx):
-        for f, scale in enumerate((1.0, 0.25, 0.25, 1.0)):
+        for f, part in enumerate((1.0, 0.25, 0.25, 1.0)):
             for m in range(count):
                 v = coarse_rows(lambda t: faces[f, i, t], m)
-                rough[f, i, m] = v if scale == 1.0 else scale * v
-    normalise(sz, rough, coef, count, COARSE_STEP, 2)
+                rough[f, i, m] = v if part == 1.0 else part * v
+    normalise(sz, rough, coef, scale, count, COARSE_STEP, 2)
 
     lane = lane_of((SUB, LANES))
     mine = (lane >= sz.halo) & (lane < sz.halo + sz.own)
@@ -425,7 +460,7 @@
             if d < sz.spans - 1:
                 v = v + even[i, body]
             store_plane(even, i, v, count)
-            source[i] = rough[2, i] * v
+            source[i] = scale[0, i] * v
         for n in range(COARSE_SWEEPS // 2):
             sweep(sz, coef, even, odd, count, 2, source)
             sweep(sz, coef, odd, even, count, 2, source)
@@ -484,7 +519,7 @@
     return jax.ShapeDtypeStruct(shape, jnp.float32)
 
 
-def call(kernel, sz, outs, scratch, *args, name):
+def call(kernel, sz, outs, scratch, *args, name, cost=None):
     held = sum(4 * math.prod(shape) for shape in scratch)
     held += sum(4 * math.prod(array.shape) for array in jax.tree.leaves((outs, args)))
     return pl.pallas_call(
@@ -492,6 +527,19 @@
         out_shape=outs,
         scratch_shapes=[pltpu.VMEM(shape, jnp.float32) for shape in scratch],
         compiler_params=pltpu.CompilerParams(vmem_limit_bytes=held + SPARE_BYTES),
+        cost_estimate=cost,
+        name=name,
+    )(*args)
+
+
+def windows(kernel, sz, out, columns, *args, name):
+    return pl.pallas_call(
+        functools.partial(kernel, sz),
+        out_shape=out,
+        in_specs=[pl.BlockSpec(memory_space=pltpu.HBM)] * len(args),
+        scratch_shapes=[pltpu.VMEM(array.shape, array.dtype) for array in args]
+        + [pltpu.VMEM(columns, jnp.float32), pltpu.SemaphoreType.DMA((len(args),))],
+        compiler_params=pltpu.CompilerParams(vmem_limit_bytes=60 * 1024 * 1024),
         name=name,
     )(*args)
 
@@ -512,18 +560,28 @@
     spans, space = lax.axis_size("tm"), lax.axis_size("space")
     sz = Sizes(spans, space, *diff_x.shape)
     nx, ny = sz.nx, sz.ny
-    inputs = (start_states, diff_x, diff_y, diff_z, stress, trap_class, cotangent)
-    coef, both = pl.pallas_call(
-        functools.partial(windows_kernel, sz),
-        out_shape=(f32(space, 4 * sz.planes * sz.quarter, LANES), f32(space, (sz.start_tiles + sz.cot_tiles) * SUB, LANES)),
-        in_specs=[pl.BlockSpec(memory_space=pltpu.HBM)] * len(inputs),
-        scratch_shapes=[pltpu.VMEM((4, sz.planes, sz.nz // LANES, ny, LANES), jnp.float32)]
-        + [pltpu.VMEM(array.shape, array.dtype) for array in inputs]
-        + [pltpu.SemaphoreType.DMA((len(inputs),))]
-        + [pltpu.VMEM((2, sz.planes, sz.nz // LANES, ny, LANES), jnp.float32)],
-        compiler_params=pltpu.CompilerParams(vmem_limit_bytes=60 * 1024 * 1024),
-        name="windows",
-    )(*inputs)
+    columns = (sz.planes, sz.nz // LANES, ny, LANES)
+    coef = windows(
+        face_windows_kernel,
+        sz,
+        f32(space, 4 * sz.planes * sz.quarter, LANES),
+        (4,) + columns,
+        diff_x,
+        diff_y,
+        diff_z,
+        stress,
+        trap_class,
+        name="face_windows",
+    )
+    both = windows(
+        field_windows_kernel,
+        sz,
+        f32(space, (sz.start_tiles + sz.cot_tiles) * SUB, LANES),
+        (2,) + columns,
+        start_states,
+        cotangent,
+        name="field_windows",
+    )
     coef = lax.all_to_all(coef, "space", 0, 0)
     both = lax.all_to_all(both, "space", 0, 0)
 
@@ -544,20 +602,30 @@
         return front + (count, SUB, LANES)
 
     both, rough = lax.optimization_barrier((both, rough))
+    coefs, scales = call(
+        factors_kernel,
+        sz,
+        (f32(*field(tiles, 6, nx)), f32(*field(tiles, 2, nx))),
+        (field(tiles, 4, nx),),
+        *pieces,
+        name="factors",
+        cost=pl.CostEstimate(flops=40 * nx * ny * LANES, bytes_accessed=12 * 4 * nx * ny * LANES, transcendentals=0),
+    )
     end, rough_end, grads = call(
         fine_kernel,
         sz,
         (f32(*field(tiles, nx)), rough_shape, f32(spans, space, sz.grad_rows, LANES)),
         (
-            field(tiles, 4, nx),
-            field(tiles, 6, nx),
+            field(tiles, 3, nx),
             field(tiles + 2, nx),
             field(tiles + 2, nx),
-            field(tiles, nx),
+            field(tiles + 2, nx),
+            field(tiles + 2, nx),
             field(tiles + 1, TOTAL + 1, nx + 1),
             field(tiles + 1, TOTAL, nx + 1),
         ),
-        *pieces,
+        coefs,
+        scales,
         both,
         name="fine",
     )
@@ -581,6 +649,7 @@
             field(tiles, 4, nx),
             field(tiles // 2, 4, nx),
             field(tiles // 2, 6, nx),
+            field(tiles // 2, 2, nx),
             field(tiles // 2 + 2, nx),
             field(tiles // 2 + 2, nx),
             field(tiles // 2, nx),

time: 108 us -> 106 us (0.981)
  blocking collectives: 45.7 us -> 24.1 us
  waiting for transfers between devices: 23.6 us -> 36 us
  starting transfers between devices: 8.98 us -> 16.3 us
    all_to_all x1 -> x0, blocking collectives: 21.8 us -> none  [shards(): coef = lax.all_to_all(coef, 'space', 0, 0)]
    all_to_all x0 -> x1, waiting for transfers between devices: none -> 11.2 us  [shards(): coef = lax.all_to_all(coef, 'space', 0, 0)]
    all_to_all x0 -> x1, starting transfers between devices: none -> 7.29 us  [shards(): coef = lax.all_to_all(coef, 'space', 0, 0)]
    pallas_call x1 -> x2, Pallas kernels: 4.01 us -> 5.72 us  [windows(): pl.pallas_call(functools.partial(kernel, sz), out_shape=out, in_specs=[pl...]
    pallas_call x5 -> x6, Pallas kernels: 24.7 us -> 23.1 us  [call(): pl.pallas_call(functools.partial(kernel, sz), out_shape=outs, scratch_sha...]
    ppermute x5, waiting for transfers between devices: 13.8 us -> 15.3 us  [exchange(): return lax.ppermute(values, axis, [(i, i ^ bit) for i in range(size)])]
  transfers between devices with their start and end apart: 7 -> 8, of which waited for: 3 -> 4; matrix products, arithmetic and copies ran while one was open for 0% -> 0% of each run, Pallas kernels for 22% -> 24%
where the time goes in v4:
time: 106 us
  waiting for transfers between devices  36 us (34%)
  Pallas kernels  28.8 us (27%)
  blocking collectives  24.1 us (23%)
  starting transfers between devices  16.3 us (15%)
    pallas_call x6, Pallas kernels, call(): pl.pallas_call(functools.partial(kernel, sz), out_shape=outs, scratch_sha...  23.1 us
    all_to_all x1, blocking collectives, shards(): joined = lax.all_to_all(joined, 'space', 0, 0)  16.9 us
    ppermute x5, waiting for transfers between devices, exchange(): return lax.ppermute(values, axis, [(i, i ^ bit) for i in range(size)])  15.3 us
    all_to_all x1, waiting for transfers between devices, shards(): coef = lax.all_to_all(coef, 'space', 0, 0)  11.2 us
    all_to_all x1, waiting for transfers between devices, shards(): both = lax.all_to_all(both, 'space', 0, 0)  9.57 us
    all_to_all x1, starting transfers between devices, shards(): coef = lax.all_to_all(coef, 'space', 0, 0)  7.29 us
    all_gather x1, blocking collectives, shards(): jumps = lax.all_gather(jumps, 'tm', axis=0)  7.17 us
    pallas_call x2, Pallas kernels, windows(): pl.pallas_call(functools.partial(kernel, sz), out_shape=out, in_specs=[pl...  5.72 us
  transfers between devices with their start and end apart: 8, of which 4 were waited for; matrix products, arithmetic and copies ran while one was open for 0% of the time, Pallas kernels for 24%

profile of v4, /device:TPU:0, one launch (start us, length us, event | category | flops | bytes accessed | tf_op | source)
XLA Modules:
  0.0 106.1 jit_solution(12894907315719736741)
XLA Ops:
  0.6 2.4 %face_windows.1 = f32[8,128,128]{2,1,0:T(8,128)} custom-call(f32[2,64,512]{2,1,0:T(8,128)} %refs_0_.2, f32[2,64,512]{2,1,0:T(8,128)} %refs_1_.2, f32[2,64,512]{2,1,0:T(8,128)} %refs_2_.1, f32[2,64,512]{2,1,0:T(8,128)} %refs_3_.1, s32[2,64,512]{2,1,0:T(8,128)} %refs_4_.1), custom_call_target="tpu_custom_call" | custom-call | tf_op jit(solution)/shard_map/face_windows/pallas_call | solution.py:536
  3.0 7.3 %all-to-all-start = ((f32[8,128,128]{2,1,0:T(8,128)}), f32[8,128,128]{2,1,0:T(8,128)S(1)}, u32[]{:S(2)}, u32[]{:S(2)}) async-start(f32[8,128,128]{2,1,0:T(8,128)} %face_windows.1), calls=%async_computation | async-start | bytes 1048576 | tf_op jit(solution)/shard_map/all_to_all | solution.py:585
  10.3 3.3 %field_windows.1 = f32[8,224,128]{2,1,0:T(8,128)} custom-call(f32[1,2,64,512]{3,2,1,0:T(8,128)} %refs_0_.3, f32[1,2,64,512]{3,2,1,0:T(8,128)} %refs_1_.3), custom_call_target="tpu_custom_call" | custom-call | tf_op jit(solution)/shard_map/field_windows/pallas_call | solution.py:536
  13.7 11.2 %all-to-all-done.refs_0_ = f32[8,128,128]{2,1,0:T(8,128)S(1)} async-done(((f32[8,128,128]{2,1,0:T(8,128)}), f32[8,128,128]{2,1,0:T(8,128)S(1)}, u32[]{:S(2)}, u32[]{:S(2)}) %all-to-all-start) | async-done | bytes 524320 | tf_op jit(solution)/shard_map/all_to_all | solution.py:585
  24.8 3.6 %all-to-all-start.1 = ((f32[8,224,128]{2,1,0:T(8,128)}), f32[8,224,128]{2,1,0:T(8,128)S(1)}, u32[]{:S(2)}, u32[]{:S(2)}) async-start(f32[8,224,128]{2,1,0:T(8,128)} %field_windows.1), calls=%async_computation.1 | async-start | bytes 1835008 | tf_op jit(solution)/shard_map/all_to_all | solution.py:586
  28.5 1.5 %collective-permute-start.1 = (f32[8,128,128]{2,1,0:T(8,128)S(1)}, f32[8,128,128]{2,1,0:T(8,128)S(1)}, u32[]{:S(2)}, u32[]{:S(2)}) collective-permute-start(f32[8,128,128]{2,1,0:T(8,128)S(1)} %all-to-all-done.refs_0_), channel_id=1, source_target_pairs={{0,16},{8,24},{16,0},{24,8},{1,17},{9,25},{17,1},{25,9},{2,18},{10... | collective-permute-start | bytes 1572872 | tf_op jit(solution)/shard_map/ppermute | solution.py:556
  30.0 0.0 collective-permute-start
  30.0 12.0 %collective-permute-done.1.refs_2_ = f32[8,128,128]{2,1,0:T(8,128)S(1)} collective-permute-done((f32[8,128,128]{2,1,0:T(8,128)S(1)}, f32[8,128,128]{2,1,0:T(8,128)S(1)}, u32[]{:S(2)}, u32[]{:S(2)}) %collective-permute-start.1) | collective-permute-done | bytes 524320 | tf_op jit(solution)/shard_map/ppermute | solution.py:556
  42.0 0.0 collective-permute-start.2
  42.0 9.6 %all-to-all-done.1.start_ref.refs_2_ = f32[8,224,128]{2,1,0:T(8,128)S(1)} async-done(((f32[8,224,128]{2,1,0:T(8,128)}), f32[8,224,128]{2,1,0:T(8,128)S(1)}, u32[]{:S(2)}, u32[]{:S(2)}) %all-to-all-start.1) | async-done | bytes 917536 | tf_op jit(solution)/shard_map/all_to_all | solution.py:586
  51.6 0.2 rough.1
  51.8 1.3 %collective-permute-start.4 = (f32[16,2,8,128]{3,2,1,0:T(8,128)S(1)}, f32[16,2,8,128]{3,2,1,0:T(8,128)S(1)}, u32[]{:S(2)}, u32[]{:S(2)}) collective-permute-start(f32[16,2,8,128]{3,2,1,0:T(8,128)S(1)} %rough.1), channel_id=1, source_target_pairs={{8,0},{16,8},{24,16},{9,1},{17,9},{25,17},{10,2},{18,10},{26,18},{... | collective-permute-start | bytes 393224 | tf_op jit(solution)/shard_map/ppermute | solution.py:599
  53.1 0.0 collective-permute-done.refs_1_
  53.1 0.0 collective-permute-done.2.refs_3_
  53.1 0.8 factors.1
  54.0 18.5 %fine.1 = (f32[16,8,8,128]{3,2,1,0:T(8,128)S(1)}, f32[16,2,8,128]{3,2,1,0:T(8,128)S(1)}, f32[4,8,48,128]{3,2,1,0:T(8,128)S(1)}) custom-call(f32[6,16,8,8,128]{4,3,2,1,0:T(8,128)S(1)} %get-tuple-element.18.refs_0_, f32[2,16,8,8,128]{4,3,2,1,0:T(8,128)S(1)} %get-tuple-element.19.refs_1_, f32[8,224,128]{2,1,0:T(8,128)S(1)} %all-to-all-done.1.start_ref.refs_2_), custom_call_target="tpu_custom_call" | custom-call | tf_op jit(solution)/shard_map/fine/pallas_call | solution.py:525
  72.5 1.2 %collective-permute-start.3 = (f32[2,8,48,128]{3,2,1,0:T(8,128)S(1)}, f32[2,8,48,128]{3,2,1,0:T(8,128)S(1)}, u32[]{:S(2)}, u32[]{:S(2)}) collective-permute-start(f32[2,8,48,128]{3,2,1,0:T(8,128)S(1)} %slice.13), channel_id=1, source_target_pairs={{0,8},{8,0},{16,24},{24,16},{1,9},{9,1},{17,25},{25,17},{2,10},{10... | collective-permute-start | bytes 1179656 | tf_op jit(solution)/shard_map/ppermute | solution.py:556
  73.7 0.0 collective-permute-done.4
  73.7 7.2 %all-gather = f32[64,2,8,128]{3,2,1,0:T(8,128)S(1)} all-gather(f32[16,2,8,128]{3,2,1,0:T(8,128)S(1)} %subtract_select_fusion), channel_id=2, replica_groups=mesh['tm'=4,'space'=8] {'tm'}, dimensions={0}, use_global_device_ids=true | all-gather | bytes 655360 | tf_op jit(solution)/shard_map/all_gather | solution.py:633
  80.9 1.4 %collective-permute-start.5 = (f32[1,8,48,128]{3,2,1,0:T(8,128)S(1)}, f32[1,8,48,128]{3,2,1,0:T(8,128)S(1)}, u32[]{:S(2)}, u32[]{:S(2)}) collective-permute-start(f32[1,8,48,128]{3,2,1,0:T(8,128)S(1)} %get-tuple-element.31), channel_id=1, source_target_pairs={{0,16},{8,24},{16,0},{24,8},{1,17},{9,25},{17,1},{25,9},{2,18},{10... | collective-permute-start | bytes 589832 | tf_op jit(solution)/shard_map/ppermute | solution.py:556
  82.3 2.6 %coarse.1.ends_ref = f32[8,72,128]{2,1,0:T(8,128)S(1)} custom-call(f32[8,128,128]{2,1,0:T(8,128)S(1)} %all-to-all-done.refs_0_, f32[8,128,128]{2,1,0:T(8,128)S(1)} %collective-permute-done.refs_1_, f32[8,128,128]{2,1,0:T(8,128)S(1)} %collective-permute-done.1.refs_2_, f32[8,128,128]{2,1,0:T(8,128)S(1)} %collective-permute-done.2.refs_3_, ...), custom_call_target="tpu_custom_call" | custom-call | tf_op jit(solution)/shard_map/coarse/pallas_call | solution.py:525
  84.9 3.2 %collective-permute-done.5.come_ref = f32[1,8,48,128]{3,2,1,0:T(8,128)S(1)} collective-permute-done((f32[1,8,48,128]{3,2,1,0:T(8,128)S(1)}, f32[1,8,48,128]{3,2,1,0:T(8,128)S(1)}, u32[]{:S(2)}, u32[]{:S(2)}) %collective-permute-start.5) | collective-permute-done | bytes 196640 | tf_op jit(solution)/shard_map/ppermute | solution.py:556
  88.2 16.9 %all_to_all.15.in_ref = f32[8,120,128]{2,1,0:T(8,128)S(1)} all-to-all(f32[8,120,128]{2,1,0:T(8,128)S(1)} %join.1), channel_id=1, replica_groups=mesh['tm'=4,'space'=8] {'space'}, dimensions={0} | all-to-all | bytes 983040 | tf_op jit(solution)/shard_map/all_to_all | solution.py:663
  105.1 1.0 unpack.1
  (6 shorter events, 0.2 us)
Async XLA Ops:
  3.0 21.8 %all-to-all-start = ((f32[8,128,128]{2,1,0:T(8,128)}), f32[8,128,128]{2,1,0:T(8,128)S(1)}, u32[]{:S(2)}, u32[]{:S(2)}) async-start(f32[8,128,128]{2,1,0:T(8,128)} %face_windows.1), calls=%async_computation | async-start | bytes 1048576 | tf_op jit(solution)/shard_map/all_to_all | solution.py:585
  24.8 26.8 %all-to-all-start.1 = ((f32[8,224,128]{2,1,0:T(8,128)}), f32[8,224,128]{2,1,0:T(8,128)S(1)}, u32[]{:S(2)}, u32[]{:S(2)}) async-start(f32[8,224,128]{2,1,0:T(8,128)} %field_windows.1), calls=%async_computation.1 | async-start | bytes 1835008 | tf_op jit(solution)/shard_map/all_to_all | solution.py:586
  28.5 13.6 %collective-permute-start.1 = (f32[8,128,128]{2,1,0:T(8,128)S(1)}, f32[8,128,128]{2,1,0:T(8,128)S(1)}, u32[]{:S(2)}, u32[]{:S(2)}) collective-permute-start(f32[8,128,128]{2,1,0:T(8,128)S(1)} %all-to-all-done.refs_0_), channel_id=1, source_target_pairs={{0,16},{8,24},{16,0},{24,8},{1,17},{9,25},{17,1},{25,9},{2,18},{10... | collective-permute-start | bytes 1572872 | tf_op jit(solution)/shard_map/ppermute | solution.py:556
  30.0 23.1 %collective-permute-start = (f32[8,128,128]{2,1,0:T(8,128)S(1)}, f32[8,128,128]{2,1,0:T(8,128)S(1)}, u32[]{:S(2)}, u32[]{:S(2)}) collective-permute-start(f32[8,128,128]{2,1,0:T(8,128)S(1)} %all-to-all-done.refs_0_), channel_id=1, source_target_pairs={{0,8},{8,0},{16,24},{24,16},{1,9},{9,1},{17,25},{25,17},{2,10},{10... | collective-permute-start | bytes 1572872 | tf_op jit(solution)/shard_map/ppermute | solution.py:556
  42.0 11.1 %collective-permute-start.2 = (f32[8,128,128]{2,1,0:T(8,128)S(1)}, f32[8,128,128]{2,1,0:T(8,128)S(1)}, u32[]{:S(2)}, u32[]{:S(2)}) collective-permute-start(f32[8,128,128]{2,1,0:T(8,128)S(1)} %collective-permute-done.1.refs_2_), channel_id=1, source_target_pairs={{0,8},{8,0},{16,24},{24,16},{1,9},{9,1},{17,25},{25,17},{2,10},{10... | collective-permute-start | bytes 1572872 | tf_op jit(solution)/shard_map/ppermute | solution.py:556
  51.8 21.9 %collective-permute-start.4 = (f32[16,2,8,128]{3,2,1,0:T(8,128)S(1)}, f32[16,2,8,128]{3,2,1,0:T(8,128)S(1)}, u32[]{:S(2)}, u32[]{:S(2)}) collective-permute-start(f32[16,2,8,128]{3,2,1,0:T(8,128)S(1)} %rough.1), channel_id=1, source_target_pairs={{8,0},{16,8},{24,16},{9,1},{17,9},{25,17},{10,2},{18,10},{26,18},{... | collective-permute-start | bytes 393224 | tf_op jit(solution)/shard_map/ppermute | solution.py:599
  72.5 8.4 %collective-permute-start.3 = (f32[2,8,48,128]{3,2,1,0:T(8,128)S(1)}, f32[2,8,48,128]{3,2,1,0:T(8,128)S(1)}, u32[]{:S(2)}, u32[]{:S(2)}) collective-permute-start(f32[2,8,48,128]{3,2,1,0:T(8,128)S(1)} %slice.13), channel_id=1, source_target_pairs={{0,8},{8,0},{16,24},{24,16},{1,9},{9,1},{17,25},{25,17},{2,10},{10... | collective-permute-start | bytes 1179656 | tf_op jit(solution)/shard_map/ppermute | solution.py:556
  80.9 7.2 %collective-permute-start.5 = (f32[1,8,48,128]{3,2,1,0:T(8,128)S(1)}, f32[1,8,48,128]{3,2,1,0:T(8,128)S(1)}, u32[]{:S(2)}, u32[]{:S(2)}) collective-permute-start(f32[1,8,48,128]{3,2,1,0:T(8,128)S(1)} %get-tuple-element.31), channel_id=1, source_target_pairs={{0,16},{8,24},{16,0},{24,8},{1,17},{9,25},{17,1},{25,9},{2,18},{10... | collective-permute-start | bytes 589832 | tf_op jit(solution)/shard_map/ppermute | solution.py:556

commit v5 on v4

--- a/solution.py
+++ b/solution.py
@@ -288,8 +288,8 @@
 
 
 def fine_kernel(sz, *refs):
-    coef, scale, field_ref, end_out, rough_out, grads_out = refs[:6]
-    sums, even, odd, back, forth, fields, weights = refs[6:]
+    coef, scale, field_ref, following_ref, end_out, jump_out, grads_out = refs[:7]
+    sums, even, odd, back, forth, fields, weights = refs[7:]
     nx, count = sz.nx, sz.tiles
     body = slice(1, count + 1)
     turn = lax.axis_index("tm")
@@ -357,10 +357,11 @@
                 store_plane(back, i, v, count)
                 keep_plane(weights, down - 1, i, v, count)
 
+    last = turn == sz.spans - 1
     for i in range(nx):
         end_out[i] = even[i, body]
         for m, rough in enumerate(pack_rough(sz, lambda t: even[i, 1 + t])):
-            rough_out[i, m] = rough
+            jump_out[i, m] = jnp.where(last, 0.0, rough - following_ref[i, m])
 
     def gather_sums(i, c):
         for t in range(count):
@@ -427,8 +428,8 @@
 
 def coarse_kernel(sz, *refs):
     pieces = refs[: sz.spans]
-    jumps_ref, end_ref, out_ref = refs[sz.spans : sz.spans + 3]
-    faces, rough, coef, scale, even, odd, source = refs[sz.spans + 3 :]
+    parts = refs[sz.spans : 2 * sz.spans]
+    end_ref, out_ref, faces, rough, coef, scale, even, odd, source, jumps = refs[2 * sz.spans :]
     nx, count = sz.nx, sz.tiles // 2
     body = slice(1, count + 1)
     turn = lax.axis_index("tm")
@@ -443,10 +444,12 @@
     lane = lane_of((SUB, LANES))
     mine = (lane >= sz.halo) & (lane < sz.halo + sz.own)
     square = jnp.zeros((SUB, LANES), jnp.float32)
-    for k in range(sz.spans - 1):
+    for key, part in enumerate(parts):
         for i in range(nx):
             for m in range(count // 2):
-                square = square + jumps_ref[k, i, m] * jumps_ref[k, i, m]
+                jump = part[i, m]
+                jumps[key, i, m] = jump
+                square = square + jump * jump
     square = jnp.where(mine, square, 0.0)
 
     for d in reversed(range(1, sz.spans)):
@@ -455,7 +458,7 @@
         for i in range(nx):
             jump = []
             for m in range(count // 2):
-                jump += unpacked(jnp.where(there, jumps_ref[which, i, m], 0.0))
+                jump += unpacked(jnp.where(there, jumps[turn ^ which, i, m], 0.0))
             v = jnp.stack(jump)
             if d < sz.spans - 1:
                 v = v + even[i, body]
@@ -554,6 +557,15 @@
 def exchange(values, axis, bit):
     size = lax.axis_size(axis)
     return lax.ppermute(values, axis, [(i, i ^ bit) for i in range(size)])
+
+
+def from_all(values, axis):
+    pieces, bit = {0: values}, lax.axis_size(axis) // 2
+    while bit:
+        for key, piece in list(pieces.items()):
+            pieces[key | bit] = exchange(piece, axis, bit)
+        bit //= 2
+    return [pieces[key] for key in range(len(pieces))]
 
 
 def shards(start_states, diff_x, diff_y, diff_z, stress, trap_class, cotangent):
@@ -585,13 +597,7 @@
     coef = lax.all_to_all(coef, "space", 0, 0)
     both = lax.all_to_all(both, "space", 0, 0)
 
-    pieces = {0: coef}
-    bit = spans // 2
-    while bit:
-        for key, piece in list(pieces.items()):
-            pieces[key | bit] = exchange(piece, "tm", bit)
-        bit //= 2
-    pieces = [pieces[key] for key in range(spans)]
+    pieces = from_all(coef, "tm")
 
     tiles = sz.tiles
     rough_shape = f32(nx, tiles // 4, SUB, LANES)
@@ -601,7 +607,6 @@
     def field(count, *front):
         return front + (count, SUB, LANES)
 
-    both, rough = lax.optimization_barrier((both, rough))
     coefs, scales = call(
         factors_kernel,
         sz,
@@ -611,7 +616,7 @@
         name="factors",
         cost=pl.CostEstimate(flops=40 * nx * ny * LANES, bytes_accessed=12 * 4 * nx * ny * LANES, transcendentals=0),
     )
-    end, rough_end, grads = call(
+    end, jumps, grads = call(
         fine_kernel,
         sz,
         (f32(*field(tiles, nx)), rough_shape, f32(spans, space, sz.grad_rows, LANES)),
@@ -627,17 +632,15 @@
         coefs,
         scales,
         both,
+        following,
         name="fine",
     )
-    jumps = jnp.where(lax.axis_index("tm") == spans - 1, 0.0, rough_end - following)
-    jumps = lax.all_gather(jumps, "tm", axis=0)
+    jumps = from_all(jumps, "tm")
 
     half, bit = spans // 2, 1
     while half:
         come = exchange(grads[half:], "tm", bit)
         kept = grads[:half]
-        if bit == 1:
-            come, jumps = lax.optimization_barrier((come, jumps))
         grads = kept + come if half > 1 else None
         half, bit = half // 2, bit * 2
 
@@ -653,9 +656,10 @@
             field(tiles // 2 + 2, nx),
             field(tiles // 2 + 2, nx),
             field(tiles // 2, nx),
+            field(tiles // 4, spans, nx),
         ),
         *pieces,
-        jumps,
+        *jumps,
         end,
         name="coarse",
     )

time: 106 us -> 106 us (level)
  blocking collectives: 24.1 us -> 17.6 us
  waiting for transfers between devices: 36 us -> 40.7 us
  starting transfers between devices: 16.3 us -> 17.5 us
    all_gather x1 -> x0, blocking collectives: 7.17 us -> none  [shards(): jumps = lax.all_gather(jumps, 'tm', axis=0)]
    ppermute x5 -> x8, waiting for transfers between devices: 15.3 us -> 18.9 us  [exchange(): return lax.ppermute(values, axis, [(i, i ^ bit) for i in range(size)])]
    ppermute x5 -> x8, starting transfers between devices: 4.07 us -> 5.26 us  [exchange(): return lax.ppermute(values, axis, [(i, i ^ bit) for i in range(size)])]
    ppermute x1, waiting for transfers between devices: 0.01 us -> 1.09 us  [shards(): lax.ppermute(rough, 'tm', [(i + 1, i) for i in range(spans - 1)])]
  transfers between devices with their start and end apart: 8 -> 11, of which waited for: 4 -> 7; matrix products, arithmetic and copies ran while one was open for 0% -> 0% of each run, Pallas kernels for 24% -> 7%
where the time goes in v5:
time: 106 us
  waiting for transfers between devices  40.7 us (38%)
  Pallas kernels  28.9 us (27%)
  blocking collectives  17.6 us (17%)
  starting transfers between devices  17.5 us (17%)
    pallas_call x6, Pallas kernels, call(): pl.pallas_call(functools.partial(kernel, sz), out_shape=outs, scratch_sha...  23.1 us
    ppermute x8, waiting for transfers between devices, exchange(): return lax.ppermute(values, axis, [(i, i ^ bit) for i in range(size)])  18.9 us
    all_to_all x1, blocking collectives, shards(): joined = lax.all_to_all(joined, 'space', 0, 0)  17.6 us
    all_to_all x1, waiting for transfers between devices, shards(): coef = lax.all_to_all(coef, 'space', 0, 0)  11.2 us
    all_to_all x1, waiting for transfers between devices, shards(): both = lax.all_to_all(both, 'space', 0, 0)  9.57 us
    all_to_all x1, starting transfers between devices, shards(): coef = lax.all_to_all(coef, 'space', 0, 0)  7.29 us
    pallas_call x2, Pallas kernels, windows(): pl.pallas_call(functools.partial(kernel, sz), out_shape=out, in_specs=[pl...  5.72 us
    ppermute x8, starting transfers between devices, exchange(): return lax.ppermute(values, axis, [(i, i ^ bit) for i in range(size)])  5.26 us
  transfers between devices with their start and end apart: 11, of which 7 were waited for; matrix products, arithmetic and copies ran while one was open for 0% of the time, Pallas kernels for 7%

profile of v5, /device:TPU:0, one launch (start us, length us, event | category | flops | bytes accessed | tf_op | source)
XLA Modules:
  0.0 105.5 jit_solution(477346343452180889)
XLA Ops:
  0.6 2.4 %face_windows.1 = f32[8,128,128]{2,1,0:T(8,128)} custom-call(f32[2,64,512]{2,1,0:T(8,128)} %refs_0_.2, f32[2,64,512]{2,1,0:T(8,128)} %refs_1_.2, f32[2,64,512]{2,1,0:T(8,128)} %refs_2_.1, f32[2,64,512]{2,1,0:T(8,128)} %refs_3_.1, s32[2,64,512]{2,1,0:T(8,128)} %refs_4_.1), custom_call_target="tpu_custom_call" | custom-call | tf_op jit(solution)/shard_map/face_windows/pallas_call | solution.py:539
  3.0 7.3 %all-to-all-start = ((f32[8,128,128]{2,1,0:T(8,128)}), f32[8,128,128]{2,1,0:T(8,128)S(1)}, u32[]{:S(2)}, u32[]{:S(2)}) async-start(f32[8,128,128]{2,1,0:T(8,128)} %face_windows.1), calls=%async_computation | async-start | bytes 1048576 | tf_op jit(solution)/shard_map/all_to_all | solution.py:597
  10.3 3.3 %field_windows.1 = f32[8,224,128]{2,1,0:T(8,128)} custom-call(f32[1,2,64,512]{3,2,1,0:T(8,128)} %refs_0_.3, f32[1,2,64,512]{3,2,1,0:T(8,128)} %refs_1_.3), custom_call_target="tpu_custom_call" | custom-call | tf_op jit(solution)/shard_map/field_windows/pallas_call | solution.py:539
  13.7 11.2 %all-to-all-done.refs_0_ = f32[8,128,128]{2,1,0:T(8,128)S(1)} async-done(((f32[8,128,128]{2,1,0:T(8,128)}), f32[8,128,128]{2,1,0:T(8,128)S(1)}, u32[]{:S(2)}, u32[]{:S(2)}) %all-to-all-start) | async-done | bytes 524320 | tf_op jit(solution)/shard_map/all_to_all | solution.py:597
  24.8 3.6 %all-to-all-start.1 = ((f32[8,224,128]{2,1,0:T(8,128)}), f32[8,224,128]{2,1,0:T(8,128)S(1)}, u32[]{:S(2)}, u32[]{:S(2)}) async-start(f32[8,224,128]{2,1,0:T(8,128)} %field_windows.1), calls=%async_computation.1 | async-start | bytes 1835008 | tf_op jit(solution)/shard_map/all_to_all | solution.py:598
  28.5 1.5 %collective-permute-start.1 = (f32[8,128,128]{2,1,0:T(8,128)S(1)}, f32[8,128,128]{2,1,0:T(8,128)S(1)}, u32[]{:S(2)}, u32[]{:S(2)}) collective-permute-start(f32[8,128,128]{2,1,0:T(8,128)S(1)} %all-to-all-done.refs_0_), channel_id=1, source_target_pairs={{0,16},{8,24},{16,0},{24,8},{1,17},{9,25},{17,1},{25,9},{2,18},{10... | collective-permute-start | bytes 1572872 | tf_op jit(solution)/shard_map/ppermute | solution.py:559
  30.0 0.0 collective-permute-start
  30.0 12.0 %collective-permute-done.1.refs_2_ = f32[8,128,128]{2,1,0:T(8,128)S(1)} collective-permute-done((f32[8,128,128]{2,1,0:T(8,128)S(1)}, f32[8,128,128]{2,1,0:T(8,128)S(1)}, u32[]{:S(2)}, u32[]{:S(2)}) %collective-permute-start.1) | collective-permute-done | bytes 524320 | tf_op jit(solution)/shard_map/ppermute | solution.py:559
  42.0 0.0 collective-permute-start.2
  42.0 9.6 %all-to-all-done.1.start_ref.refs_2_ = f32[8,224,128]{2,1,0:T(8,128)S(1)} async-done(((f32[8,224,128]{2,1,0:T(8,128)}), f32[8,224,128]{2,1,0:T(8,128)S(1)}, u32[]{:S(2)}, u32[]{:S(2)}) %all-to-all-start.1) | async-done | bytes 917536 | tf_op jit(solution)/shard_map/all_to_all | solution.py:598
  51.6 0.2 rough.1
  51.8 1.3 %collective-permute-start.3 = (f32[16,2,8,128]{3,2,1,0:T(8,128)S(1)}, f32[16,2,8,128]{3,2,1,0:T(8,128)S(1)}, u32[]{:S(2)}, u32[]{:S(2)}) collective-permute-start(f32[16,2,8,128]{3,2,1,0:T(8,128)S(1)} %rough.1), channel_id=1, source_target_pairs={{8,0},{16,8},{24,16},{9,1},{17,9},{25,17},{10,2},{18,10},{26,18},{... | collective-permute-start | bytes 393224 | tf_op jit(solution)/shard_map/ppermute | solution.py:605
  53.1 0.0 collective-permute-done.refs_1_
  53.1 0.8 factors.1
  54.0 1.1 %collective-permute-done.3.refs_3_ = f32[16,2,8,128]{3,2,1,0:T(8,128)S(1)} collective-permute-done((f32[16,2,8,128]{3,2,1,0:T(8,128)S(1)}, f32[16,2,8,128]{3,2,1,0:T(8,128)S(1)}, u32[]{:S(2)}, u32[]{:S(2)}) %collective-permute-start.3) | collective-permute-done | bytes 131104 | tf_op jit(solution)/shard_map/ppermute | solution.py:605
  55.1 18.5 %fine.1 = (f32[16,8,8,128]{3,2,1,0:T(8,128)S(1)}, f32[16,2,8,128]{3,2,1,0:T(8,128)S(1)}, f32[4,8,48,128]{3,2,1,0:T(8,128)S(1)}) custom-call(f32[6,16,8,8,128]{4,3,2,1,0:T(8,128)S(1)} %get-tuple-element.15.refs_0_, f32[2,16,8,8,128]{4,3,2,1,0:T(8,128)S(1)} %get-tuple-element.16.refs_1_, f32[8,224,128]{2,1,0:T(8,128)S(1)} %all-to-all-done.1.start_ref.refs_2_, ...), custom_call_target="tpu_custom_call" | custom-call | tf_op jit(solution)/shard_map/fine/pallas_call | solution.py:528
  73.6 3.0 %collective-permute-start.4 = (f32[2,8,48,128]{3,2,1,0:T(8,128)S(1)}, f32[2,8,48,128]{3,2,1,0:T(8,128)S(1)}, u32[]{:S(2)}, u32[]{:S(2)}) collective-permute-start(f32[2,8,48,128]{3,2,1,0:T(8,128)S(1)} %slice.13), channel_id=1, source_target_pairs={{0,8},{8,0},{16,24},{24,16},{1,9},{9,1},{17,25},{25,17},{2,10},{10... | collective-permute-start | bytes 1179656 | tf_op jit(solution)/shard_map/ppermute | solution.py:559
  76.5 1.3 %collective-permute-done.4 = f32[2,8,48,128]{3,2,1,0:T(8,128)S(1)} collective-permute-done((f32[2,8,48,128]{3,2,1,0:T(8,128)S(1)}, f32[2,8,48,128]{3,2,1,0:T(8,128)S(1)}, u32[]{:S(2)}, u32[]{:S(2)}) %collective-permute-start.4) | collective-permute-done | bytes 393248 | tf_op jit(solution)/shard_map/ppermute | solution.py:559
  78.0 0.7 collective-permute-start.5
  78.7 4.2 %collective-permute-done.7.refs_6_ = f32[16,2,8,128]{3,2,1,0:T(8,128)S(1)} collective-permute-done((f32[16,2,8,128]{3,2,1,0:T(8,128)S(1)}, f32[16,2,8,128]{3,2,1,0:T(8,128)S(1)}, u32[]{:S(2)}, u32[]{:S(2)}) %collective-permute-start.7) | collective-permute-done | bytes 131104 | tf_op jit(solution)/shard_map/ppermute | solution.py:559
  82.9 1.3 %collective-permute-done.8.refs_7_ = f32[16,2,8,128]{3,2,1,0:T(8,128)S(1)} collective-permute-done((f32[16,2,8,128]{3,2,1,0:T(8,128)S(1)}, f32[16,2,8,128]{3,2,1,0:T(8,128)S(1)}, u32[]{:S(2)}, u32[]{:S(2)}) %collective-permute-start.8) | collective-permute-done | bytes 131104 | tf_op jit(solution)/shard_map/ppermute | solution.py:559
  84.2 2.6 %coarse.1.ends_ref = f32[8,72,128]{2,1,0:T(8,128)S(1)} custom-call(f32[8,128,128]{2,1,0:T(8,128)S(1)} %all-to-all-done.refs_0_, f32[8,128,128]{2,1,0:T(8,128)S(1)} %collective-permute-done.refs_1_, f32[8,128,128]{2,1,0:T(8,128)S(1)} %collective-permute-done.1.refs_2_, f32[8,128,128]{2,1,0:T(8,128)S(1)} %collective-permute-done.2.refs_3_, ...), custom_call_target="tpu_custom_call" | custom-call | tf_op jit(solution)/shard_map/coarse/pallas_call | solution.py:528
  86.9 17.6 %all_to_all.15.in_ref = f32[8,120,128]{2,1,0:T(8,128)S(1)} all-to-all(f32[8,120,128]{2,1,0:T(8,128)S(1)} %join.1), channel_id=1, replica_groups=mesh['tm'=4,'space'=8] {'space'}, dimensions={0} | all-to-all | bytes 983040 | tf_op jit(solution)/shard_map/all_to_all | solution.py:667
  104.6 1.0 unpack.1
  (10 shorter events, 0.2 us)
Async XLA Ops:
  3.0 21.8 %all-to-all-start = ((f32[8,128,128]{2,1,0:T(8,128)}), f32[8,128,128]{2,1,0:T(8,128)S(1)}, u32[]{:S(2)}, u32[]{:S(2)}) async-start(f32[8,128,128]{2,1,0:T(8,128)} %face_windows.1), calls=%async_computation | async-start | bytes 1048576 | tf_op jit(solution)/shard_map/all_to_all | solution.py:597
  24.8 26.8 %all-to-all-start.1 = ((f32[8,224,128]{2,1,0:T(8,128)}), f32[8,224,128]{2,1,0:T(8,128)S(1)}, u32[]{:S(2)}, u32[]{:S(2)}) async-start(f32[8,224,128]{2,1,0:T(8,128)} %field_windows.1), calls=%async_computation.1 | async-start | bytes 1835008 | tf_op jit(solution)/shard_map/all_to_all | solution.py:598
  28.5 13.6 %collective-permute-start.1 = (f32[8,128,128]{2,1,0:T(8,128)S(1)}, f32[8,128,128]{2,1,0:T(8,128)S(1)}, u32[]{:S(2)}, u32[]{:S(2)}) collective-permute-start(f32[8,128,128]{2,1,0:T(8,128)S(1)} %all-to-all-done.refs_0_), channel_id=1, source_target_pairs={{0,16},{8,24},{16,0},{24,8},{1,17},{9,25},{17,1},{25,9},{2,18},{10... | collective-permute-start | bytes 1572872 | tf_op jit(solution)/shard_map/ppermute | solution.py:559
  30.0 23.1 %collective-permute-start = (f32[8,128,128]{2,1,0:T(8,128)S(1)}, f32[8,128,128]{2,1,0:T(8,128)S(1)}, u32[]{:S(2)}, u32[]{:S(2)}) collective-permute-start(f32[8,128,128]{2,1,0:T(8,128)S(1)} %all-to-all-done.refs_0_), channel_id=1, source_target_pairs={{0,8},{8,0},{16,24},{24,16},{1,9},{9,1},{17,25},{25,17},{2,10},{10... | collective-permute-start | bytes 1572872 | tf_op jit(solution)/shard_map/ppermute | solution.py:559
  42.0 11.1 %collective-permute-start.2 = (f32[8,128,128]{2,1,0:T(8,128)S(1)}, f32[8,128,128]{2,1,0:T(8,128)S(1)}, u32[]{:S(2)}, u32[]{:S(2)}) collective-permute-start(f32[8,128,128]{2,1,0:T(8,128)S(1)} %collective-permute-done.1.refs_2_), channel_id=1, source_target_pairs={{0,8},{8,0},{16,24},{24,16},{1,9},{9,1},{17,25},{25,17},{2,10},{10... | collective-permute-start | bytes 1572872 | tf_op jit(solution)/shard_map/ppermute | solution.py:559
  51.8 3.2 %collective-permute-start.3 = (f32[16,2,8,128]{3,2,1,0:T(8,128)S(1)}, f32[16,2,8,128]{3,2,1,0:T(8,128)S(1)}, u32[]{:S(2)}, u32[]{:S(2)}) collective-permute-start(f32[16,2,8,128]{3,2,1,0:T(8,128)S(1)} %rough.1), channel_id=1, source_target_pairs={{8,0},{16,8},{24,16},{9,1},{17,9},{25,17},{10,2},{18,10},{26,18},{... | collective-permute-start | bytes 393224 | tf_op jit(solution)/shard_map/ppermute | solution.py:605
  73.6 4.3 %collective-permute-start.4 = (f32[2,8,48,128]{3,2,1,0:T(8,128)S(1)}, f32[2,8,48,128]{3,2,1,0:T(8,128)S(1)}, u32[]{:S(2)}, u32[]{:S(2)}) collective-permute-start(f32[2,8,48,128]{3,2,1,0:T(8,128)S(1)} %slice.13), channel_id=1, source_target_pairs={{0,8},{8,0},{16,24},{24,16},{1,9},{9,1},{17,25},{25,17},{2,10},{10... | collective-permute-start | bytes 1179656 | tf_op jit(solution)/shard_map/ppermute | solution.py:559
  76.5 6.4 %collective-permute-start.7 = (f32[16,2,8,128]{3,2,1,0:T(8,128)S(1)}, f32[16,2,8,128]{3,2,1,0:T(8,128)S(1)}, u32[]{:S(2)}, u32[]{:S(2)}) collective-permute-start(f32[16,2,8,128]{3,2,1,0:T(8,128)S(1)} %get-tuple-element.18.refs_4_), channel_id=1, source_target_pairs={{0,16},{8,24},{16,0},{24,8},{1,17},{9,25},{17,1},{25,9},{2,18},{10... | collective-permute-start | bytes 393224 | tf_op jit(solution)/shard_map/ppermute | solution.py:559
  78.0 8.9 %collective-permute-start.5 = (f32[1,8,48,128]{3,2,1,0:T(8,128)S(1)}, f32[1,8,48,128]{3,2,1,0:T(8,128)S(1)}, u32[]{:S(2)}, u32[]{:S(2)}) collective-permute-start(f32[1,8,48,128]{3,2,1,0:T(8,128)S(1)} %get-tuple-element.25), channel_id=1, source_target_pairs={{0,16},{8,24},{16,0},{24,8},{1,17},{9,25},{17,1},{25,9},{2,18},{10... | collective-permute-start | bytes 589832 | tf_op jit(solution)/shard_map/ppermute | solution.py:559
  78.7 4.2 %collective-permute-start.6 = (f32[16,2,8,128]{3,2,1,0:T(8,128)S(1)}, f32[16,2,8,128]{3,2,1,0:T(8,128)S(1)}, u32[]{:S(2)}, u32[]{:S(2)}) collective-permute-start(f32[16,2,8,128]{3,2,1,0:T(8,128)S(1)} %get-tuple-element.18.refs_4_), channel_id=1, source_target_pairs={{0,8},{8,0},{16,24},{24,16},{1,9},{9,1},{17,25},{25,17},{2,10},{10... | collective-permute-start | bytes 393224 | tf_op jit(solution)/shard_map/ppermute | solution.py:559
  82.9 1.3 %collective-permute-start.8 = (f32[16,2,8,128]{3,2,1,0:T(8,128)S(1)}, f32[16,2,8,128]{3,2,1,0:T(8,128)S(1)}, u32[]{:S(2)}, u32[]{:S(2)}) collective-permute-start(f32[16,2,8,128]{3,2,1,0:T(8,128)S(1)} %collective-permute-done.7.refs_6_), channel_id=1, source_target_pairs={{0,8},{8,0},{16,24},{24,16},{1,9},{9,1},{17,25},{25,17},{2,10},{10... | collective-permute-start | bytes 393224 | tf_op jit(solution)/shard_map/ppermute | solution.py:559

commit v6 on v5

--- a/solution.py
+++ b/solution.py
@@ -426,13 +426,10 @@
             out_ref[i, m] = rough
 
 
-def coarse_kernel(sz, *refs):
+def coarse_factors_kernel(sz, *refs):
     pieces = refs[: sz.spans]
-    parts = refs[sz.spans : 2 * sz.spans]
-    end_ref, out_ref, faces, rough, coef, scale, even, odd, source, jumps = refs[2 * sz.spans :]
+    coef, scale, faces, rough = refs[sz.spans :]
     nx, count = sz.nx, sz.tiles // 2
-    body = slice(1, count + 1)
-    turn = lax.axis_index("tm")
     lay_out_faces(sz, pieces, faces)
     for i in range(nx):
         for f, part in enumerate((1.0, 0.25, 0.25, 1.0)):
@@ -440,6 +437,15 @@
                 v = coarse_rows(lambda t: faces[f, i, t], m)
                 rough[f, i, m] = v if part == 1.0 else part * v
     normalise(sz, rough, coef, scale, count, COARSE_STEP, 2)
+
+
+def coarse_kernel(sz, *refs):
+    coef, scale = refs[:2]
+    parts = refs[2 : 2 + sz.spans]
+    end_ref, out_ref, even, odd, source, jumps = refs[2 + sz.spans :]
+    nx, count = sz.nx, sz.tiles // 2
+    body = slice(1, count + 1)
+    turn = lax.axis_index("tm")
 
     lane = lane_of((SUB, LANES))
     mine = (lane >= sz.halo) & (lane < sz.halo + sz.own)
@@ -644,21 +650,27 @@
         grads = kept + come if half > 1 else None
         half, bit = half // 2, bit * 2
 
+    half_tiles = tiles // 2
+    coarse_coefs, coarse_scales = call(
+        coarse_factors_kernel,
+        sz,
+        (f32(*field(half_tiles, 6, nx)), f32(*field(half_tiles, 2, nx))),
+        (field(tiles, 4, nx), field(half_tiles, 4, nx)),
+        *pieces,
+        name="coarse_factors",
+    )
     ends = call(
         coarse_kernel,
         sz,
         f32(space, sz.end_rows + SUB, LANES),
         (
-            field(tiles, 4, nx),
-            field(tiles // 2, 4, nx),
-            field(tiles // 2, 6, nx),
-            field(tiles // 2, 2, nx),
-            field(tiles // 2 + 2, nx),
-            field(tiles // 2 + 2, nx),
-            field(tiles // 2, nx),
+            field(half_tiles + 2, nx),
+            field(half_tiles + 2, nx),
+            field(half_tiles, nx),
             field(tiles // 4, spans, nx),
         ),
-        *pieces,
+        coarse_coefs,
+        coarse_scales,
         *jumps,
         end,
         name="coarse",

time: 106 us -> 105 us (level)
    pallas_call x6 -> x7, Pallas kernels: 23.1 us -> 23.1 us  [call(): pl.pallas_call(functools.partial(kernel, sz), out_shape=outs, scratch_sha...]
where the time goes in v6:
time: 105 us
  waiting for transfers between devices  40.1 us (38%)
  Pallas kernels  28.9 us (28%)
  starting transfers between devices  17.5 us (17%)
  blocking collectives  17.4 us (17%)
    pallas_call x7, Pallas kernels, call(): pl.pallas_call(functools.partial(kernel, sz), out_shape=outs, scratch_sha...  23.1 us
    ppermute x8, waiting for transfers between devices, exchange(): return lax.ppermute(values, axis, [(i, i ^ bit) for i in range(size)])  18.2 us
    all_to_all x1, blocking collectives, shards(): joined = lax.all_to_all(joined, 'space', 0, 0)  17.4 us
    all_to_all x1, waiting for transfers between devices, shards(): coef = lax.all_to_all(coef, 'space', 0, 0)  11.2 us
    all_to_all x1, waiting for transfers between devices, shards(): both = lax.all_to_all(both, 'space', 0, 0)  9.57 us
    all_to_all x1, starting transfers between devices, shards(): coef = lax.all_to_all(coef, 'space', 0, 0)  7.29 us
    pallas_call x2, Pallas kernels, windows(): pl.pallas_call(functools.partial(kernel, sz), out_shape=out, in_specs=[pl...  5.73 us
    ppermute x8, starting transfers between devices, exchange(): return lax.ppermute(values, axis, [(i, i ^ bit) for i in range(size)])  5.26 us
  transfers between devices with their start and end apart: 11, of which 7 were waited for; matrix products, arithmetic and copies ran while one was open for 0% of the time, Pallas kernels for 7%

profile of v6, /device:TPU:0, one launch (start us, length us, event | category | flops | bytes accessed | tf_op | source)
XLA Modules:
  0.0 104.6 jit_solution(13655381903271583887)
XLA Ops:
  0.6 2.4 %face_windows.1 = f32[8,128,128]{2,1,0:T(8,128)} custom-call(f32[2,64,512]{2,1,0:T(8,128)} %refs_0_.2, f32[2,64,512]{2,1,0:T(8,128)} %refs_1_.2, f32[2,64,512]{2,1,0:T(8,128)} %refs_2_.1, f32[2,64,512]{2,1,0:T(8,128)} %refs_3_.1, s32[2,64,512]{2,1,0:T(8,128)} %refs_4_.1), custom_call_target="tpu_custom_call" | custom-call | tf_op jit(solution)/shard_map/face_windows/pallas_call | solution.py:545
  3.1 7.3 %all-to-all-start = ((f32[8,128,128]{2,1,0:T(8,128)}), f32[8,128,128]{2,1,0:T(8,128)S(1)}, u32[]{:S(2)}, u32[]{:S(2)}) async-start(f32[8,128,128]{2,1,0:T(8,128)} %face_windows.1), calls=%async_computation | async-start | bytes 1048576 | tf_op jit(solution)/shard_map/all_to_all | solution.py:603
  10.3 3.3 %field_windows.1 = f32[8,224,128]{2,1,0:T(8,128)} custom-call(f32[1,2,64,512]{3,2,1,0:T(8,128)} %refs_0_.3, f32[1,2,64,512]{3,2,1,0:T(8,128)} %refs_1_.3), custom_call_target="tpu_custom_call" | custom-call | tf_op jit(solution)/shard_map/field_windows/pallas_call | solution.py:545
  13.7 11.2 %all-to-all-done.refs_0_ = f32[8,128,128]{2,1,0:T(8,128)S(1)} async-done(((f32[8,128,128]{2,1,0:T(8,128)}), f32[8,128,128]{2,1,0:T(8,128)S(1)}, u32[]{:S(2)}, u32[]{:S(2)}) %all-to-all-start) | async-done | bytes 524320 | tf_op jit(solution)/shard_map/all_to_all | solution.py:603
  24.8 3.6 %all-to-all-start.1 = ((f32[8,224,128]{2,1,0:T(8,128)}), f32[8,224,128]{2,1,0:T(8,128)S(1)}, u32[]{:S(2)}, u32[]{:S(2)}) async-start(f32[8,224,128]{2,1,0:T(8,128)} %field_windows.1), calls=%async_computation.1 | async-start | bytes 1835008 | tf_op jit(solution)/shard_map/all_to_all | solution.py:604
  28.5 1.5 %collective-permute-start.1 = (f32[8,128,128]{2,1,0:T(8,128)S(1)}, f32[8,128,128]{2,1,0:T(8,128)S(1)}, u32[]{:S(2)}, u32[]{:S(2)}) collective-permute-start(f32[8,128,128]{2,1,0:T(8,128)S(1)} %all-to-all-done.refs_0_), channel_id=1, source_target_pairs={{0,16},{8,24},{16,0},{24,8},{1,17},{9,25},{17,1},{25,9},{2,18},{10... | collective-permute-start | bytes 1572872 | tf_op jit(solution)/shard_map/ppermute | solution.py:565
  30.0 12.0 %collective-permute-done.1.refs_2_ = f32[8,128,128]{2,1,0:T(8,128)S(1)} collective-permute-done((f32[8,128,128]{2,1,0:T(8,128)S(1)}, f32[8,128,128]{2,1,0:T(8,128)S(1)}, u32[]{:S(2)}, u32[]{:S(2)}) %collective-permute-start.1) | collective-permute-done | bytes 524320 | tf_op jit(solution)/shard_map/ppermute | solution.py:565
  42.0 0.0 collective-permute-start.2
  42.0 9.6 %all-to-all-done.1.start_ref.refs_2_ = f32[8,224,128]{2,1,0:T(8,128)S(1)} async-done(((f32[8,224,128]{2,1,0:T(8,128)}), f32[8,224,128]{2,1,0:T(8,128)S(1)}, u32[]{:S(2)}, u32[]{:S(2)}) %all-to-all-start.1) | async-done | bytes 917536 | tf_op jit(solution)/shard_map/all_to_all | solution.py:604
  51.6 0.2 rough.1
  51.8 1.3 %collective-permute-start.3 = (f32[16,2,8,128]{3,2,1,0:T(8,128)S(1)}, f32[16,2,8,128]{3,2,1,0:T(8,128)S(1)}, u32[]{:S(2)}, u32[]{:S(2)}) collective-permute-start(f32[16,2,8,128]{3,2,1,0:T(8,128)S(1)} %rough.1), channel_id=1, source_target_pairs={{8,0},{16,8},{24,16},{9,1},{17,9},{25,17},{10,2},{18,10},{26,18},{... | collective-permute-start | bytes 393224 | tf_op jit(solution)/shard_map/ppermute | solution.py:611
  53.1 0.8 factors.1
  54.0 1.1 %collective-permute-done.3.refs_3_ = f32[16,2,8,128]{3,2,1,0:T(8,128)S(1)} collective-permute-done((f32[16,2,8,128]{3,2,1,0:T(8,128)S(1)}, f32[16,2,8,128]{3,2,1,0:T(8,128)S(1)}, u32[]{:S(2)}, u32[]{:S(2)}) %collective-permute-start.3) | collective-permute-done | bytes 131104 | tf_op jit(solution)/shard_map/ppermute | solution.py:611
  55.1 18.5 %fine.1 = (f32[16,8,8,128]{3,2,1,0:T(8,128)S(1)}, f32[16,2,8,128]{3,2,1,0:T(8,128)S(1)}, f32[4,8,48,128]{3,2,1,0:T(8,128)S(1)}) custom-call(f32[6,16,8,8,128]{4,3,2,1,0:T(8,128)S(1)} %get-tuple-element.17.refs_0_, f32[2,16,8,8,128]{4,3,2,1,0:T(8,128)S(1)} %get-tuple-element.18.refs_1_, f32[8,224,128]{2,1,0:T(8,128)S(1)} %all-to-all-done.1.start_ref.refs_2_, ...), custom_call_target="tpu_custom_call" | custom-call | tf_op jit(solution)/shard_map/fine/pallas_call | solution.py:534
  73.6 3.0 %collective-permute-start.4 = (f32[2,8,48,128]{3,2,1,0:T(8,128)S(1)}, f32[2,8,48,128]{3,2,1,0:T(8,128)S(1)}, u32[]{:S(2)}, u32[]{:S(2)}) collective-permute-start(f32[2,8,48,128]{3,2,1,0:T(8,128)S(1)} %slice.13), channel_id=1, source_target_pairs={{0,8},{8,0},{16,24},{24,16},{1,9},{9,1},{17,25},{25,17},{2,10},{10... | collective-permute-start | bytes 1179656 | tf_op jit(solution)/shard_map/ppermute | solution.py:565
  76.6 1.3 %collective-permute-done.4 = f32[2,8,48,128]{3,2,1,0:T(8,128)S(1)} collective-permute-done((f32[2,8,48,128]{3,2,1,0:T(8,128)S(1)}, f32[2,8,48,128]{3,2,1,0:T(8,128)S(1)}, u32[]{:S(2)}, u32[]{:S(2)}) %collective-permute-start.4) | collective-permute-done | bytes 393248 | tf_op jit(solution)/shard_map/ppermute | solution.py:565
  78.0 0.7 collective-permute-start.5
  78.7 4.2 %collective-permute-done.7.refs_4_ = f32[16,2,8,128]{3,2,1,0:T(8,128)S(1)} collective-permute-done((f32[16,2,8,128]{3,2,1,0:T(8,128)S(1)}, f32[16,2,8,128]{3,2,1,0:T(8,128)S(1)}, u32[]{:S(2)}, u32[]{:S(2)}) %collective-permute-start.7) | collective-permute-done | bytes 131104 | tf_op jit(solution)/shard_map/ppermute | solution.py:565
  82.9 1.3 %coarse_factors.1 = (f32[6,16,4,8,128]{4,3,2,1,0:T(8,128)S(1)}, f32[2,16,4,8,128]{4,3,2,1,0:T(8,128)S(1)}) custom-call(f32[8,128,128]{2,1,0:T(8,128)S(1)} %all-to-all-done.refs_0_, f32[8,128,128]{2,1,0:T(8,128)S(1)} %collective-permute-done.refs_1_, f32[8,128,128]{2,1,0:T(8,128)S(1)} %collective-permute-done.1.refs_2_, ...), custom_call_target="tpu_custom_call" | custom-call | tf_op jit(solution)/shard_map/coarse_factors/pallas_call | solution.py:534
  84.2 0.1 collective-permute-done.8.refs_5_
  84.3 1.4 %coarse.1.ends_ref = f32[8,72,128]{2,1,0:T(8,128)S(1)} custom-call(f32[6,16,4,8,128]{4,3,2,1,0:T(8,128)S(1)} %get-tuple-element.20.refs_0_, f32[2,16,4,8,128]{4,3,2,1,0:T(8,128)S(1)} %get-tuple-element.21.refs_1_, f32[16,2,8,128]{3,2,1,0:T(8,128)S(1)} %get-tuple-element.22.refs_2_, f32[16,2,8,128]{3,2,1,0:T(8,128)S(1)} %collective-permute-done.6.refs_3_, ...), custom_call_target="tpu_custom_call" | custom-call | tf_op jit(solution)/shard_map/coarse/pallas_call | solution.py:534
  85.6 0.6 collective-permute-done.5.come_ref
  86.3 17.4 %all_to_all.15.in_ref = f32[8,120,128]{2,1,0:T(8,128)S(1)} all-to-all(f32[8,120,128]{2,1,0:T(8,128)S(1)} %join.1), channel_id=1, replica_groups=mesh['tm'=4,'space'=8] {'space'}, dimensions={0} | all-to-all | bytes 983040 | tf_op jit(solution)/shard_map/all_to_all | solution.py:679
  103.7 1.0 unpack.1
  (11 shorter events, 0.2 us)
Async XLA Ops:
  3.1 21.8 %all-to-all-start = ((f32[8,128,128]{2,1,0:T(8,128)}), f32[8,128,128]{2,1,0:T(8,128)S(1)}, u32[]{:S(2)}, u32[]{:S(2)}) async-start(f32[8,128,128]{2,1,0:T(8,128)} %face_windows.1), calls=%async_computation | async-start | bytes 1048576 | tf_op jit(solution)/shard_map/all_to_all | solution.py:603
  24.8 26.8 %all-to-all-start.1 = ((f32[8,224,128]{2,1,0:T(8,128)}), f32[8,224,128]{2,1,0:T(8,128)S(1)}, u32[]{:S(2)}, u32[]{:S(2)}) async-start(f32[8,224,128]{2,1,0:T(8,128)} %field_windows.1), calls=%async_computation.1 | async-start | bytes 1835008 | tf_op jit(solution)/shard_map/all_to_all | solution.py:604
  28.5 13.6 %collective-permute-start.1 = (f32[8,128,128]{2,1,0:T(8,128)S(1)}, f32[8,128,128]{2,1,0:T(8,128)S(1)}, u32[]{:S(2)}, u32[]{:S(2)}) collective-permute-start(f32[8,128,128]{2,1,0:T(8,128)S(1)} %all-to-all-done.refs_0_), channel_id=1, source_target_pairs={{0,16},{8,24},{16,0},{24,8},{1,17},{9,25},{17,1},{25,9},{2,18},{10... | collective-permute-start | bytes 1572872 | tf_op jit(solution)/shard_map/ppermute | solution.py:565
  30.0 23.1 %collective-permute-start = (f32[8,128,128]{2,1,0:T(8,128)S(1)}, f32[8,128,128]{2,1,0:T(8,128)S(1)}, u32[]{:S(2)}, u32[]{:S(2)}) collective-permute-start(f32[8,128,128]{2,1,0:T(8,128)S(1)} %all-to-all-done.refs_0_), channel_id=1, source_target_pairs={{0,8},{8,0},{16,24},{24,16},{1,9},{9,1},{17,25},{25,17},{2,10},{10... | collective-permute-start | bytes 1572872 | tf_op jit(solution)/shard_map/ppermute | solution.py:565
  42.0 11.1 %collective-permute-start.2 = (f32[8,128,128]{2,1,0:T(8,128)S(1)}, f32[8,128,128]{2,1,0:T(8,128)S(1)}, u32[]{:S(2)}, u32[]{:S(2)}) collective-permute-start(f32[8,128,128]{2,1,0:T(8,128)S(1)} %collective-permute-done.1.refs_2_), channel_id=1, source_target_pairs={{0,8},{8,0},{16,24},{24,16},{1,9},{9,1},{17,25},{25,17},{2,10},{10... | collective-permute-start | bytes 1572872 | tf_op jit(solution)/shard_map/ppermute | solution.py:565
  51.8 3.2 %collective-permute-start.3 = (f32[16,2,8,128]{3,2,1,0:T(8,128)S(1)}, f32[16,2,8,128]{3,2,1,0:T(8,128)S(1)}, u32[]{:S(2)}, u32[]{:S(2)}) collective-permute-start(f32[16,2,8,128]{3,2,1,0:T(8,128)S(1)} %rough.1), channel_id=1, source_target_pairs={{8,0},{16,8},{24,16},{9,1},{17,9},{25,17},{10,2},{18,10},{26,18},{... | collective-permute-start | bytes 393224 | tf_op jit(solution)/shard_map/ppermute | solution.py:611
  73.6 4.3 %collective-permute-start.4 = (f32[2,8,48,128]{3,2,1,0:T(8,128)S(1)}, f32[2,8,48,128]{3,2,1,0:T(8,128)S(1)}, u32[]{:S(2)}, u32[]{:S(2)}) collective-permute-start(f32[2,8,48,128]{3,2,1,0:T(8,128)S(1)} %slice.13), channel_id=1, source_target_pairs={{0,8},{8,0},{16,24},{24,16},{1,9},{9,1},{17,25},{25,17},{2,10},{10... | collective-permute-start | bytes 1179656 | tf_op jit(solution)/shard_map/ppermute | solution.py:565
  76.6 6.4 %collective-permute-start.7 = (f32[16,2,8,128]{3,2,1,0:T(8,128)S(1)}, f32[16,2,8,128]{3,2,1,0:T(8,128)S(1)}, u32[]{:S(2)}, u32[]{:S(2)}) collective-permute-start(f32[16,2,8,128]{3,2,1,0:T(8,128)S(1)} %get-tuple-element.22.refs_2_), channel_id=1, source_target_pairs={{0,16},{8,24},{16,0},{24,8},{1,17},{9,25},{17,1},{25,9},{2,18},{10... | collective-permute-start | bytes 393224 | tf_op jit(solution)/shard_map/ppermute | solution.py:565
  78.0 8.3 %collective-permute-start.5 = (f32[1,8,48,128]{3,2,1,0:T(8,128)S(1)}, f32[1,8,48,128]{3,2,1,0:T(8,128)S(1)}, u32[]{:S(2)}, u32[]{:S(2)}) collective-permute-start(f32[1,8,48,128]{3,2,1,0:T(8,128)S(1)} %get-tuple-element.29), channel_id=1, source_target_pairs={{0,16},{8,24},{16,0},{24,8},{1,17},{9,25},{17,1},{25,9},{2,18},{10... | collective-permute-start | bytes 589832 | tf_op jit(solution)/shard_map/ppermute | solution.py:565
  78.7 5.5 %collective-permute-start.6 = (f32[16,2,8,128]{3,2,1,0:T(8,128)S(1)}, f32[16,2,8,128]{3,2,1,0:T(8,128)S(1)}, u32[]{:S(2)}, u32[]{:S(2)}) collective-permute-start(f32[16,2,8,128]{3,2,1,0:T(8,128)S(1)} %get-tuple-element.22.refs_2_), channel_id=1, source_target_pairs={{0,8},{8,0},{16,24},{24,16},{1,9},{9,1},{17,25},{25,17},{2,10},{10... | collective-permute-start | bytes 393224 | tf_op jit(solution)/shard_map/ppermute | solution.py:565
  82.9 1.3 %collective-permute-start.8 = (f32[16,2,8,128]{3,2,1,0:T(8,128)S(1)}, f32[16,2,8,128]{3,2,1,0:T(8,128)S(1)}, u32[]{:S(2)}, u32[]{:S(2)}) collective-permute-start(f32[16,2,8,128]{3,2,1,0:T(8,128)S(1)} %collective-permute-done.7.refs_4_), channel_id=1, source_target_pairs={{0,8},{8,0},{16,24},{24,16},{1,9},{9,1},{17,25},{25,17},{2,10},{10... | collective-permute-start | bytes 393224 | tf_op jit(solution)/shard_map/ppermute | solution.py:565
